TPU v7x, 32 devices: a whole 2x2x4 slice. The times are simulated.
32 devices in a mesh: tm: 8 (over z, y), src: 4 (over x, core).
Axes of the slice: x: 2, y: 2, z: 4, core: 2. Of those that a mesh axis runs over, the one named last changes fastest.
Arguments:
- mix_in: float32 [32768, 128], P('tm')
- skip_in: float32 [32768, 128], P('tm'), may hold values from -6 to 6
- encoded: float32 [32768, 512], P('tm'), may hold values from 0.1 to 3
- lengths: int32 [5], replicated, may hold values from 3999 to 8772, as said below
- w_in: float32 [128, 512], P(None, 'src'), may hold values from -0.5 to 0.5
- b_in: float32 [512], P('src'), may hold values from -3 to 3
- slope_in: float32 [512], P('src'), may hold values from 0.05 to 0.5
- gain_in: float32 [512], P('src'), may hold values from 0.25 to 1.75
- beta_in: float32 [512], P('src'), may hold values from -3 to 3
- w_depth: float32 [3, 512], P(None, 'src'), may hold values from -3 to 3
- b_depth: float32 [512], P('src'), may hold values from -3 to 3
- slope_mid: float32 [512], P('src'), may hold values from 0.05 to 0.5
- gain_mid: float32 [512], P('src'), may hold values from 0.25 to 1.75
- beta_mid: float32 [512], P('src'), may hold values from -3 to 3
- w_out: float32 [512, 256], P('src'), may hold values from -0.25 to 0.25
- b_out: float32 [256], replicated, may hold values from -3 to 3
- slope_skip: float32 [128], replicated, may hold values from 0.05 to 0.5
- w_mask: float32 [128, 1024], P(None, 'src'), may hold values from -0.5 to 0.5
- b_mask: float32 [1024], P('src'), may hold values from -3 to 3
- basis: float32 [512, 16], replicated, may hold values from -0.25 to 0.25
- cot_out: float32 [32768, 128], P('tm'), may hold values from -6 to 6
- cot_wave: float32 [2, 262144], P(None, 'tm'), may hold values from -6 to 6
Outputs:
- block_out: float32 [32768, 128], P('tm')
- wave: float32 [2, 262144], P(None, 'tm')
- grad_mix_in: float32 [32768, 128], P('tm')
- grad_skip_in: float32 [32768, 128], P('tm')
- grad_encoded: float32 [32768, 512], P('tm')
- grad_w_in: float32 [128, 512], P(None, 'src')
- grad_b_in: float32 [512], P('src')
- grad_slope_in: float32 [512], P('src')
- grad_gain_in: float32 [512], P('src')
- grad_beta_in: float32 [512], P('src')
- grad_w_depth: float32 [3, 512], P(None, 'src')
- grad_b_depth: float32 [512], P('src')
- grad_slope_mid: float32 [512], P('src')
- grad_gain_mid: float32 [512], P('src')
- grad_beta_mid: float32 [512], P('src')
- grad_w_out: float32 [512, 256], P('src')
- grad_b_out: float32 [256], replicated
- grad_slope_skip: float32 [128], replicated
- grad_w_mask: float32 [128, 1024], P(None, 'src')
- grad_b_mask: float32 [1024], P('src')
- grad_basis: float32 [512, 16], replicated
Inputs may be any that keep to these rules, and one draw needn't show every extreme that they name: The 5 items are 2 items of 3999 frames, 2 items of 7999 frames and one item of the remaining frames, in an order drawn from the seed; the lengths sum to 32768.
All inputs are finite; a program needn't handle non-finite values.
Results may differ from a plain program's by a relative error of at most 0.0003.
Values sent between devices are 32-bit elements; how exact they have to be, the bound alone decides.
No kernel may reach another device: no remote copies, remote signals or barrier semaphores. Data moves between devices by JAX's collectives and lax.ppermute only.
A program may use at most 128 MiB of HBM per device.

v0:
```python
import jax
import jax.numpy as jnp
from jax import lax
from jax.sharding import PartitionSpec as P

L = 16
HIDDEN_WIDTH = 512
DILATION_STEP = 128


epsilon = 1e-05


def padded(array, sides, width):
    for axis, dim in sides:
        size, length = (lax.axis_size(axis), array.shape[dim])
        up = [(i, (i + 1) % size) for i in range(size - 1)]
        down = [(j, i) for i, j in up]
        last = lax.slice_in_dim(array, length - width, length, axis=dim)
        first = lax.slice_in_dim(array, 0, width, axis=dim)
        before = lax.ppermute(last, axis, up)
        after = lax.ppermute(first, axis, down)
        array = jnp.concatenate([before, array, after], axis=dim)
    return array


def product(matrix, weights):
    return jnp.dot(
        matrix, weights, precision=lax.Precision.HIGHEST, preferred_element_type=jnp.float32
    )


def inner(matrix, weights):
    return lax.dot_general(
        matrix,
        weights,
        (((0,), (0,)), ((), ())),
        precision=lax.Precision.HIGHEST,
        preferred_element_type=jnp.float32,
    )


def outer_back(matrix, weights):
    return lax.dot_general(
        matrix,
        weights,
        (((1,), (1,)), ((), ())),
        precision=lax.Precision.HIGHEST,
        preferred_element_type=jnp.float32,
    )


def item_sums(rows, indicator_matrix):
    return jnp.dot(rows, indicator_matrix, precision=lax.Precision.HIGHEST)


def param_silu(value_entries, slopes):
    return slopes * value_entries + (1.0 - slopes) * jax.nn.silu(value_entries)


def param_slope(value_entries, slopes):
    logistic = jax.nn.sigmoid(value_entries)
    return slopes + (1.0 - slopes) * logistic * (1.0 + value_entries * (1.0 - logistic))


def item_lookup_tables(lengths, frame_slots, spacing):
    item_ends = jnp.cumsum(lengths, dtype=jnp.int32)
    item_starts = item_ends - lengths

    def item_of(places):
        return jnp.sum((places[:, None] >= item_ends[None, :]).astype(jnp.int32), axis=1)

    item_ids = item_of(frame_slots)
    indicator_matrix = (
        (frame_slots[:, None] >= item_starts[None, :]) & (frame_slots[:, None] < item_ends[None, :])
    ).astype(jnp.float32)
    lower_matches_item = (
        (frame_slots >= spacing) & (item_of(frame_slots - spacing) == item_ids)
    ).astype(jnp.float32)
    upper_matches_item = (item_of(frame_slots + spacing) == item_ids).astype(jnp.float32)
    preceding_matches_item = ((frame_slots >= 1) & (item_of(frame_slots - 1) == item_ids)).astype(
        jnp.float32
    )
    following_matches_item = (item_of(frame_slots + 1) == item_ids).astype(jnp.float32)
    return (
        indicator_matrix,
        lower_matches_item,
        upper_matches_item,
        preceding_matches_item,
        following_matches_item,
    )


def normalize(value_entries, norm_gain, norm_bias, indicator_matrix, counts):
    totals = lax.psum(item_sums(jnp.sum(value_entries, axis=1), indicator_matrix), ("tm", "src"))
    means = totals / counts
    centered = value_entries - product(indicator_matrix, means[:, None])
    squares = lax.psum(
        item_sums(jnp.sum(centered * centered, axis=1), indicator_matrix), ("tm", "src")
    )
    spread = squares / counts
    inv_rows = product(indicator_matrix, lax.rsqrt(spread + epsilon)[:, None])
    normed = centered * inv_rows
    return (normed * norm_gain + norm_bias, normed, inv_rows)


def normalize_back(grad_norm, normed, inv_rows, norm_gain, indicator_matrix, counts):
    scaled = grad_norm * norm_gain
    sum_plain, sum_cross = lax.psum(
        (
            item_sums(jnp.sum(scaled, axis=1), indicator_matrix),
            item_sums(jnp.sum(scaled * normed, axis=1), indicator_matrix),
        ),
        ("tm", "src"),
    )
    mean_plain = product(indicator_matrix, (sum_plain / counts)[:, None])
    mean_cross = product(indicator_matrix, (sum_cross / counts)[:, None])
    grad_values = (scaled - mean_plain - normed * mean_cross) * inv_rows
    return (grad_values, jnp.sum(grad_norm * normed, axis=0), jnp.sum(grad_norm, axis=0))


def dilated(value_entries, kernel, lower_matches_item, upper_matches_item):
    frame_count = value_entries.shape[0]
    padded_rows = padded(value_entries, (("tm", 0),), DILATION_STEP)
    lower_neighbor = padded_rows[:frame_count] * lower_matches_item[:, None]
    upper_neighbor = padded_rows[2 * DILATION_STEP :] * upper_matches_item[:, None]
    return (
        kernel[0] * lower_neighbor + kernel[1] * value_entries + kernel[2] * upper_neighbor,
        lower_neighbor,
        upper_neighbor,
    )


def local(
    mix_in,
    skip_in,
    encoded,
    lengths,
    w_in,
    b_in,
    slope_in,
    gain_in,
    beta_in,
    w_depth,
    b_depth,
    slope_mid,
    gain_mid,
    beta_mid,
    w_out,
    b_out,
    slope_skip,
    w_mask,
    b_mask,
    basis,
    cot_out,
    cot_wave,
):
    stride = L // 2
    shard_rows = mix_in.shape[0]
    first_frame = lax.axis_index("tm") * shard_rows
    frame_count = mix_in.shape[0]
    width_in = mix_in.shape[1]
    frame_slots = first_frame + jnp.arange(frame_count, dtype=jnp.int32)
    (
        indicator_matrix,
        lower_matches_item,
        upper_matches_item,
        preceding_matches_item,
        following_matches_item,
    ) = item_lookup_tables(lengths, frame_slots, DILATION_STEP)
    counts = lengths.astype(jnp.float32) * HIDDEN_WIDTH
    hidden_in = product(mix_in, w_in) + b_in
    input_norm, normed_in, inv_in = normalize(
        param_silu(hidden_in, slope_in), gain_in, beta_in, indicator_matrix, counts
    )
    depth_sum, lower_in, upper_in = dilated(
        input_norm, w_depth, lower_matches_item, upper_matches_item
    )
    depth_out = depth_sum + b_depth
    norm_mid, normed_mid, inv_mid = normalize(
        param_silu(depth_out, slope_mid), gain_mid, beta_mid, indicator_matrix, counts
    )
    branch = lax.psum(product(norm_mid, w_out), "src") + b_out
    block_out = mix_in + branch[:, :width_in]
    skip_total = skip_in + branch[:, width_in:]
    active_skip = param_silu(skip_total, slope_skip)
    mask = jax.nn.sigmoid(product(active_skip, w_mask) + b_mask)
    half_width = encoded.shape[1] // 2
    position = lax.axis_index("src")
    source = position // 2
    half_index = position % 2
    enc_half = lax.dynamic_slice_in_dim(encoded, half_index * half_width, half_width, 1)
    basis_half = lax.dynamic_slice_in_dim(basis, half_index * half_width, half_width, 0)
    masked = mask * enc_half
    source_slot = (jnp.arange(2, dtype=jnp.int32) == source).astype(jnp.float32)
    decoded = lax.psum(source_slot[:, None, None] * product(masked, basis_half)[None], "src")
    joined = jnp.concatenate([decoded, cot_wave.reshape(2, frame_count, stride)], axis=2)
    edge_rows = padded(joined, (("tm", 1),), 1)
    tails = edge_rows[:, :frame_count, stride:L] * preceding_matches_item[None, :, None]
    wave = (decoded[:, :, :stride] + tails).reshape(2, frame_count * stride)
    ahead = edge_rows[:, 2:, L:] * following_matches_item[None, :, None]
    grad_decoded = jnp.concatenate([joined[:, :, L:], ahead], axis=2)
    grad_own = lax.dynamic_index_in_dim(grad_decoded, source, 0, keepdims=False)
    grad_masked = outer_back(grad_own, basis_half)
    grad_basis_half = inner(masked, grad_own)
    grad_mask = grad_masked * enc_half
    grad_enc_half = grad_masked * mask
    enc_padded = lax.dynamic_update_slice_in_dim(
        jnp.zeros((frame_count, 2 * half_width), jnp.float32),
        grad_enc_half,
        half_index * half_width,
        1,
    )
    basis_padded = lax.dynamic_update_slice_in_dim(
        jnp.zeros((2 * half_width, L), jnp.float32), grad_basis_half, half_index * half_width, 0
    )
    grad_encoded, basis_source = lax.psum((enc_padded, basis_padded), "src")
    grad_logits = grad_mask * mask * (1.0 - mask)
    grad_active = lax.psum(outer_back(grad_logits, w_mask), "src")
    grad_w_mask = inner(active_skip, grad_logits)
    grad_b_mask = jnp.sum(grad_logits, axis=0)
    grad_skip_in = grad_active * param_slope(skip_total, slope_skip)
    grad_slope_skip = jnp.sum(grad_active * (skip_total - jax.nn.silu(skip_total)), axis=0)
    grad_branch = jnp.concatenate([cot_out, grad_skip_in], axis=1)
    grad_b_out = jnp.sum(grad_branch, axis=0)
    grad_w_out = inner(norm_mid, grad_branch)
    grad_norm_mid = outer_back(grad_branch, w_out)
    grad_act_mid, grad_gain_mid, grad_beta_mid = normalize_back(
        grad_norm_mid, normed_mid, inv_mid, gain_mid, indicator_matrix, counts
    )
    grad_depth = grad_act_mid * param_slope(depth_out, slope_mid)
    grad_slope_mid = jnp.sum(grad_act_mid * (depth_out - jax.nn.silu(depth_out)), axis=0)
    grad_b_depth = jnp.sum(grad_depth, axis=0)
    grad_w_depth = jnp.stack(
        [
            jnp.sum(grad_depth * lower_in, axis=0),
            jnp.sum(grad_depth * input_norm, axis=0),
            jnp.sum(grad_depth * upper_in, axis=0),
        ]
    )
    grad_norm_in = dilated(grad_depth, w_depth[::-1], lower_matches_item, upper_matches_item)[0]
    grad_act_in, grad_gain_in, grad_beta_in = normalize_back(
        grad_norm_in, normed_in, inv_in, gain_in, indicator_matrix, counts
    )
    grad_hidden = grad_act_in * param_slope(hidden_in, slope_in)
    grad_slope_in = jnp.sum(grad_act_in * (hidden_in - jax.nn.silu(hidden_in)), axis=0)
    grad_b_in = jnp.sum(grad_hidden, axis=0)
    grad_w_in = inner(mix_in, grad_hidden)
    grad_mix_in = cot_out + lax.psum(outer_back(grad_hidden, w_in), "src")
    summed = lax.psum(
        (
            grad_w_in,
            grad_b_in,
            grad_slope_in,
            grad_gain_in,
            grad_beta_in,
            grad_w_depth,
            grad_b_depth,
            grad_slope_mid,
            grad_gain_mid,
            grad_beta_mid,
            grad_w_out,
            grad_b_out,
            grad_slope_skip,
            grad_w_mask,
            grad_b_mask,
            basis_source,
        ),
        "tm",
    )
    return (
        block_out,
        wave,
        grad_mix_in,
        grad_skip_in,
        grad_encoded,
        summed[0],
        summed[1],
        summed[2],
        summed[3],
        summed[4],
        summed[5],
        summed[6],
        summed[7],
        summed[8],
        summed[9],
        summed[10],
        summed[11],
        summed[12],
        summed[13],
        summed[14],
        summed[15],
    )


def solution(mesh):
    in_specs = (
        P("tm", None),
        P("tm", None),
        P("tm", None),
        P(),
        P(None, "src"),
        P("src"),
        P("src"),
        P("src"),
        P("src"),
        P(None, "src"),
        P("src"),
        P("src"),
        P("src"),
        P("src"),
        P("src", None),
        P(),
        P(),
        P(None, "src"),
        P("src"),
        P(),
        P("tm", None),
        P(None, "tm"),
    )
    out_specs = (
        P("tm", None),
        P(None, "tm"),
        P("tm", None),
        P("tm", None),
        P("tm", None),
        P(None, "src"),
        P("src"),
        P("src"),
        P("src"),
        P("src"),
        P(None, "src"),
        P("src"),
        P("src"),
        P("src"),
        P("src"),
        P("src", None),
        P(),
        P(),
        P(None, "src"),
        P("src"),
        P(),
    )
    return jax.shard_map(local, mesh=mesh, in_specs=in_specs, out_specs=out_specs, check_vma=False)
```

profile of v0, /device:TPU:0, one launch (start us, length us, event | category | flops | bytes accessed | tf_op | source)
XLA Modules:
  0.0 837.6 jit_solution(4465717691623649947)
XLA Ops:
  13.8 42.0 %psum.210 = f32[5]{0:T(128)S(1)} all-reduce(f32[5]{0:T(128)S(1)} %convolution_bitcast_fusion.8), channel_id=1, replica_groups=mesh['tm'=8,'src'=4] {'tm','src'}, use_global_device_ids=true, to_apply=%region_2.3 | all-reduce | flops 5 | bytes 40 | tf_op jit(solution)/shard_map/psum | solution.py:95
  57.5 40.1 %psum.211 = f32[5]{0:T(128)S(1)} all-reduce(f32[5]{0:T(128)S(1)} %convolution_bitcast_fusion.7), channel_id=1, replica_groups=mesh['tm'=8,'src'=4] {'tm','src'}, use_global_device_ids=true, to_apply=%region_4.5 | all-reduce | flops 5 | bytes 40 | tf_op jit(solution)/shard_map/psum | solution.py:98
  112.5 40.1 %psum.212 = f32[5]{0:T(128)S(1)} all-reduce(f32[5]{0:T(128)S(1)} %convolution_bitcast_fusion.6), channel_id=1, replica_groups=mesh['tm'=8,'src'=4] {'tm','src'}, use_global_device_ids=true, to_apply=%region_9.10 | all-reduce | flops 5 | bytes 40 | tf_op jit(solution)/shard_map/psum | solution.py:95
  154.3 39.1 %psum.213 = f32[5]{0:T(128)S(1)} all-reduce(f32[5]{0:T(128)S(1)} %convolution_bitcast_fusion.5), channel_id=1, replica_groups=mesh['tm'=8,'src'=4] {'tm','src'}, use_global_device_ids=true, to_apply=%region_11.12 | all-reduce | flops 5 | bytes 40 | tf_op jit(solution)/shard_map/psum | solution.py:98
  193.6 5.9 fusion.18
  200.2 85.8 %all-reduce.11.cloned.1.call-done = f32[4096,256]{1,0:T(8,128)} async-done(((f32[4096,256]{1,0:T(8,128)}), f32[4096,256]{1,0:T(8,128)}) %all-reduce.11.cloned.1.call-update) | async-done | bytes 4194320 | tf_op jit(solution)/shard_map/psum | solution.py:183
  307.4 26.0 %all-reduce.13.cloned.1.call-done = f32[2,4096,16]{1,2,0:T(8,128)} async-done(((f32[2,4096,16]{1,2,0:T(8,128)}), f32[2,4096,16]{1,2,0:T(8,128)}) %all-reduce.13.cloned.1.call-update) | async-done | bytes 524304 | tf_op jit(solution)/shard_map/psum | solution.py:196
  342.9 7.6 fusion.71
  357.3 53.2 %all-reduce.15.cloned.1.call-done = f32[4096,128]{1,0:T(8,128)} async-done(((f32[4096,128]{1,0:T(8,128)}), f32[4096,128]{1,0:T(8,128)}) %all-reduce.15.cloned.1.call-update) | async-done | bytes 2097168 | tf_op jit(solution)/shard_map/psum | solution.py:219
  414.1 5.1 multiply_reduce_fusion.13
  419.7 5.4 broadcast_in_dim.4
  428.8 39.4 %all-reduce.1 = (f32[5]{0:T(128)S(1)}, f32[5]{0:T(128)S(1)}) all-reduce(f32[5]{0:T(128)S(1)} %convolution_bitcast_fusion.3, f32[5]{0:T(128)S(1)} %convolution_bitcast_fusion.4), channel_id=1, replica_groups=mesh['tm'=8,'src'=4] {'tm','src'}, use_global_device_ids=true, to_apply=%region_20.21 | all-reduce | flops 10 | bytes 80 | tf_op jit(solution)/shard_map/psum | solution.py:109
  468.6 8.8 %multiply_reduce_fusion.5 = (f32[128]{0:T(128)S(1)}, f32[128]{0:T(128)S(1)}, f32[128]{0:T(128)S(1)}, f32[128]{0:T(128)S(1)}, f32[4096,128]{1,0:T(8,128)S(1)}) fusion(f32[4096,128]{1,0:T(8,128)} %copy-done.4, f32[128,128]{1,0:T(8,128)S(1)} %collective-permute-done, f32[4096]{0:T(1024)S(1)} %get-tuple-element.171, f32[4096]{0:T(1024)S(1)} %get-tuple-element.170, ...), kind=kLoop, calls=%fused_computation.32 | loop fusion | flops 17825280 | bytes 8623616 | tf_op jit(solution)/shard_map/reduce_sum | solution.py:236
  488.3 7.8 multiply_reduce_fusion.12
  496.6 5.4 fusion.5
  502.0 41.4 %all-reduce = (f32[5]{0:T(128)S(1)}, f32[5]{0:T(128)S(1)}) all-reduce(f32[5]{0:T(128)S(1)} %convolution_bitcast_fusion.1, f32[5]{0:T(128)S(1)} %convolution_bitcast_fusion.2), channel_id=1, replica_groups=mesh['tm'=8,'src'=4] {'tm','src'}, use_global_device_ids=true, to_apply=%region_24.25 | all-reduce | flops 10 | bytes 80 | tf_op jit(solution)/shard_map/psum | solution.py:109
  543.8 6.4 multiply_reduce_fusion.6
  563.3 5.0 reshape.177
  568.3 5.7 fusion.21
  574.0 11.4 %psum.238 = f32[512,16]{0,1:T(8,128)S(1)} all-reduce(f32[512,16]{0,1:T(8,128)S(1)} %fusion.21), channel_id=1, replica_groups=mesh['tm'=8,'src'=4] {'src'}, use_global_device_ids=true, to_apply=%region_56.57 | all-reduce | flops 8192 | bytes 65536 | tf_op jit(solution)/shard_map/psum | solution.py:217
  589.0 5.5 multiply_reduce_fusion.1
  594.4 37.3 %all-reduce.2 = (f32[128]{0:T(128)}, f32[128]{0:T(128)}, f32[128]{0:T(128)}, f32[128]{0:T(128)}, f32[3,128]{1,0:T(4,128)}, /*index=5*/f32[128]{0:T(128)}, f32[12...) all-reduce(f32[128]{0:T(128)S(1)} %get-tuple-element.154, ...), channel_id=1, replica_groups=mesh['tm'=8,'src'=4] {'tm'}, use_global_device_ids=true, to_apply=%region_29.30 | all-reduce | flops 10240 | bytes 81920 | tf_op jit(solution)/shard_map/psum | solution.py:250
  633.3 184.6 %all-reduce.19.cloned.1.call-done = (f32[4096,128]{1,0:T(8,128)}, f32[4096,512]{1,0:T(8,128)}) async-done(((f32[4096,128]{1,0:T(8,128)}, f32[4096,512]{1,0:T(8,128)}), (f32[4096,128]{1,0:T(8,128)}, f32[4096,512]{1,0:T(8,128)})) %all-reduce.19.cloned.1.call-update) | async-done | bytes 10485776 | tf_op jit(solution)/shard_map/psum | solution.py:249
  821.7 7.8 copy.65
  (183 shorter events, 105.8 us)
Async XLA Ops:
  7.2 186.4 %copy-start = (f32[128,256]{1,0:T(8,128)S(1)}, f32[128,256]{1,0:T(8,128)}, u32[]{:S(2)}) copy-start(f32[128,256]{1,0:T(8,128)} %param.36) | copy-start | bytes 393220
  7.2 278.7 %all-reduce.11.cloned.1.call-start = ((), (), s32[]{:S(2)}) async-start(), calls=%async_computation | async-start | bytes 8388608 | tf_op jit(solution)/shard_map/psum | solution.py:183
  9.5 46.2 %copy-start.46 = (s32[5]{0:T(128)S(1)}, s32[5]{0:T(128)}, u32[]{:S(2)}) copy-start(s32[5]{0:T(128)} %param.25) | copy-start | bytes 64
  9.5 46.4 %copy-start.29 = (f32[128]{0:T(128)S(1)}, f32[128]{0:T(128)}, u32[]{:S(2)}) copy-start(f32[128]{0:T(128)} %param.28) | copy-start | bytes 1540
  13.5 85.8 %copy-start.8 = (f32[4096,128]{1,0:T(8,128)}, f32[4096,128]{1,0:T(8,128)S(1)}, u32[]{:S(2)}) copy-start(f32[4096,128]{1,0:T(8,128)S(1)} %get-tuple-element.176) | copy-start | bytes 6291460
  13.5 84.4 %copy-start.31 = (f32[128]{0:T(128)S(1)}, f32[128]{0:T(128)}, u32[]{:S(2)}) copy-start(f32[128]{0:T(128)} %param.29) | copy-start | bytes 1540
  13.5 84.4 %copy-start.44 = (f32[128]{0:T(128)S(1)}, f32[128]{0:T(128)}, u32[]{:S(2)}) copy-start(f32[128]{0:T(128)} %param.30) | copy-start | bytes 1540
  99.4 6.1 collective-permute-start
  103.6 6.2 collective-permute-start.1
  112.2 81.3 %copy-start.28 = (f32[128]{0:T(128)S(1)}, f32[128]{0:T(128)}, u32[]{:S(2)}) copy-start(f32[128]{0:T(128)} %param.34) | copy-start | bytes 1540
  112.2 81.3 %copy-start.36 = (f32[128]{0:T(128)S(1)}, f32[128]{0:T(128)}, u32[]{:S(2)}) copy-start(f32[128]{0:T(128)} %param.35) | copy-start | bytes 1540
  199.5 86.4 %copy-start.39 = (f32[256]{0:T(256)S(1)}, f32[256]{0:T(256)}, u32[]{:S(2)}) copy-start(f32[256]{0:T(256)} %param.37) | copy-start | bytes 3076
  199.5 134.0 %all-reduce.13.cloned.1.call-start = ((), (), s32[]{:S(2)}) async-start(), calls=%async_computation.1 | async-start | bytes 1048576 | tf_op jit(solution)/shard_map/psum | solution.py:196
  200.2 91.0 %copy-start.42 = (f32[128]{0:T(128)}, f32[128]{0:T(128)S(1)}, u32[]{:S(2)}) copy-start(f32[128]{0:T(128)S(1)} %broadcast_subtract_fusion) | copy-start | bytes 1540
  300.0 110.5 %all-reduce.15.cloned.1.call-start = ((), (), s32[]{:S(2)}) async-start(), calls=%async_computation.2 | async-start | bytes 4194304 | tf_op jit(solution)/shard_map/psum | solution.py:219
  334.3 6.1 collective-permute-start.3
  335.6 6.1 collective-permute-start.2
  357.2 53.3 %copy-start.41 = (f32[128]{0:T(128)S(1)}, f32[128]{0:T(128)}, u32[]{:S(2)}) copy-start(f32[128]{0:T(128)} %param.38) | copy-start | bytes 1540
  357.2 53.3 %copy-start.43 = (f32[128]{0:T(128)S(1)}, f32[128]{0:T(128)}, u32[]{:S(2)}) copy-start(f32[128]{0:T(128)} %copy-done.42) | copy-start | bytes 1540
  357.2 274.5 %all-reduce.17.cloned.1.call-start = ((), (), s32[]{:S(2)}) async-start(), calls=%async_computation.3 | async-start | bytes 655360 | tf_op jit(solution)/shard_map/psum | solution.py:250
  426.2 42.4 %copy-start.35 = (f32[128]{0:T(128)S(1)}, f32[128]{0:T(128)}, u32[]{:S(2)}) copy-start(f32[128]{0:T(128)} %copy-done.34) | copy-start | bytes 1540
  477.5 10.8 %collective-permute-start.4 = (f32[128,128]{1,0:T(8,128)S(1)}, f32[128,128]{1,0:T(8,128)S(1)}, u32[]{:S(2)}, u32[]{:S(2)}) collective-permute-start(f32[128,128]{1,0:T(8,128)S(1)} %get-tuple-element.160), channel_id=1, source_target_pairs={{0,4},{4,8},{8,12},{12,16},{16,20},{20,24},{24,28},{1,5},{5,9},{9,... | collective-permute-start | bytes 196616 | tf_op jit(solution)/shard_map/ppermute | solution.py:21
  481.7 6.6 collective-permute-start.5
  555.8 262.1 %all-reduce.19.cloned.1.call-start = ((), (), s32[]{:S(2)}) async-start(), calls=%async_computation.4 | async-start | bytes 20971520 | tf_op jit(solution)/shard_map/psum | solution.py:249
  (37 other events, 296.6 us)
Sparse Core Ops, SparseCore 0:
  199.6 86.2 all-reduce.10
  300.1 33.3 all-reduce.12
  357.3 53.0 all-reduce.14
  556.0 72.3 all-reduce.16
  631.6 186.3 all-reduce.18
where the time goes:
time: 846 us; the launch traced here: 838 us
  waiting for transfers between devices  355 us (42%)
  blocking collectives  291 us (34%)
  matrix products  63.3 us (7%)
  other arithmetic  57.6 us (7%)
  local copies, waits for them, and re-layouts  37.5 us (4%)
  starting transfers between devices  17.9 us (2%)
  between operations  14.9 us (2%)
    psum x1, waiting for transfers between devices, local(): grad_mix_in = cot_out + lax.psum(outer_back(grad_hidden, w_in), 'src')  185 us
    psum x1, waiting for transfers between devices, local(): branch = lax.psum(product(norm_mid, w_out), 'src') + b_out  85.8 us
    psum x2, blocking collectives, normalize(): lax.psum(item_sums(jnp.sum(value_entries, axis=1), indicator_matrix), ('t...  82.1 us
    psum x2, blocking collectives, normalize_back(): lax.psum((item_sums(jnp.sum(scaled, axis=1), indicator_matrix), item_sums...  80.8 us
    psum x2, blocking collectives, normalize(): lax.psum(item_sums(jnp.sum(centered * centered, axis=1), indicator_matrix...  79.2 us
    psum x1, waiting for transfers between devices, local(): grad_active = lax.psum(outer_back(grad_logits, w_mask), 'src')  53.2 us
    psum x1, blocking collectives, local(): lax.psum((grad_w_in, grad_b_in, grad_slope_in, grad_gain_in, grad_beta_in...  37.3 us
    psum x1, waiting for transfers between devices, local(): lax.psum(source_slot[:, None, None] * product(masked, basis_half)[None],...  26 us
  transfers between devices with their start and end apart: 11, of which 7 were waited for; matrix products, arithmetic and copies ran while one was open for 5% of the time, Pallas kernels for 0%

commit v1 on v0

v1 whole, which is shorter than its diff:
```python
import functools

import jax
import jax.numpy as jnp
from jax import lax
from jax.experimental import pallas as pl
from jax.experimental.pallas import tpu as pltpu
from jax.sharding import PartitionSpec as P

L = 16
STRIDE = L // 2
HIDDEN = 512
STEP = 128
EPS = 1e-05
T = 256
T1 = 512
LANES = 128
F32 = jnp.float32
BF16 = jnp.bfloat16
NVEC = 16
PACK_IN = 128 + NVEC


def split(x):
    hi = x.astype(BF16)
    return hi, (x - hi.astype(F32)).astype(BF16)


def mm(a, b):
    return lax.dot_general(a, b, (((1,), (0,)), ((), ())), preferred_element_type=F32)


def mm_tn(a, b):
    return lax.dot_general(a, b, (((0,), (0,)), ((), ())), preferred_element_type=F32)


def mm_nt(a, b):
    return lax.dot_general(a, b, (((1,), (1,)), ((), ())), preferred_element_type=F32)


def cat(parts, axis):
    return jnp.concatenate(parts, axis=axis)


def iota(shape, axis):
    return lax.broadcasted_iota(jnp.int32, shape, axis)


def sigmoid(x):
    return 1.0 / (1.0 + jnp.exp(-x))


def colsum(x):
    return jnp.sum(x, axis=0, keepdims=True)


def boundary(pos_ref, items, start):
    ahead = jnp.where(start - STEP >= 0, 0, -1)
    edge = jnp.int32(0)
    for k in range(items):
        end = pos_ref[3 + k]
        passed = end <= start - STEP
        ahead = ahead + passed.astype(jnp.int32)
    for k in range(items):
        edge = jnp.where(ahead == k, pos_ref[3 + k], edge)
    return edge, ahead


def item_rows(ahead, items):
    return jnp.maximum(ahead, 0), jnp.minimum(ahead + 1, items - 1)


def lane_items(ahead, items):
    lane = iota((1, LANES), 1)
    return (lane == ahead).astype(F32), (lane == ahead + 1).astype(F32)


def put_statistics(msg_ref, sums, squares, counts, onehot):
    groups = sums.shape[0]
    count = counts[:, :1]
    safe = jnp.maximum(count, 1.0)
    total = jnp.sum(sum(sums[g] for g in range(groups)), axis=1, keepdims=True)
    number = count * (groups * LANES)
    mean = total / jnp.maximum(number, 1.0)
    spread = 0.0
    for g in range(groups):
        away = sums[g] / safe - mean
        spread = spread + squares[g] + count * away * away
    spread = jnp.sum(spread, axis=1, keepdims=True)
    item_sum = colsum(onehot * total)
    item_number = colsum(onehot * number)
    item_mean = item_sum / jnp.maximum(item_number, 1.0)
    away = mean - item_mean
    item_spread = colsum(onehot * (spread + number * away * away))
    msg = cat(
        [item_sum, item_spread, item_number, item_mean, jnp.zeros((4, LANES), F32)], 0
    )
    for i in range(msg_ref.shape[0]):
        msg_ref[i] = msg


def to_rows(row, items_padded):
    wide = jnp.broadcast_to(row, (items_padded, LANES))
    own = iota((items_padded, LANES), 0) == iota((items_padded, LANES), 1)
    column = jnp.sum(jnp.where(own, wide, 0.0), axis=1, keepdims=True)
    return jnp.broadcast_to(column, (items_padded, HIDDEN))


def merge_statistics(msg_ref, table_ref):
    msg = msg_ref[...]
    item_sum = jnp.sum(msg[:, 0:1, :], axis=0)
    number = jnp.sum(msg[:, 2:3, :], axis=0)
    mean = item_sum / jnp.maximum(number, 1.0)
    away = msg[:, 3:4, :] - mean[None]
    squares = jnp.sum(msg[:, 1:2, :] + msg[:, 2:3, :] * away * away, axis=0)
    inverse = lax.rsqrt(squares / jnp.maximum(number, 1.0) + EPS)
    padded = table_ref.shape[1]
    table_ref[0] = to_rows(mean, padded)
    table_ref[1] = to_rows(inverse, padded)


def two_part_statistics(act, after, before, counts, sums_ref, squares_ref, counts_ref, onehot_ref, entry, ahead):
    n_before, n_after = counts
    groups = sums_ref.shape[0]
    sum_b = colsum(jnp.where(before, act, 0.0))
    sum_a = colsum(jnp.where(after, act, 0.0))
    mean_b = sum_b / jnp.maximum(n_before, 1.0)
    mean_a = sum_a / jnp.maximum(n_after, 1.0)
    dev = act - jnp.where(after, mean_a, mean_b)
    dev = dev * dev
    sq_b = colsum(jnp.where(before, dev, 0.0))
    sq_a = colsum(jnp.where(after, dev, 0.0))
    for g in range(groups):
        cut = slice(g * LANES, (g + 1) * LANES)
        sums_ref[g, pl.ds(2 * entry, 1), :] = sum_b[:, cut]
        sums_ref[g, pl.ds(2 * entry + 1, 1), :] = sum_a[:, cut]
        squares_ref[g, pl.ds(2 * entry, 1), :] = sq_b[:, cut]
        squares_ref[g, pl.ds(2 * entry + 1, 1), :] = sq_a[:, cut]
    counts_ref[pl.ds(2 * entry, 1), :] = jnp.full((1, LANES), n_before, F32)
    counts_ref[pl.ds(2 * entry + 1, 1), :] = jnp.full((1, LANES), n_after, F32)
    hot_b, hot_a = lane_items(ahead, 0)
    onehot_ref[pl.ds(2 * entry, 1), :] = hot_b
    onehot_ref[pl.ds(2 * entry + 1, 1), :] = hot_a


def first_kernel(items, pos_ref, mix_ref, w_ref, b_ref, slope_ref, msg_ref, sums, squares, counts, onehot):
    j = pl.program_id(0)
    start = pos_ref[0] + j * T1
    edge, ahead = boundary(pos_ref, items, start)
    m_hi, m_lo = split(mix_ref[...])
    w_hi, w_lo = split(w_ref[...])
    hidden = mm(cat([m_hi, m_lo], 1), cat([w_hi, w_hi], 0)) + mm(m_hi, w_lo) + b_ref[...]
    slope = slope_ref[...]
    act = hidden * (slope + (1.0 - slope) * sigmoid(hidden))
    offset = iota((T1, LANES), 0) + (start - edge)
    n_before = jnp.clip(edge - start, 0, T1).astype(F32)
    two_part_statistics(
        act, offset >= 0, offset < 0, (n_before, T1 - n_before), sums, squares, counts, onehot, j, ahead
    )

    @pl.when(j == pl.num_programs(0) - 1)
    def _():
        put_statistics(msg_ref, sums[...], squares[...], counts[...], onehot[...])


def depth_kernel(
    items, pos_ref, msg_in_ref, mix_ref, prev_ref, next_ref, own_ref, core_ref, x_ref, far_ref,
    hidden_ref, depth_ref, msg_ref, vec_ref, table_ref,
    gathered, sems, w_stack, w_low, ring, sums, squares, counts, onehot,
):
    m = pl.program_id(0)
    last = pl.num_programs(0) - 1
    half = pos_ref[1]
    own_rows = (last - 1) * T

    @pl.when(m == 0)
    def _():
        me = pos_ref[2]
        copies = [
            pltpu.make_async_copy(ref.at[pl.ds(0, PACK_IN)], gathered.at[me ^ k], sems.at[k])
            for k, ref in enumerate((own_ref, core_ref, x_ref, far_ref))
        ]
        for copy in copies:
            copy.start()
        merge_statistics(msg_in_ref, table_ref)
        sums[...] = jnp.zeros_like(sums)
        squares[...] = jnp.zeros_like(squares)
        counts[...] = jnp.zeros_like(counts)
        onehot[...] = jnp.zeros_like(onehot)
        for copy in copies:
            copy.wait()
        for s in range(4):
            cut = slice(s * LANES, (s + 1) * LANES)
            hi, lo = split(gathered[s, 0:128, :])
            w_stack[0:128, cut] = hi
            w_stack[128:256, cut] = hi
            w_low[:, cut] = lo
            vec_ref[:, cut] = gathered[s, 128 : 128 + NVEC, :]

    def vec(row):
        return vec_ref[row : row + 1, :]

    start = pos_ref[0] + half * own_rows + (m - 1) * T
    edge, ahead = boundary(pos_ref, items, start)
    block = half * (own_rows // T) + m - 1
    top = 2 * (own_rows // T)
    mix = jnp.where(block < 0, prev_ref[...], jnp.where(block >= top, next_ref[...], mix_ref[...]))
    m_hi, m_lo = split(mix)
    hidden = mm(cat([m_hi, m_lo], 1), w_stack[...]) + mm(m_hi, w_low[...]) + vec(0)

    @pl.when((m > 0) & (m < last))
    def _():
        hidden_ref[...] = hidden

    slope = vec(1)
    act = hidden * (slope + (1.0 - slope) * sigmoid(hidden))
    row_b, row_a = item_rows(ahead, items)
    inv_b, inv_a = table_ref[1, pl.ds(row_b, 1), :], table_ref[1, pl.ds(row_a, 1), :]
    mean_b, mean_a = table_ref[0, pl.ds(row_b, 1), :], table_ref[0, pl.ds(row_a, 1), :]
    scale_b, scale_a = inv_b * vec(2), inv_a * vec(2)
    shift_b, shift_a = vec(3) - mean_b * scale_b, vec(3) - mean_a * scale_a
    after = iota((T, HIDDEN), 0) + (start - edge) >= 0

    @pl.when(m > 0)
    def _():
        ring[0:T, :] = ring[T : 2 * T, :]

    ring[T : 2 * T, :] = act * jnp.where(after, scale_a, scale_b) + jnp.where(after, shift_a, shift_b)

    @pl.when(m > 0)
    def _():
        begin = start - STEP
        edge, ahead = boundary(pos_ref, items, begin)
        offset = iota((T, HIDDEN), 0) + (begin - edge)
        lower = jnp.where((offset >= 0) & (offset < STEP), 0.0, ring[0:T, :])
        upper = jnp.where((offset < 0) & (offset >= -STEP), 0.0, ring[T : 2 * T, :])
        depth = vec(4) * lower + vec(5) * ring[STEP : STEP + T, :] + vec(6) * upper + vec(7)
        depth_ref[...] = depth
        slope = vec(8)
        act = depth * (slope + (1.0 - slope) * sigmoid(depth))
        low = jnp.where(m == 1, STEP, 0)
        high = jnp.where(m == last, STEP, T)
        row = iota((T, HIDDEN), 0)
        own = (row >= low) & (row < high)
        n_before = jnp.clip(edge - begin, low, high) - low
        n_after = (high - low - n_before).astype(F32)
        two_part_statistics(
            act, own & (offset >= 0), own & (offset < 0), (n_before.astype(F32), n_after),
            sums, squares, counts, onehot, m - 1, ahead,
        )

    @pl.when(m == last)
    def _():
        put_statistics(msg_ref, sums[...], squares[...], counts[...], onehot[...])


def mask_kernel(
    items, pos_ref, msg_in_ref, depth_a_ref, depth_b_ref, mix_ref, skip_ref, enc_ref, cot_ref, wave_cot_ref,
    wave_next_ref, edge_next_ref, basis_ref, vec_ref, b_out_ref, slope_skip_ref, own_ref, core_ref, x_ref, far_ref,
    block_ref, grad_skip_ref, grad_enc_ref, send_ref, wave_ref, r_ref, up_ref, down_ref, keep_ref, give_ref, msg_ref,
    table_ref,
    gathered, sems, wo_hi, wo_lo, wot_hi, wot_lo, wm_stack, wm_low, wmt, basis_hi, basis_lo, basis_back, select_hi,
    select_lo, norm_hi, norm_lo, logit_hi, logit_lo, carry, acc_out, acc_mask, acc_basis, acc_vec, acc_small, entries,
    onehot,
):
    j = pl.program_id(0)
    last = pl.num_programs(0) - 1
    half = pos_ref[1]
    me = pos_ref[2]
    side = me // 2
    own_rows = (last + 1) * T

    def vec(row):
        return vec_ref[row : row + 1, :]

    @pl.when(j == 0)
    def _():
        rows = own_ref.shape[0] - PACK_IN
        copies = [
            pltpu.make_async_copy(ref.at[pl.ds(PACK_IN, rows)], gathered.at[me ^ k], sems.at[k])
            for k, ref in enumerate((own_ref, core_ref, x_ref, far_ref))
        ]
        for copy in copies:
            copy.start()
        merge_statistics(msg_in_ref, table_ref)
        acc_out[...] = jnp.zeros_like(acc_out)
        acc_mask[...] = jnp.zeros_like(acc_mask)
        acc_basis[...] = jnp.zeros_like(acc_basis)
        acc_vec[...] = jnp.zeros_like(acc_vec)
        acc_small[...] = jnp.zeros_like(acc_small)
        carry[...] = jnp.zeros_like(carry)
        b_hi, b_lo = split(basis_ref[...])
        col = iota((L, 2 * LANES), 1)
        row = iota((L, 2 * LANES), 0)
        spread = ((col & 7) == (row & 7)) & ((col >> 7) == (row >> 3))
        spread = spread.astype(F32).astype(BF16)
        basis_hi[...] = mm(b_hi, spread).astype(BF16)
        basis_lo[...] = mm(b_lo, spread).astype(BF16)
        for c in range(2):
            row = iota((LANES, L), 0) - 48 * c
            col = iota((LANES, L), 1)
            with_hi = ((row == col) | (row == col + 32)).astype(F32).astype(BF16)
            with_lo = (row == col + 16).astype(F32).astype(BF16)
            back = mm_nt(with_hi, b_hi) + mm_nt(with_lo, b_lo)
            basis_back[:, c * HIDDEN : (c + 1) * HIDDEN] = back.astype(BF16)
            row = iota((2 * LANES, LANES), 0)
            col = iota((2 * LANES, LANES), 1) - 48 * c
            place = (row & 7) + ((row >> 7) << 3)
            select_hi[c] = ((col == place) | (col == place + 16)).astype(F32).astype(BF16)
            select_lo[c] = (col == place + 32).astype(F32).astype(BF16)
        for copy in copies:
            copy.wait()
        for s in range(4):
            cut = slice(s * LANES, (s + 1) * LANES)
            for k in range(2):
                col = slice(k * LANES, (k + 1) * LANES)
                part = gathered[s, k * LANES : (k + 1) * LANES, :]
                hi, lo = split(part)
                wo_hi[cut, col] = hi
                wo_lo[cut, col] = lo
                hi, lo = split(part.T)
                wot_hi[col, cut] = hi
                wot_lo[col, cut] = lo
                part = gathered[s, (2 + k) * LANES : (3 + k) * LANES, :]
                wide = slice(s * 256 + k * LANES, s * 256 + (k + 1) * LANES)
                hi, lo = split(part)
                wm_stack[0:128, wide] = hi
                wm_stack[128:256, wide] = hi
                wm_low[:, wide] = lo
                hi, lo = split(part.T)
                wmt[wide, 0:128] = hi
                wmt[wide, 128:256] = lo

    start = pos_ref[0] + half * own_rows + j * T
    edge, ahead = boundary(pos_ref, items, start)
    row_b, row_a = item_rows(ahead, items)
    offset = iota((T, LANES), 0) + (start - edge)
    after = offset >= 0
    after4 = cat([after] * 4, 1) if False else (iota((T, HIDDEN), 0) + (start - edge) >= 0)

    depth = cat([depth_a_ref[...], depth_b_ref[...]], 0)
    slope = vec(8)
    s = sigmoid(depth)
    part = (1.0 - slope) * s
    act = depth * (slope + part)
    inv = jnp.where(after4, table_ref[1, pl.ds(row_a, 1), :], table_ref[1, pl.ds(row_b, 1), :])
    mean = jnp.where(after4, table_ref[0, pl.ds(row_a, 1), :], table_ref[0, pl.ds(row_b, 1), :])
    normed = (act - mean) * inv
    hi, lo = split(normed * vec(9) + vec(10))
    norm_hi[...] = hi
    norm_lo[...] = lo
    branch = mm(hi, wo_hi[...]) + mm(hi, wo_lo[...]) + mm(lo, wo_hi[...]) + b_out_ref[...]
    block = mix_ref[...] + branch[:, 0:128]
    block_ref[...] = block
    send_ref[:, 0:128] = block
    total = skip_ref[...] + branch[:, 128:256]
    slope_skip = slope_skip_ref[...]
    s_skip = sigmoid(total)
    active = total * (slope_skip + (1.0 - slope_skip) * s_skip)
    a_hi, a_lo = split(active)
    a_both = cat([a_hi, a_lo], 1)

    lane_frame = iota((T, LANES), 1) >> 3
    frame = iota((T, LANES), 0) & 15
    here = lane_frame == frame
    ahead_same = offset != -1
    packed = 0.0
    for c in range(2):
        rows = [wave_cot_ref[c : c + 1, q * LANES : (q + 1) * LANES] for q in range(T // 16)]
        final = jnp.where(
            (half == 1) & (j == last), edge_next_ref[c : c + 1, :], wave_next_ref[c : c + 1, 0:LANES]
        )
        spread_rows = cat([jnp.broadcast_to(r, (16, LANES)) for r in rows], 0)
        next_rows = cat([jnp.broadcast_to(r, (16, LANES)) for r in rows[1:] + [final]], 0)
        current = jnp.where(here, spread_rows, 0.0)
        following = jnp.where(lane_frame == frame + 1, spread_rows, 0.0)
        following = jnp.where((frame == 15) & (lane_frame == 0), next_rows, following)
        following = jnp.where(ahead_same, following, 0.0)
        hi, lo = split(cat([current, following], 1))
        packed = packed + mm(hi, select_hi[c]) + mm(lo, select_lo[c])
    packed = packed.astype(BF16)

    decoded = [0.0, 0.0]
    back = 0.0
    for n in range(2):
        enc = enc_ref[:, n * 256 : (n + 1) * 256]
        grad_enc = 0.0
        for c in range(2):
            chunk = slice(c * HIDDEN + n * 256, c * HIDDEN + (n + 1) * 256)
            bias = vec_ref[11:12, 2 * c * 128 + n * 128 : 2 * c * 128 + n * 128 + 128]
            bias = cat([bias, vec_ref[12:13, 2 * c * 128 + n * 128 : 2 * c * 128 + n * 128 + 128]], 1)
            logits = mm(a_both, wm_stack[:, chunk]) + mm(a_hi, wm_low[:, chunk]) + bias
            mask = sigmoid(logits)
            masked = mask * enc
            hi, lo = split(masked)
            b_hi, b_lo = basis_hi[n * 256 : (n + 1) * 256, :], basis_lo[n * 256 : (n + 1) * 256, :]
            decoded[c] = decoded[c] + mm(hi, b_hi) + mm(hi, b_lo) + mm(lo, b_hi)
            acc_basis[c, :, n * 256 : (n + 1) * 256] += mm_tn(packed, hi) + mm_tn(packed, lo)
            grad_masked = mm(packed, basis_back[:, chunk])
            grad_enc = grad_enc + grad_masked * mask
            grad_logits = grad_masked * masked * (1.0 - mask)
            hi, lo = split(grad_logits)
            logit_hi[c, :, n * 256 : (n + 1) * 256] = hi
            logit_lo[c, :, n * 256 : (n + 1) * 256] = lo
            back = back + mm(hi, wmt[chunk, :]) + mm(lo, wmt[chunk, :])
            acc_vec[2 : 3, chunk] += colsum(grad_logits)
        grad_enc_ref[:, n * 256 : (n + 1) * 256] = grad_enc
        send_ref[:, 256 + n * 256 : 256 + (n + 1) * 256] = grad_enc
    grad_active = back[:, 0:128] + back[:, 128:256]

    for c in range(2):
        tail = decoded[c][:, 128:256]
        shifted = pltpu.roll(tail, 1, 0)
        first = iota((T, LANES), 0) == 0
        shifted = jnp.where(first, carry[c : c + 1, :], shifted)
        carry[c : c + 1, :] = tail[T - 1 : T, :]
        value = decoded[c][:, 0:128] + jnp.where(offset == 0, 0.0, shifted)
        value = jnp.where(here, value, 0.0)
        lines = jnp.sum(value.reshape(T // 16, 16, LANES), axis=1)
        for q in range(T // 16):
            wave_ref[c : c + 1, q * LANES : (q + 1) * LANES] = lines[q : q + 1, :]

    u = 1.0 - s_skip
    grad_skip = grad_active * (slope_skip + (1.0 - slope_skip) * s_skip * (1.0 + total * u))
    grad_skip_ref[...] = grad_skip
    send_ref[:, 128:256] = grad_skip
    cot = cot_ref[...]
    acc_small[0:1, 0:128] += colsum(grad_active * (total * u))
    acc_small[1:2, 0:128] += colsum(cot)
    acc_small[2:3, 0:128] += colsum(grad_skip)
    g_hi, g_lo = split(cat([cot, grad_skip], 1))
    r = mm(g_hi, wot_hi[...]) + mm(g_hi, wot_lo[...]) + mm(g_lo, wot_hi[...])
    r_ref[...] = r

    @pl.when(j == 0)
    def _():
        down_ref[...] = r[0:128, :]

    @pl.when(j == last)
    def _():
        up_ref[0:128, :] = r[T - 128 : T, :]
        up_ref[128:136, :] = jnp.zeros((8, HIDDEN), F32)
        up_ref[128:130, 0:128] = carry[0:2, :]

    wide = pl.ds(pl.multiple_of(side * 256, 256), 256)
    n_hi, n_lo = norm_hi[:, wide], norm_lo[:, wide]
    acc_out[...] += mm_tn(n_hi, g_hi) + mm_tn(n_lo, g_hi) + mm_tn(n_hi, g_lo)
    l_hi, l_lo = logit_hi[side], logit_lo[side]
    both = mm_tn(a_both, l_hi)
    acc_mask[...] += both[0:128] + both[128:256] + mm_tn(a_hi, l_lo)
    acc_vec[0:1, 0:HIDDEN] += colsum(r * normed)
    acc_vec[1:2, 0:HIDDEN] += colsum(r)

    offset4 = iota((T, HIDDEN), 0) + (start - edge)
    taps = jnp.where((offset4 >= 0) & (offset4 < STEP), 0.0, vec(4)) + vec(5)
    taps = taps + jnp.where((offset4 < 0) & (offset4 >= -STEP), 0.0, vec(6))
    pull = inv * (slope + part * (1.0 + depth * (1.0 - s)))
    plain = pull * (vec(2) * taps)
    cross = pull * (depth - vec(7) - vec(3) * taps)
    q = r * vec(9)
    quantities = (q, q * normed, plain * q, plain, plain * normed, cross * q, cross, cross * normed)
    for i, value in enumerate(quantities):
        value = value[:, 0:128] + value[:, 128:256] + value[:, 256:384] + value[:, 384:512]
        entries[i, pl.ds(2 * j, 1), :] = colsum(jnp.where(after, 0.0, value))
        entries[i, pl.ds(2 * j + 1, 1), :] = colsum(jnp.where(after, value, 0.0))
    hot_b, hot_a = lane_items(ahead, items)
    onehot[pl.ds(2 * j, 1), :] = hot_b
    onehot[pl.ds(2 * j + 1, 1), :] = hot_a

    @pl.when(j == last)
    def _():
        hot = onehot[...]
        lines = [colsum(hot * jnp.sum(entries[i], axis=1, keepdims=True)) for i in range(8)]
        msg = cat(lines, 0)
        for i in range(msg_ref.shape[0]):
            msg_ref[i] = msg
        for ref, h in ((keep_ref, half), (give_ref, 1 - half)):
            own = pl.ds(pl.multiple_of(h * 128, 128), 128)
            ref[0:128, :] = acc_out[own, 0:128]
            ref[128:256, :] = acc_out[own, 128:256]
            pair = pl.ds(pl.multiple_of(h * 256, 256), 256)
            mask_part = acc_mask[:, pair]
            ref[256:384, :] = mask_part[:, 0:128]
            ref[384:512, :] = mask_part[:, 128:256]
            bias = acc_vec[2:3, pl.ds(pl.multiple_of(side * 512 + h * 256, 256), 256)]
            channels = pl.ds(pl.multiple_of(side * 256 + h * 128, 128), 128)
            ref[512:520, :] = cat(
                [
                    bias[:, 0:128], bias[:, 128:256], acc_vec[0:1, channels], acc_vec[1:2, channels],
                    acc_small[0:3, 0:128], jnp.zeros((1, LANES), F32),
                ], 0,
            )
            for k in range(4):
                cut = slice(k * 128, (k + 1) * 128)
                ref[520 + 16 * k : 536 + 16 * k, :] = (
                    acc_basis[0, 0:16, cut] + acc_basis[0, 32:48, cut]
                    + acc_basis[1, 48:64, cut] + acc_basis[1, 80:96, cut]
                )


def back_kernel(
    items, pos_ref, msg_in_ref, depth_ref, r_a_ref, r_b_ref, low_ref, high_ref, hidden_ref, mix_ref, cot_ref,
    vec_ref, table_in_ref, table_mid_ref, own_ref, core_ref, x_ref, far_ref, got_ref, block_in, skip_in, enc_in,
    grad_mix_ref, send_ref, keep_ref, give_ref, block_ref, skip_ref, enc_ref,
    gathered, sems, table, wt, ring, grad_hi, grad_lo, acc_w, acc_vec,
):
    j = pl.program_id(0)
    last = pl.num_programs(0) - 1
    half = pos_ref[1]
    me = pos_ref[2]
    side = me // 2
    own_rows = last * T

    def vec(row):
        return vec_ref[row : row + 1, :]

    @pl.when(j == 0)
    def _():
        copies = [
            pltpu.make_async_copy(ref.at[pl.ds(0, 128)], gathered.at[me ^ k], sems.at[k])
            for k, ref in enumerate((own_ref, core_ref, x_ref, far_ref))
        ]
        for copy in copies:
            copy.start()
        totals = 0.5 * jnp.sum(msg_in_ref[...], axis=0)
        lane = iota((1, LANES), 1)
        number = jnp.zeros((1, LANES), jnp.int32)
        for k in range(items):
            begin = pos_ref[2 + k] if k else 0
            number = jnp.where(lane == k, pos_ref[3 + k] - begin, number)
        number = jnp.maximum(number.astype(F32) * HIDDEN, 1.0)
        m1 = totals[0:1] / number
        m2 = totals[1:2] / number
        p1 = (totals[2:3] - m1 * totals[3:4] - m2 * totals[4:5]) / number
        p2 = (totals[5:6] - m1 * totals[6:7] - m2 * totals[7:8]) / number
        padded = table.shape[1]
        for i, value in enumerate((m1, m2, p1, p2)):
            table[i] = to_rows(value, padded)
        acc_w[...] = jnp.zeros_like(acc_w)
        acc_vec[...] = jnp.zeros_like(acc_vec)
        for copy in copies:
            copy.wait()
        for s in range(4):
            cut = slice(s * LANES, (s + 1) * LANES)
            hi, lo = split(gathered[s].T)
            wt[cut, 0:128] = hi
            wt[cut, 128:256] = lo

    block_ref[...] = got_ref[:, 0:128]
    skip_ref[...] = got_ref[:, 128:256]
    enc_ref[...] = got_ref[:, 256:768]

    begin = pos_ref[0] + half * own_rows + j * T - STEP
    edge, ahead = boundary(pos_ref, items, begin)
    row_b, row_a = item_rows(ahead, items)
    after = iota((T, HIDDEN), 0) + (begin - edge) >= 0

    def pick(ref, i, after, row_a, row_b):
        return jnp.where(after, ref[i, pl.ds(row_a, 1), :], ref[i, pl.ds(row_b, 1), :])

    depth = depth_ref[...]
    r = cat(
        [
            jnp.where(j == 0, low_ref[0:128, :], r_a_ref[...]),
            jnp.where(j == last, high_ref[...], r_b_ref[...]),
        ], 0,
    )
    slope = vec(8)
    s = sigmoid(depth)
    u = depth * (1.0 - s)
    part = (1.0 - slope) * s
    act = depth * (slope + part)
    inv = pick(table_mid_ref, 1, after, row_a, row_b)
    normed = (act - pick(table_mid_ref, 0, after, row_a, row_b)) * inv
    grad_act = inv * (r * vec(9) - pick(table, 0, after, row_a, row_b) - normed * pick(table, 1, after, row_a, row_b))
    in_low = jnp.where(j > 0, 1.0, 0.0)
    in_high = jnp.where(j < last, 1.0, 0.0)
    along = grad_act * u
    acc_vec[8:9, :] += in_low * colsum(along[0:128]) + in_high * colsum(along[128:256])

    @pl.when(j > 0)
    def _():
        ring[0:T, :] = ring[T : 2 * T, :]

    ring[T : 2 * T, :] = grad_act * (slope + part * (1.0 + u))

    @pl.when(j > 0)
    def _():
        start = pos_ref[0] + half * own_rows + (j - 1) * T
        edge, ahead = boundary(pos_ref, items, start)
        row_b, row_a = item_rows(ahead, items)
        offset = iota((T, HIDDEN), 0) + (start - edge)
        after = offset >= 0
        grad_low = jnp.where((offset >= 0) & (offset < STEP), 0.0, ring[0:T, :])
        grad_high = jnp.where((offset < 0) & (offset >= -STEP), 0.0, ring[T : 2 * T, :])
        grad_mid = ring[STEP : STEP + T, :]
        grad_norm = vec(5) * grad_mid + vec(4) * grad_high + vec(6) * grad_low
        hidden = hidden_ref[...]
        slope = vec(1)
        s = sigmoid(hidden)
        u = hidden * (1.0 - s)
        part = (1.0 - slope) * s
        act = hidden * (slope + part)
        inv = pick(table_in_ref, 1, after, row_a, row_b)
        normed = (act - pick(table_in_ref, 0, after, row_a, row_b)) * inv
        norm = normed * vec(2) + vec(3)
        grad_act = inv * (
            grad_norm * vec(2) - pick(table, 2, after, row_a, row_b) - normed * pick(table, 3, after, row_a, row_b)
        )
        grad_hidden = grad_act * (slope + part * (1.0 + u))
        sums = (
            grad_hidden, grad_act * u, grad_norm * normed, grad_norm, norm * grad_high, norm * grad_mid,
            norm * grad_low, grad_mid,
        )
        acc_vec[0:8, :] += cat([colsum(value) for value in sums], 0)
        hi, lo = split(grad_hidden)
        grad_hi[...] = hi
        grad_lo[...] = lo
        back = mm(hi, wt[...]) + mm(lo, wt[...])
        grad_mix = cot_ref[...] + back[:, 0:128] + back[:, 128:256]
        grad_mix_ref[...] = grad_mix
        send_ref[...] = grad_mix
        wide = pl.ds(pl.multiple_of(side * 256, 256), 256)
        m_hi, m_lo = split(mix_ref[...])
        both = mm_tn(cat([m_hi, m_lo], 1), grad_hi[:, wide])
        acc_w[...] += both[0:128] + both[128:256] + mm_tn(m_hi, grad_lo[:, wide])

    @pl.when(j == last)
    def _():
        for ref, h in ((keep_ref, half), (give_ref, 1 - half)):
            ref[0:128, :] = acc_w[:, pl.ds(pl.multiple_of(h * 128, 128), 128)]
            channels = pl.ds(pl.multiple_of(side * 256 + h * 128, 128), 128)
            ref[128:144, :] = acc_vec[:, channels]


def last_kernel(
    a_ref, b_ref, c_ref, d_ref, w_in, b_in, slope_in, gain_in, beta_in, w_depth, b_depth, slope_mid, gain_mid,
    beta_mid, w_out, b_out, slope_skip, w_mask, b_mask, basis,
):
    late = a_ref[...] + b_ref[...]
    w_in[...] = late[0:128]
    for ref, row in (
        (b_in, 128), (slope_in, 129), (gain_in, 130), (beta_in, 131), (b_depth, 135), (slope_mid, 136),
    ):
        ref[...] = late[row : row + 1]
    w_depth[...] = late[132:135]
    early = c_ref[...] + d_ref[...]
    w_out[:, 0:128] = early[0:128]
    w_out[:, 128:256] = early[128:256]
    w_mask[:, 0:128] = early[256:384]
    w_mask[:, 128:256] = early[384:512]
    b_mask[:, 0:128] = early[512:513]
    b_mask[:, 128:256] = early[513:514]
    gain_mid[...] = early[514:515]
    beta_mid[...] = early[515:516]
    slope_skip[...] = early[516:517]
    b_out[:, 0:128] = early[517:518]
    b_out[:, 128:256] = early[518:519]
    for k in range(4):
        basis[k * 128 : (k + 1) * 128, :] = early[520 + 16 * k : 536 + 16 * k].T


def local(
    mix_in, skip_in, encoded, lengths, w_in, b_in, slope_in, gain_in, beta_in, w_depth, b_depth, slope_mid, gain_mid,
    beta_mid, w_out, b_out, slope_skip, w_mask, b_mask, basis, cot_out, cot_wave,
):
    n_tm, n_src = lax.axis_size("tm"), lax.axis_size("src")
    devices = n_tm * n_src
    frames = mix_in.shape[0]
    own_rows = frames // 2
    items = lengths.shape[0]
    padded = -(-items // 8) * 8
    tiles = own_rows // T
    tm, me = lax.axis_index("tm"), lax.axis_index("src")
    half = me % 2
    pos = jnp.concatenate(
        [jnp.stack([tm * frames, half, me]).astype(jnp.int32), jnp.cumsum(lengths, dtype=jnp.int32)]
    )
    up = [(i, i + 1) for i in range(n_tm - 1)]
    down = [(j, i) for i, j in up]
    swap = [(i, i ^ 1) for i in range(n_src)]
    cross = [(i, i ^ 2) for i in range(n_src)]

    mix_prev = lax.ppermute(mix_in[frames - T :], "tm", up)
    mix_next = lax.ppermute(mix_in[:T], "tm", down)
    cot_next = lax.ppermute(cot_wave[:, :LANES], "tm", down)

    def params(**kw):
        return pltpu.CompilerParams(vmem_limit_bytes=50 * 2**20, **kw)

    def struct(*shape):
        return jax.ShapeDtypeStruct(shape, F32)

    def whole(shape):
        zeros = (0,) * len(shape)
        return pl.BlockSpec(shape, lambda i, pos: zeros)

    anywhere = pl.BlockSpec(memory_space=pl.ANY)

    def vmem(*shape):
        return pltpu.VMEM(shape, F32)

    def vmem16(*shape):
        return pltpu.VMEM(shape, BF16)

    def call(kernel, name, grid, in_specs, out_specs, out_shape, scratch, **kw):
        return pl.pallas_call(
            functools.partial(kernel, items),
            grid_spec=pltpu.PrefetchScalarGridSpec(
                num_scalar_prefetch=1, grid=(grid,), in_specs=in_specs, out_specs=out_specs, scratch_shapes=scratch
            ),
            out_shape=out_shape,
            compiler_params=params(dimension_semantics=("arbitrary",)),
            name=name,
            **kw,
        )

    message = struct(devices, 8, LANES)

    def exchange(msg):
        return lax.all_to_all(msg, ("tm", "src"), 0, 0)

    n1 = frames // T1
    msg1 = call(
        first_kernel, "first", n1,
        [pl.BlockSpec((T1, 128), lambda i, pos: (i, 0)), whole((128, 128)), whole((1, 128)), whole((1, 128))],
        whole(message.shape), message,
        [vmem(1, 2 * n1, 128), vmem(1, 2 * n1, 128), vmem(2 * n1, 128), vmem(2 * n1, 128)],
    )(pos, mix_in, w_in, b_in.reshape(1, 128), slope_in.reshape(1, 128))

    vectors = jnp.concatenate(
        [
            b_in[None], slope_in[None], gain_in[None], beta_in[None], w_depth, b_depth[None], slope_mid[None],
            gain_mid[None], beta_mid[None], b_mask.reshape(2, 128), jnp.zeros((3, 128), F32),
        ]
    )
    pack = jnp.concatenate([w_in, vectors, w_out[:, :128], w_out[:, 128:], w_mask[:, :128], w_mask[:, 128:]])
    pack_core = lax.ppermute(pack, "src", swap)
    pack_x = lax.ppermute(pack, "src", cross)
    pack_far = lax.ppermute(pack_x, "src", swap)
    packs = (pack, pack_core, pack_x, pack_far)

    msg1 = exchange(msg1)

    entries = -(-2 * (tiles + 1) // 8) * 8
    hidden, depth, msg2, vec, table_in = call(
        depth_kernel, "depth", tiles + 2,
        [
            whole(message.shape),
            pl.BlockSpec((T, 128), lambda i, pos: (jnp.clip(pos[1] * tiles + i - 1, 0, 2 * tiles - 1), 0)),
            whole((T, 128)), whole((T, 128)), anywhere, anywhere, anywhere, anywhere,
        ],
        [
            pl.BlockSpec((T, HIDDEN), lambda i, pos: (jnp.clip(i - 1, 0, tiles - 1), 0)),
            pl.BlockSpec((T, HIDDEN), lambda i, pos: (jnp.maximum(i - 1, 0), 0)),
            whole(message.shape), whole((NVEC, HIDDEN)), whole((2, padded, HIDDEN)),
        ],
        [
            struct(own_rows, HIDDEN), struct(own_rows + T, HIDDEN), message, struct(NVEC, HIDDEN),
            struct(2, padded, HIDDEN),
        ],
        [
            vmem(4, PACK_IN, 128), pltpu.SemaphoreType.DMA((4,)), vmem16(256, HIDDEN), vmem16(128, HIDDEN),
            vmem(2 * T, HIDDEN), vmem(4, entries, 128), vmem(4, entries, 128), vmem(entries, 128),
            vmem(entries, 128),
        ],
    )(pos, msg1, mix_in, mix_prev, mix_next, *packs)
    msg2 = exchange(msg2)

    def half_rows(width):
        return pl.BlockSpec((T, width), lambda i, pos: (pos[1] * tiles + i, 0))

    def rows(width):
        return pl.BlockSpec((T, width), lambda i, pos: (i, 0))

    def other_rows(width):
        return pl.BlockSpec(
            (T, width), lambda i, pos: ((1 - pos[1]) * tiles + jnp.minimum(i, tiles - 1), 0)
        )

    pack_early = 584
    (block_out, grad_skip, grad_enc, send, wave_half, r, r_up, r_down, keep, give, msg3, table_mid) = call(
        mask_kernel, "mask", tiles,
        [
            whole(message.shape),
            pl.BlockSpec((128, HIDDEN), lambda i, pos: (2 * i + 1, 0)),
            pl.BlockSpec((128, HIDDEN), lambda i, pos: (2 * i + 2, 0)),
            half_rows(128), half_rows(128), half_rows(HIDDEN), half_rows(128),
            pl.BlockSpec((2, T * STRIDE), lambda i, pos: (0, pos[1] * tiles + i)),
            pl.BlockSpec((2, T * STRIDE), lambda i, pos: (0, jnp.minimum(pos[1] * tiles + i + 1, 2 * tiles - 1))),
            whole((2, 128)), whole((HIDDEN, L)), whole((NVEC, HIDDEN)), whole((1, 256)), whole((1, 128)),
            anywhere, anywhere, anywhere, anywhere,
        ],
        [
            half_rows(128), half_rows(128), half_rows(HIDDEN), rows(768),
            pl.BlockSpec((2, T * STRIDE), lambda i, pos: (0, i)),
            rows(HIDDEN), whole((136, HIDDEN)), whole((128, HIDDEN)), whole((pack_early, 128)),
            whole((pack_early, 128)), whole(message.shape), whole((2, padded, HIDDEN)),
        ],
        [
            struct(frames, 128), struct(frames, 128), struct(frames, HIDDEN), struct(own_rows, 768),
            struct(2, own_rows * STRIDE), struct(own_rows, HIDDEN), struct(136, HIDDEN), struct(128, HIDDEN),
            struct(pack_early, 128), struct(pack_early, 128), message, struct(2, padded, HIDDEN),
        ],
        [
            vmem(4, 512, 128), pltpu.SemaphoreType.DMA((4,)), vmem16(HIDDEN, 256), vmem16(HIDDEN, 256),
            vmem16(256, HIDDEN), vmem16(256, HIDDEN), vmem16(256, 1024), vmem16(128, 1024), vmem16(1024, 256),
            vmem16(HIDDEN, 256), vmem16(HIDDEN, 256), vmem16(128, 1024), vmem16(2, 256, 128), vmem16(2, 256, 128),
            vmem16(T, HIDDEN), vmem16(T, HIDDEN), vmem16(2, T, HIDDEN), vmem16(2, T, HIDDEN), vmem(8, 128),
            vmem(256, 256), vmem(128, HIDDEN), vmem(2, 128, HIDDEN), vmem(8, 1024), vmem(8, 128),
            vmem(8, 2 * tiles, 128), vmem(2 * tiles, 128),
        ],
    )(
        pos, msg2, depth, depth, mix_in, skip_in, encoded, cot_out, cot_wave, cot_wave, cot_next, basis, vec,
        b_out.reshape(1, 256), slope_skip.reshape(1, 128), *packs,
    )

    both = ("tm", "src")
    later, earlier = [], []
    for i in range(n_tm):
        for s in range(n_src):
            here = i * n_src + s
            there = here + 1 if s % 2 == 0 else (i + 1) * n_src + s - 1
            if s % 2 == 0 or i + 1 < n_tm:
                later.append((here, there))
                earlier.append((there, here))
    got_low = lax.ppermute(r_up, both, later)
    got_high = lax.ppermute(r_down, both, earlier)
    got = lax.ppermute(send, "src", swap)
    early = keep + lax.ppermute(give, "src", swap)
    wave_other = lax.ppermute(wave_half, "src", swap)
    msg3 = exchange(msg3)

    grad_mix, mix_send, keep, give, block_out, grad_skip, grad_enc = call(
        back_kernel, "back", tiles + 1,
        [
            whole(message.shape), rows(HIDDEN),
            pl.BlockSpec((128, HIDDEN), lambda i, pos: (jnp.maximum(2 * i - 1, 0), 0)),
            pl.BlockSpec((128, HIDDEN), lambda i, pos: (jnp.minimum(2 * i, 2 * tiles - 1), 0)),
            whole((136, HIDDEN)), whole((128, HIDDEN)),
            pl.BlockSpec((T, HIDDEN), lambda i, pos: (jnp.maximum(i - 1, 0), 0)),
            pl.BlockSpec((T, 128), lambda i, pos: (pos[1] * tiles + jnp.maximum(i - 1, 0), 0)),
            pl.BlockSpec((T, 128), lambda i, pos: (pos[1] * tiles + jnp.maximum(i - 1, 0), 0)),
            whole((NVEC, HIDDEN)), whole((2, padded, HIDDEN)), whole((2, padded, HIDDEN)),
            anywhere, anywhere, anywhere, anywhere,
            pl.BlockSpec((T, 768), lambda i, pos: (jnp.minimum(i, tiles - 1), 0)), anywhere, anywhere, anywhere,
        ],
        [
            pl.BlockSpec((T, 128), lambda i, pos: (pos[1] * tiles + jnp.maximum(i - 1, 0), 0)),
            pl.BlockSpec((T, 128), lambda i, pos: (jnp.maximum(i - 1, 0), 0)),
            whole((144, 128)), whole((144, 128)), other_rows(128), other_rows(128), other_rows(HIDDEN),
        ],
        [
            struct(frames, 128), struct(own_rows, 128), struct(144, 128), struct(144, 128), struct(frames, 128),
            struct(frames, 128), struct(frames, HIDDEN),
        ],
        [
            vmem(4, 128, 128), pltpu.SemaphoreType.DMA((4,)), vmem(4, padded, HIDDEN), vmem16(HIDDEN, 256),
            vmem(2 * T, HIDDEN), vmem16(T, HIDDEN), vmem16(T, HIDDEN), vmem(128, 256),
            vmem(16, HIDDEN),
        ],
        input_output_aliases={18: 4, 19: 5, 20: 6},
    )(
        pos, msg3, depth, r, r, got_low, got_high, hidden, mix_in, cot_out, vec, table_in, table_mid, *packs, got,
        block_out, grad_skip, grad_enc,
    )

    starts = jnp.concatenate([jnp.zeros((1,), jnp.int32), pos[3:]])
    mine = pos[0] + half * own_rows
    theirs = pos[0] + (1 - half) * own_rows
    same_mine = jnp.where(jnp.any(starts == mine), 0.0, 1.0)
    edge_mine = jnp.where(same_mine > 0, got_low[128:130, :STRIDE], 0.0)
    wave_half = wave_half.at[:, :STRIDE].add(edge_mine)
    del theirs, wave_other
    wave_other = lax.ppermute(wave_half, "src", swap)
    first = jnp.where(half == 0, wave_half, wave_other)
    second = jnp.where(half == 0, wave_other, wave_half)
    wave = jnp.concatenate([first, second], axis=1)

    mix_got = lax.ppermute(mix_send, "src", swap)
    grad_mix = lax.dynamic_update_slice_in_dim(grad_mix, mix_got, (1 - half) * own_rows, 0)

    late = keep + lax.ppermute(give, "src", swap)
    bits = n_tm.bit_length() - 1
    for bit in range(bits):
        perm = [(i, i ^ (1 << bit)) for i in range(n_tm)]
        late_other = lax.ppermute(late, "tm", perm)
        early_other = lax.ppermute(early, "tm", perm)
        if bit < bits - 1:
            late, early = late + late_other, early + early_other

    outs = pl.pallas_call(
        last_kernel,
        out_shape=[
            struct(128, 128), struct(1, 128), struct(1, 128), struct(1, 128), struct(1, 128), struct(3, 128),
            struct(1, 128), struct(1, 128), struct(1, 128), struct(1, 128), struct(128, 256), struct(1, 256),
            struct(1, 128), struct(128, 256), struct(1, 256), struct(HIDDEN, L),
        ],
        compiler_params=params(),
        name="last",
    )(late, late_other, early, early_other)
    outs = [o.reshape(-1) if o.shape[0] == 1 else o for o in outs]
    return (block_out, wave, grad_mix, grad_skip, grad_enc, *outs)


def solution(mesh):
    frames, channels = P("tm", None), P("src")
    in_specs = (
        frames, frames, frames, P(), P(None, "src"), channels, channels, channels, channels, P(None, "src"), channels,
        channels, channels, channels, P("src", None), P(), P(), P(None, "src"), channels, P(), frames, P(None, "tm"),
    )
    out_specs = (
        frames, P(None, "tm"), frames, frames, frames, P(None, "src"), channels, channels, channels, channels,
        P(None, "src"), channels, channels, channels, channels, P("src", None), P(), P(), P(None, "src"), channels,
        P(),
    )
    return jax.shard_map(local, mesh=mesh, in_specs=in_specs, out_specs=out_specs, check_vma=False)
```

time: 846 us -> 192 us (0.23)
  waiting for transfers between devices: 355 us -> 37 us
  blocking collectives: 291 us -> 0 us
  Pallas kernels: 0 us -> 93.2 us
  matrix products: 63.3 us -> 0 us
  other arithmetic: 57.6 us -> 5.94 us
  local copies, waits for them, and re-layouts: 37.5 us -> 15.5 us
  starting transfers between devices: 17.9 us -> 37.5 us
  between operations: 14.9 us -> 1.56 us
    psum x5 -> x0, waiting for transfers between devices: 350 us -> none  [the longest x1 185 us: local(): grad_mix_in = cot_out + lax.psum(outer_back(grad_hidden, w_in), 'src')]
    psum x8 -> x0, blocking collectives: 291 us -> none  [the longest x2 82.1 us: normalize(): lax.psum(item_sums(jnp.sum(value_entries, axis=1), indicator_matrix), ('t...]
    pallas_call x0 -> x5, Pallas kernels: none -> 93.2 us  [the longest x1 44.7 us: local(): call(mask_kernel, 'mask', tiles, [whole(message.shape), pl.BlockSpec((128...]
    dot_general x28 -> x0, matrix products: 63.3 us -> none  [the longest x4 22.2 us: outer_back(): lax.dot_general(matrix, weights, (((1,), (1,)), ((), ())), precision=lax....]
    reduce_sum x10 -> x0, other arithmetic: 40.4 us -> none  [the longest x2 11.9 us: normalize_back(): jnp.sum(grad_norm * normed, axis=0)]
    ppermute x6 -> x19, waiting for transfers between devices: 5.74 us -> 31.4 us  [the longest x3 18.5 us: local(): early_other = lax.ppermute(early, 'tm', perm)]
    all_to_all x0 -> x3, starting transfers between devices: none -> 16.7 us  [exchange(): return lax.all_to_all(msg, ('tm', 'src'), 0, 0)]
    reshape x3 -> x0, local copies, waits for them, and re-layouts: 12.4 us -> none  [the longest x2 7.38 us: local(): cot_wave.reshape(2, frame_count, stride)]
  transfers between devices with their start and end apart: 11 -> 22, of which waited for: 7 -> 9; matrix products, arithmetic and copies ran while one was open for 5% -> 4% of each run, Pallas kernels for 0% -> 16%
where the time goes in v1:
time: 192 us; the launch traced here: 191 us
  Pallas kernels  93.2 us (49%)
  starting transfers between devices  37.5 us (20%)
  waiting for transfers between devices  37 us (19%)
  local copies, waits for them, and re-layouts  15.5 us (8%)
  other arithmetic  5.94 us (3%)
    pallas_call x1, Pallas kernels, local(): call(mask_kernel, 'mask', tiles, [whole(message.shape), pl.BlockSpec((128...  44.7 us
    pallas_call x1, Pallas kernels, local(): call(back_kernel, 'back', tiles + 1, [whole(message.shape), rows(HIDDEN),...  25.3 us
    ppermute x3, waiting for transfers between devices, local(): early_other = lax.ppermute(early, 'tm', perm)  18.5 us
    pallas_call x1, Pallas kernels, local(): call(depth_kernel, 'depth', tiles + 2, [whole(message.shape), pl.BlockSpe...  17.1 us
    all_to_all x3, starting transfers between devices, exchange(): return lax.all_to_all(msg, ('tm', 'src'), 0, 0)  16.7 us
    unnamed x34, local copies, waits for them, and re-layouts  10.3 us
    all_to_all x3, waiting for transfers between devices, exchange(): return lax.all_to_all(msg, ('tm', 'src'), 0, 0)  5.58 us
    pallas_call x1, Pallas kernels, local(): call(first_kernel, 'first', n1, [pl.BlockSpec((T1, 128), lambda i, pos: (...  5.25 us
  transfers between devices with their start and end apart: 22, of which 9 were waited for; matrix products, arithmetic and copies ran while one was open for 4% of the time, Pallas kernels for 16%

profile of v1, /device:TPU:0, one launch (start us, length us, event | category | flops | bytes accessed | tf_op | source)
XLA Modules:
  0.0 190.7 jit_solution(14938899448124422957)
XLA Ops:
  1.6 2.4 %concatenate.15.own_ref = f32[656,128]{1,0:T(8,128)S(1)} concatenate(f32[128,128]{1,0:T(8,128)} %w_ref.1, f32[1,128]{1,0:T(1,128)} %bitcast.27, f32[1,128]{1,0:T(1,128)} %bitcast.29, f32[1,128]{1,0:T(1,128)} %bitcast.36, f32[1,128]{1,0:T(1,128)} %bitcast.37, f32[3,128]{1,0:T(4,128)} %param.33, f32[1,128]{1,0:T(1,128)} %bitcast.38, f32[1,128]{1,0:T(1,128)} %bitcast.39, ...), dimensions={0} | concatenate | bytes 671744 | tf_op jit(solution)/shard_map/concatenate | solution.py:737
  4.0 3.0 %collective-permute-start.3 = (f32[656,128]{1,0:T(8,128)S(1)}, f32[656,128]{1,0:T(8,128)S(1)}, u32[]{:S(2)}, u32[]{:S(2)}) collective-permute-start(f32[656,128]{1,0:T(8,128)S(1)} %concatenate.15.own_ref), channel_id=1, source_target_pairs={{0,2},{1,3},{2,0},{3,1},{4,6},{5,7},{6,4},{7,5},{8,10},{9,11},{10,... | collective-permute-start | bytes 1007624 | tf_op jit(solution)/shard_map/ppermute | solution.py:739
  7.9 1.6 copy-done
  11.7 5.3 %first.1 = f32[32,8,128]{2,1,0:T(8,128)} custom-call(s32[8]{0:T(128)S(1)} %pad_add_fusion.pos_ref, f32[4096,128]{1,0:T(8,128)S(1)} %copy-done, f32[128,128]{1,0:T(8,128)S(1)} %copy-done.3, f32[1,128]{1,0:T(1,128)S(1)} %bitcast.28, f32[1,128]{1,0:T(1,128)S(1)} %bitcast.30), custom_call_target="tpu_custom_call" | custom-call | tf_op jit(solution)/shard_map/first/pallas_call | solution.py:724
  16.9 5.2 %all-to-all-start = ((f32[32,8,128]{2,1,0:T(8,128)}), f32[32,8,128]{2,1,0:T(8,128)}, u32[]{:S(2)}, u32[]{:S(2)}) async-start(f32[32,8,128]{2,1,0:T(8,128)} %first.1), calls=%async_computation | async-start | bytes 262144 | tf_op jit(solution)/shard_map/all_to_all | solution.py:721
  22.4 3.6 %collective-permute-start = (f32[256,128]{1,0:T(8,128)S(1)}, f32[256,128]{1,0:T(8,128)S(1)}, u32[]{:S(2)}, u32[]{:S(2)}) collective-permute-start(f32[256,128]{1,0:T(8,128)S(1)} %get-tuple-element.135), channel_id=1, source_target_pairs={{0,4},{4,8},{8,12},{12,16},{16,20},{20,24},{24,28},{1,5},{5,9},{9,... | collective-permute-start | bytes 393224 | tf_op jit(solution)/shard_map/ppermute | solution.py:684
  26.0 1.3 collective-permute-start.1
  27.3 2.3 %collective-permute-done.prev_ref = f32[256,128]{1,0:T(8,128)S(1)} collective-permute-done((f32[256,128]{1,0:T(8,128)S(1)}, f32[256,128]{1,0:T(8,128)S(1)}, u32[]{:S(2)}, u32[]{:S(2)}) %collective-permute-start) | collective-permute-done | bytes 131104 | tf_op jit(solution)/shard_map/ppermute | solution.py:684
  30.2 3.2 %collective-permute-done.1.next_ref = f32[256,128]{1,0:T(8,128)S(1)} collective-permute-done((f32[256,128]{1,0:T(8,128)S(1)}, f32[256,128]{1,0:T(8,128)S(1)}, u32[]{:S(2)}, u32[]{:S(2)}) %collective-permute-start.1) | collective-permute-done | bytes 131104 | tf_op jit(solution)/shard_map/ppermute | solution.py:685
  35.9 17.1 %depth.1 = (f32[2048,512]{1,0:T(8,128)}, f32[2304,512]{1,0:T(8,128)}, f32[32,8,128]{2,1,0:T(8,128)S(1)}, f32[16,512]{1,0:T(8,128)S(1)}, f32[2,8,512]{2,1,0:T(8,128)S(1)}) custom-call(s32[8]{0:T(128)S(1)} %pad_add_fusion.pos_ref, f32[32,8,128]{2,1,0:T(8,128)} %all-to-all-done.msg_in_ref, f32[4096,128]{1,0:T(8,128)S(1)} %copy-done.1, ...), custom_call_target="tpu_custom_call" | custom-call | tf_op jit(solution)/shard_map/depth/pallas_call | solution.py:746
  53.6 5.5 %all-to-all-start.1 = ((f32[32,8,128]{2,1,0:T(8,128)}), f32[32,8,128]{2,1,0:T(8,128)S(1)}, u32[]{:S(2)}, u32[]{:S(2)}) async-start(f32[32,8,128]{2,1,0:T(8,128)} %copy-done.8), calls=%async_computation.1 | async-start | bytes 262144 | tf_op jit(solution)/shard_map/all_to_all | solution.py:721
  61.2 4.0 %collective-permute-done.5.edge_next_ref = f32[2,128]{1,0:T(2,128)S(1)} collective-permute-done((f32[2,128]{1,0:T(2,128)S(1)}, f32[2,128]{1,0:T(2,128)S(1)}, u32[]{:S(2)}, u32[]{:S(2)}) %collective-permute-start.5) | collective-permute-done | bytes 1056 | tf_op jit(solution)/shard_map/ppermute | solution.py:686
  65.2 2.1 %all-to-all-done.1.msg_in_ref = f32[32,8,128]{2,1,0:T(8,128)S(1)} async-done(((f32[32,8,128]{2,1,0:T(8,128)}), f32[32,8,128]{2,1,0:T(8,128)S(1)}, u32[]{:S(2)}, u32[]{:S(2)}) %all-to-all-start.1) | async-done | bytes 131104 | tf_op jit(solution)/shard_map/all_to_all | solution.py:721
  68.3 44.7 %mask.1 = (f32[4096,128]{1,0:T(8,128)}, f32[4096,128]{1,0:T(8,128)}, f32[4096,512]{1,0:T(8,128)}, f32[2048,768]{1,0:T(8,128)}, f32[2,16384]{1,0:T(2,128)S(1)}, /...) custom-call(s32[8]{0:T(128)S(1)} %pad_add_fusion.pos_ref, ...), custom_call_target="tpu_custom_call" | custom-call | tf_op jit(solution)/shard_map/mask/pallas_call | solution.py:782
  113.6 2.1 %collective-permute-start.6 = (f32[136,512]{1,0:T(8,128)S(1)}, f32[136,512]{1,0:T(8,128)S(1)}, u32[]{:S(2)}, u32[]{:S(2)}) collective-permute-start(f32[136,512]{1,0:T(8,128)S(1)} %get-tuple-element.78), channel_id=1, source_target_pairs={{0,1},{1,4},{2,3},{3,6},{4,5},{5,8},{6,7},{7,10},{8,9},{9,12},{10,... | collective-permute-start | bytes 835592 | tf_op jit(solution)/shard_map/ppermute | solution.py:827
  117.0 6.1 %all-to-all-start.2 = ((f32[32,8,128]{2,1,0:T(8,128)}), f32[32,8,128]{2,1,0:T(8,128)S(1)}, u32[]{:S(2)}, u32[]{:S(2)}) async-start(f32[32,8,128]{2,1,0:T(8,128)} %get-tuple-element.76), calls=%async_computation.2 | async-start | bytes 262144 | tf_op jit(solution)/shard_map/all_to_all | solution.py:721
  126.1 1.7 collective-permute-start.16
  127.8 3.5 %all-to-all-done.2.msg_in_ref = f32[32,8,128]{2,1,0:T(8,128)S(1)} async-done(((f32[32,8,128]{2,1,0:T(8,128)}), f32[32,8,128]{2,1,0:T(8,128)S(1)}, u32[]{:S(2)}, u32[]{:S(2)}) %all-to-all-start.2) | async-done | bytes 131104 | tf_op jit(solution)/shard_map/all_to_all | solution.py:721
  131.2 25.3 %back.1 = (f32[4096,128]{1,0:T(8,128)}, f32[2048,128]{1,0:T(8,128)S(1)}, f32[144,128]{1,0:T(8,128)S(1)}, f32[144,128]{1,0:T(8,128)S(1)}, f32[4096,128]{1,0:T(8,1...) custom-call(s32[8]{0:T(128)S(1)} %pad_add_fusion.pos_ref, ...), custom_call_target="tpu_custom_call", output_to_operand_aliasing={{4}: (18, {}), {5}: (19, {}), {6}: (20, {})} | custom-call | tf_op jit(solution)/shard_map/back/pallas_call | solution.py:834
  161.4 2.0 %collective-permute-done.12 = f32[144,128]{1,0:T(8,128)S(1)} collective-permute-done((f32[144,128]{1,0:T(8,128)S(1)}, f32[144,128]{1,0:T(8,128)S(1)}, u32[]{:S(2)}, u32[]{:S(2)}) %collective-permute-start.12) | collective-permute-done | bytes 73760 | tf_op jit(solution)/shard_map/ppermute | solution.py:887
  164.2 6.1 %collective-permute-done.17 = f32[584,128]{1,0:T(8,128)S(1)} collective-permute-done((f32[584,128]{1,0:T(8,128)S(1)}, f32[584,128]{1,0:T(8,128)S(1)}, u32[]{:S(2)}, u32[]{:S(2)}) %collective-permute-start.17) | collective-permute-done | bytes 299040 | tf_op jit(solution)/shard_map/ppermute | solution.py:888
  171.2 2.3 %collective-permute-start.14 = (f32[144,128]{1,0:T(8,128)S(1)}, f32[144,128]{1,0:T(8,128)S(1)}, u32[]{:S(2)}, u32[]{:S(2)}) collective-permute-start(f32[144,128]{1,0:T(8,128)S(1)} %add.41.a_ref), channel_id=1, source_target_pairs={{0,16},{4,20},{8,24},{12,28},{16,0},{20,4},{24,8},{28,12},{1,17},{... | collective-permute-start | bytes 221192 | tf_op jit(solution)/shard_map/ppermute | solution.py:887
  174.3 12.4 %collective-permute-done.18.d_ref = f32[584,128]{1,0:T(8,128)S(1)} collective-permute-done((f32[584,128]{1,0:T(8,128)S(1)}, f32[584,128]{1,0:T(8,128)S(1)}, u32[]{:S(2)}, u32[]{:S(2)}) %collective-permute-start.18) | collective-permute-done | bytes 299040 | tf_op jit(solution)/shard_map/ppermute | solution.py:888
  186.7 1.4 collective-permute-done.14.b_ref
  (79 shorter events, 25.2 us)
Async XLA Ops:
  4.0 18.1 %collective-permute-start.3 = (f32[656,128]{1,0:T(8,128)S(1)}, f32[656,128]{1,0:T(8,128)S(1)}, u32[]{:S(2)}, u32[]{:S(2)}) collective-permute-start(f32[656,128]{1,0:T(8,128)S(1)} %concatenate.15.own_ref), channel_id=1, source_target_pairs={{0,2},{1,3},{2,0},{3,1},{4,6},{5,7},{6,4},{7,5},{8,10},{9,11},{10,... | collective-permute-start | bytes 1007624 | tf_op jit(solution)/shard_map/ppermute | solution.py:739
  7.0 27.0 %collective-permute-start.2 = (f32[656,128]{1,0:T(8,128)S(1)}, f32[656,128]{1,0:T(8,128)S(1)}, u32[]{:S(2)}, u32[]{:S(2)}) collective-permute-start(f32[656,128]{1,0:T(8,128)S(1)} %concatenate.15.own_ref), channel_id=1, source_target_pairs={{0,1},{1,0},{2,3},{3,2},{4,5},{5,4},{6,7},{7,6},{8,9},{9,8},{10,11... | collective-permute-start | bytes 1007624 | tf_op jit(solution)/shard_map/ppermute | solution.py:738
  16.9 17.1 %all-to-all-start = ((f32[32,8,128]{2,1,0:T(8,128)}), f32[32,8,128]{2,1,0:T(8,128)}, u32[]{:S(2)}, u32[]{:S(2)}) async-start(f32[32,8,128]{2,1,0:T(8,128)} %first.1), calls=%async_computation | async-start | bytes 262144 | tf_op jit(solution)/shard_map/all_to_all | solution.py:721
  22.1 12.0 %collective-permute-start.4 = (f32[656,128]{1,0:T(8,128)S(1)}, f32[656,128]{1,0:T(8,128)S(1)}, u32[]{:S(2)}, u32[]{:S(2)}) collective-permute-start(f32[656,128]{1,0:T(8,128)S(1)} %collective-permute-done.3.x_ref), channel_id=1, source_target_pairs={{0,1},{1,0},{2,3},{3,2},{4,5},{5,4},{6,7},{7,6},{8,9},{9,8},{10,11... | collective-permute-start | bytes 1007624 | tf_op jit(solution)/shard_map/ppermute | solution.py:740
  22.4 7.2 %collective-permute-start = (f32[256,128]{1,0:T(8,128)S(1)}, f32[256,128]{1,0:T(8,128)S(1)}, u32[]{:S(2)}, u32[]{:S(2)}) collective-permute-start(f32[256,128]{1,0:T(8,128)S(1)} %get-tuple-element.135), channel_id=1, source_target_pairs={{0,4},{4,8},{8,12},{12,16},{16,20},{20,24},{24,28},{1,5},{5,9},{9,... | collective-permute-start | bytes 393224 | tf_op jit(solution)/shard_map/ppermute | solution.py:684
  26.0 41.3 %copy-start.11 = (f32[256]{0:T(256)S(1)}, f32[256]{0:T(256)}, u32[]{:S(2)}) copy-start(f32[256]{0:T(256)} %param.39) | copy-start | bytes 3076
  26.0 41.3 %copy-start.12 = (f32[128]{0:T(128)S(1)}, f32[128]{0:T(128)}, u32[]{:S(2)}) copy-start(f32[128]{0:T(128)} %param.40) | copy-start | bytes 1540
  26.0 7.4 %collective-permute-start.1 = (f32[256,128]{1,0:T(8,128)S(1)}, f32[256,128]{1,0:T(8,128)S(1)}, u32[]{:S(2)}, u32[]{:S(2)}) collective-permute-start(f32[256,128]{1,0:T(8,128)S(1)} %get-tuple-element.134), channel_id=1, source_target_pairs={{4,0},{8,4},{12,8},{16,12},{20,16},{24,20},{28,24},{5,1},{9,5},{13... | collective-permute-start | bytes 393224 | tf_op jit(solution)/shard_map/ppermute | solution.py:685
  53.6 13.7 %all-to-all-start.1 = ((f32[32,8,128]{2,1,0:T(8,128)}), f32[32,8,128]{2,1,0:T(8,128)S(1)}, u32[]{:S(2)}, u32[]{:S(2)}) async-start(f32[32,8,128]{2,1,0:T(8,128)} %copy-done.8), calls=%async_computation.1 | async-start | bytes 262144 | tf_op jit(solution)/shard_map/all_to_all | solution.py:721
  59.8 5.5 %collective-permute-start.5 = (f32[2,128]{1,0:T(2,128)S(1)}, f32[2,128]{1,0:T(2,128)S(1)}, u32[]{:S(2)}, u32[]{:S(2)}) collective-permute-start(f32[2,128]{1,0:T(2,128)S(1)} %slice.49), channel_id=1, source_target_pairs={{4,0},{8,4},{12,8},{16,12},{20,16},{24,20},{28,24},{5,1},{9,5},{13... | collective-permute-start | bytes 3080 | tf_op jit(solution)/shard_map/ppermute | solution.py:686
  113.0 18.2 %collective-permute-start.8 = (f32[2048,768]{1,0:T(8,128)}, f32[2048,768]{1,0:T(8,128)}, u32[]{:S(2)}, u32[]{:S(2)}) collective-permute-start(f32[2048,768]{1,0:T(8,128)} %get-tuple-element.83), channel_id=1, source_target_pairs={{0,1},{1,0},{2,3},{3,2},{4,5},{5,4},{6,7},{7,6},{8,9},{9,8},{10,11... | collective-permute-start | bytes 18874376 | tf_op jit(solution)/shard_map/ppermute | solution.py:829
  113.3 11.8 %collective-permute-start.15 = (f32[584,128]{1,0:T(8,128)S(1)}, f32[584,128]{1,0:T(8,128)}, u32[]{:S(2)}, u32[]{:S(2)}) collective-permute-start(f32[584,128]{1,0:T(8,128)S(1)} %get-tuple-element.96), channel_id=1, source_target_pairs={{0,1},{1,0},{2,3},{3,2},{4,5},{5,4},{6,7},{7,6},{8,9},{9,8},{10,11... | collective-permute-start | bytes 897032 | tf_op jit(solution)/shard_map/ppermute | solution.py:830
  113.6 17.7 %collective-permute-start.6 = (f32[136,512]{1,0:T(8,128)S(1)}, f32[136,512]{1,0:T(8,128)S(1)}, u32[]{:S(2)}, u32[]{:S(2)}) collective-permute-start(f32[136,512]{1,0:T(8,128)S(1)} %get-tuple-element.78), channel_id=1, source_target_pairs={{0,1},{1,4},{2,3},{3,6},{4,5},{5,8},{6,7},{7,10},{8,9},{9,12},{10,... | collective-permute-start | bytes 835592 | tf_op jit(solution)/shard_map/ppermute | solution.py:827
  115.7 15.5 %collective-permute-start.7 = (f32[128,512]{1,0:T(8,128)S(1)}, f32[128,512]{1,0:T(8,128)S(1)}, u32[]{:S(2)}, u32[]{:S(2)}) collective-permute-start(f32[128,512]{1,0:T(8,128)S(1)} %get-tuple-element.79), channel_id=1, source_target_pairs={{1,0},{4,1},{3,2},{6,3},{5,4},{8,5},{7,6},{10,7},{9,8},{12,9},{11,... | collective-permute-start | bytes 786440 | tf_op jit(solution)/shard_map/ppermute | solution.py:828
  117.0 14.2 %all-to-all-start.2 = ((f32[32,8,128]{2,1,0:T(8,128)}), f32[32,8,128]{2,1,0:T(8,128)S(1)}, u32[]{:S(2)}, u32[]{:S(2)}) async-start(f32[32,8,128]{2,1,0:T(8,128)} %get-tuple-element.76), calls=%async_computation.2 | async-start | bytes 262144 | tf_op jit(solution)/shard_map/all_to_all | solution.py:721
  126.1 33.6 %collective-permute-start.16 = (f32[584,128]{1,0:T(8,128)S(1)}, f32[584,128]{1,0:T(8,128)}, u32[]{:S(2)}, u32[]{:S(2)}) collective-permute-start(f32[584,128]{1,0:T(8,128)S(1)} %add.42), channel_id=1, source_target_pairs={{0,4},{4,0},{8,12},{12,8},{16,20},{20,16},{24,28},{28,24},{1,5},{5... | collective-permute-start | bytes 897032 | tf_op jit(solution)/shard_map/ppermute | solution.py:888
  157.6 1.4 collective-permute-start.11
  158.6 5.6 %collective-permute-start.9 = (f32[2,16384]{1,0:T(2,128)S(1)}, f32[2,16384]{1,0:T(2,128)S(1)}, u32[]{:S(2)}, u32[]{:S(2)}) collective-permute-start(f32[2,16384]{1,0:T(2,128)S(1)} %scatter-add.4), channel_id=1, source_target_pairs={{0,1},{1,0},{2,3},{3,2},{4,5},{5,4},{6,7},{7,6},{8,9},{9,8},{10,11... | collective-permute-start | bytes 393224 | tf_op jit(solution)/shard_map/ppermute | solution.py:875
  159.0 4.4 %collective-permute-start.12 = (f32[144,128]{1,0:T(8,128)S(1)}, f32[144,128]{1,0:T(8,128)S(1)}, u32[]{:S(2)}, u32[]{:S(2)}) collective-permute-start(f32[144,128]{1,0:T(8,128)S(1)} %add.39), channel_id=1, source_target_pairs={{0,4},{4,0},{8,12},{12,8},{16,20},{20,16},{24,28},{28,24},{1,5},{5... | collective-permute-start | bytes 221192 | tf_op jit(solution)/shard_map/ppermute | solution.py:887
  160.7 9.7 %collective-permute-start.17 = (f32[584,128]{1,0:T(8,128)S(1)}, f32[584,128]{1,0:T(8,128)S(1)}, u32[]{:S(2)}, u32[]{:S(2)}) collective-permute-start(f32[584,128]{1,0:T(8,128)S(1)} %add.43), channel_id=1, source_target_pairs={{0,8},{4,12},{8,0},{12,4},{16,24},{20,28},{24,16},{28,20},{1,9},{5... | collective-permute-start | bytes 897032 | tf_op jit(solution)/shard_map/ppermute | solution.py:888
  163.4 7.8 %collective-permute-start.13 = (f32[144,128]{1,0:T(8,128)S(1)}, f32[144,128]{1,0:T(8,128)S(1)}, u32[]{:S(2)}, u32[]{:S(2)}) collective-permute-start(f32[144,128]{1,0:T(8,128)S(1)} %add.40), channel_id=1, source_target_pairs={{0,8},{4,12},{8,0},{12,4},{16,24},{20,28},{24,16},{28,20},{1,9},{5... | collective-permute-start | bytes 221192 | tf_op jit(solution)/shard_map/ppermute | solution.py:887
  170.4 16.3 %collective-permute-start.18 = (f32[584,128]{1,0:T(8,128)S(1)}, f32[584,128]{1,0:T(8,128)S(1)}, u32[]{:S(2)}, u32[]{:S(2)}) collective-permute-start(f32[584,128]{1,0:T(8,128)S(1)} %add.44.c_ref), channel_id=1, source_target_pairs={{0,16},{4,20},{8,24},{12,28},{16,0},{20,4},{24,8},{28,12},{1,17},{... | collective-permute-start | bytes 897032 | tf_op jit(solution)/shard_map/ppermute | solution.py:888
  171.1 18.5 %collective-permute-start.10 = (f32[2048,128]{1,0:T(8,128)S(1)}, f32[2048,128]{1,0:T(8,128)S(1)}, u32[]{:S(2)}, u32[]{:S(2)}) collective-permute-start(f32[2048,128]{1,0:T(8,128)S(1)} %copy-done.14), channel_id=1, source_target_pairs={{0,1},{1,0},{2,3},{3,2},{4,5},{5,4},{6,7},{7,6},{8,9},{9,8},{10,11... | collective-permute-start | bytes 3145736 | tf_op jit(solution)/shard_map/ppermute | solution.py:880
  171.2 16.9 %collective-permute-start.14 = (f32[144,128]{1,0:T(8,128)S(1)}, f32[144,128]{1,0:T(8,128)S(1)}, u32[]{:S(2)}, u32[]{:S(2)}) collective-permute-start(f32[144,128]{1,0:T(8,128)S(1)} %add.41.a_ref), channel_id=1, source_target_pairs={{0,16},{4,20},{8,24},{12,28},{16,0},{20,4},{24,8},{28,12},{1,17},{... | collective-permute-start | bytes 221192 | tf_op jit(solution)/shard_map/ppermute | solution.py:887
  (14 other events, 72.4 us)

commit v2 on v1

v2 whole, which is shorter than its diff:
```python
import functools

import jax
import jax.numpy as jnp
from jax import lax
from jax.experimental import pallas as pl
from jax.experimental.pallas import tpu as pltpu
from jax.sharding import PartitionSpec as P

L = 16
STRIDE = L // 2
HIDDEN = 512
STEP = 128
EPS = 1e-05
T = 256
T1 = 512
TM = 512
ROWS = 32
LANES = 128
F32 = jnp.float32
BF16 = jnp.bfloat16
NVEC = 16
PACK_IN = 128 + NVEC
PACK = PACK_IN + 512
EARLY = 584
VMEM = 63 * 2**20 + 2**19
LOG2E = 1.4426950408889634


def split(x):
    hi = x.astype(BF16)
    return hi, (x - hi.astype(F32)).astype(BF16)


def mm(a, b):
    return lax.dot_general(a, b, (((1,), (0,)), ((), ())), preferred_element_type=F32)


def mm_tn(a, b):
    return lax.dot_general(a, b, (((0,), (0,)), ((), ())), preferred_element_type=F32)


def mm_nt(a, b):
    return lax.dot_general(a, b, (((1,), (1,)), ((), ())), preferred_element_type=F32)


def cat(parts, axis):
    return jnp.concatenate(parts, axis=axis)


def three(x, axis):
    hi, lo = x
    return cat([hi, lo, hi], axis)


def two_of(x, axis):
    hi, lo = x
    return cat([hi, hi, lo], axis)


def iota(shape, axis):
    return lax.broadcasted_iota(jnp.int32, shape, axis)


def sigmoid(x):
    return 1.0 / (1.0 + jnp.exp2(x * -LOG2E))


def colsum(x):
    return jnp.sum(x, axis=0, keepdims=True)


def fold(x):
    total = x[0:8]
    for i in range(8, x.shape[0], 8):
        total = total + x[i : i + 8]
    return total


def plus(a, b):
    return b if a is None else a + b


def column(c):
    return slice(c * LANES, (c + 1) * LANES)


def ones_block(rows):
    return jnp.where(iota((rows, LANES), 1) < 3, 1.0, 0.0).astype(BF16)


def bias_rows(bias, rows):
    hi, lo = split(bias)
    low = (bias - hi.astype(F32) - lo.astype(F32)).astype(BF16)
    place = iota((rows, bias.shape[1]), 0)
    zero = jnp.zeros((rows, bias.shape[1]), F32)
    out = jnp.where(place == 0, hi.astype(F32), zero)
    out = jnp.where(place == 1, lo.astype(F32), out)
    return jnp.where(place == 2, low.astype(F32), out).astype(BF16)


def item_ends(len_ref):
    ends, total = [], jnp.int32(0)
    for k in range(len_ref.shape[0]):
        total = total + len_ref[k]
        ends.append(total)
    return ends


def boundary(ends, start):
    ahead = jnp.where(start - STEP >= 0, 0, -1)
    for end in ends:
        ahead = ahead + (end <= start - STEP).astype(jnp.int32)
    edge = jnp.int32(0)
    for k, end in enumerate(ends):
        edge = jnp.where(ahead == k, end, edge)
    return edge, ahead


def item_rows(ahead, items):
    return jnp.maximum(ahead, 0), jnp.minimum(ahead + 1, items - 1)


def lane_items(ahead, items):
    lane = iota((1, LANES), 1)
    return (lane == ahead).astype(F32), (lane == ahead + 1).astype(F32)


def put_statistics(msg_ref, sums, squares, counts, onehot):
    groups = sums.shape[0]
    count = counts[:, :1]
    safe = jnp.maximum(count, 1.0)
    total = jnp.sum(jnp.sum(sums, axis=0), axis=1, keepdims=True)
    number = count * (groups * LANES)
    mean = total / jnp.maximum(number, 1.0)
    spread = 0.0
    for g in range(groups):
        away = sums[g] / safe - mean
        spread = spread + squares[g] + count * away * away
    spread = jnp.sum(spread, axis=1, keepdims=True)
    item_sum = colsum(onehot * total)
    item_number = colsum(onehot * number)
    item_mean = item_sum / jnp.maximum(item_number, 1.0)
    away = mean - item_mean
    item_spread = colsum(onehot * (spread + number * away * away))
    msg = cat(
        [item_sum, item_spread, item_number, item_mean, jnp.zeros((4, LANES), F32)], 0
    )
    for i in range(msg_ref.shape[0]):
        msg_ref[i] = msg


def to_rows(row, items_padded):
    wide = jnp.broadcast_to(row, (items_padded, LANES))
    own = iota((items_padded, LANES), 0) == iota((items_padded, LANES), 1)
    column = jnp.sum(jnp.where(own, wide, 0.0), axis=1, keepdims=True)
    return jnp.broadcast_to(column, (items_padded, LANES))


def merge_statistics(msg_ref, table_ref):
    msg = msg_ref[...]
    item_sum = jnp.sum(msg[:, 0:1, :], axis=0)
    number = jnp.sum(msg[:, 2:3, :], axis=0)
    mean = item_sum / jnp.maximum(number, 1.0)
    away = msg[:, 3:4, :] - mean[None]
    squares = jnp.sum(msg[:, 1:2, :] + msg[:, 2:3, :] * away * away, axis=0)
    inverse = lax.rsqrt(squares / jnp.maximum(number, 1.0) + EPS)
    padded = table_ref.shape[1]
    table_ref[0] = to_rows(mean, padded)
    table_ref[1] = to_rows(inverse, padded)


def put_entry(refs, groups, entry, sums, squares, number, hot):
    sums_ref, squares_ref, counts_ref, onehot_ref = refs
    row = pl.ds(entry, 1)
    for g in range(groups):
        sums_ref[g, row, :] = sums[g]
        squares_ref[g, row, :] = squares[g]
    counts_ref[row, :] = jnp.full((1, LANES), number, F32)
    onehot_ref[row, :] = hot


def general_entries(refs, acts, after, before, n_after, n_before, entry, ahead):
    hot_b, hot_a = lane_items(ahead, 0)
    for part, keep, number, hot in ((0, before, n_before, hot_b), (1, after, n_after, hot_a)):
        sums, squares = [], []
        for act in acts:
            total = colsum(jnp.where(keep, act, 0.0))
            away = act - total / jnp.maximum(number, 1.0)
            sums.append(total)
            squares.append(colsum(jnp.where(keep, away * away, 0.0)))
        put_entry(refs, len(acts), 2 * entry + part, sums, squares, number, hot)


def prep_kernel(
    top_ref, bottom_ref, cot_ref, w_in_ref, w_out_ref, w_mask_ref, b_in, slope_in, gain_in, beta_in, w_depth, b_depth,
    slope_mid, gain_mid, beta_mid, b_mask, pack_ref, wide_ref, low_ref, high_ref,
):
    pack_ref[0:128, :] = w_in_ref[...]
    vectors = (b_in, slope_in, gain_in, beta_in, w_depth, b_depth, slope_mid, gain_mid, beta_mid)
    bias = b_mask[...]
    pack_ref[128:144, :] = cat(
        [ref[...] for ref in vectors] + [bias[:, 0:128], bias[:, 128:256], jnp.zeros((3, LANES), F32)], 0
    )
    for k in range(2):
        wide_ref[128 * k : 128 * (k + 1), :] = w_out_ref[:, column(k)]
        wide_ref[128 * (k + 2) : 128 * (k + 3), :] = w_mask_ref[:, column(k)]
    low_ref[0:T, :] = top_ref[...]
    low_ref[T : T + 8, :] = cat([cot_ref[...], jnp.zeros((6, LANES), F32)], 0)
    high_ref[...] = bottom_ref[...]


def first_kernel(len_ref, mix_ref, w_in_ref, b_in, slope_in, msg_ref, sums, squares, counts, onehot):
    step = pl.program_id(0)
    last = pl.num_programs(0) - 1
    tiles = mix_ref.shape[0] // T1
    ends = item_ends(len_ref)
    weights = two_of(split(w_in_ref[...]), 0)
    slope = slope_in[...]
    keep = 1.0 - slope
    bias = b_in[...]
    refs = (sums, squares, counts, onehot)
    for t in range(tiles):
        j = step * tiles + t
        start = lax.axis_index("tm") * ((last + 1) * tiles * T1) + j * T1
        edge, ahead = boundary(ends, start)
        hidden = mm(three(split(mix_ref[t * T1 : (t + 1) * T1, :]), 1), weights)
        pieces, total = [], None
        for i in range(0, T1, ROWS):
            x = hidden[i : i + ROWS] + bias
            act = x * (slope + keep * sigmoid(x))
            pieces.append(act)
            total = plus(total, fold(act))
        total = colsum(total)
        mean = total / T1
        square = None
        for act in pieces:
            away = act - mean
            square = plus(square, fold(away * away))
        put_entry(refs, 1, 2 * j, [total], [colsum(square)], jnp.float32(T1), lane_items(ahead, 0)[0])
        nothing = jnp.zeros((1, LANES), F32)
        put_entry(refs, 1, 2 * j + 1, [nothing], [nothing], jnp.float32(0.0), nothing)

        @pl.when(edge < start + T1)
        def _():
            offset = iota((T1, LANES), 0) + (start - edge)
            n_before = jnp.clip(edge - start, 0, T1).astype(F32)
            act = cat(pieces, 0)
            general_entries(refs, [act], offset >= 0, offset < 0, T1 - n_before, n_before, j, ahead)

    @pl.when(step == last)
    def _():
        put_statistics(msg_ref, sums[...], squares[...], counts[...], onehot[...])


def depth_kernel(
    len_ref, msg_in_ref, mix_ref, prev_ref, next_ref, own_ref, core_ref, x_ref, far_ref,
    hidden_ref, depth_ref, msg_ref, vec_ref, table_ref,
    gathered, sems, weights, ring, sums, squares, counts, onehot,
):
    m = pl.program_id(0)
    last = pl.num_programs(0) - 1
    items = len_ref.shape[0]
    me = lax.axis_index("src")
    half = me & 1
    own_rows = (last - 1) * T

    @pl.when(m == 0)
    def _():
        copies = [
            pltpu.make_async_copy(ref, gathered.at[half ^ k], sems.at[k])
            for k, ref in enumerate((own_ref, core_ref, x_ref, far_ref))
        ]
        for copy in copies:
            copy.start()
        merge_statistics(msg_in_ref, table_ref)
        for ref in (sums, squares, counts, onehot):
            ref[...] = jnp.zeros_like(ref)
        for copy in copies:
            copy.wait()
        for s in range(4):
            cut = column(s)
            weights[0:384, cut] = two_of(split(gathered[s, 0:128, :]), 0)
            weights[384:512, cut] = bias_rows(gathered[s, 128:129, :], 128)
            vec_ref[:, cut] = gathered[s, 128 : 128 + NVEC, :]

    def vec(row, c):
        return vec_ref[row : row + 1, column(c)]

    ends = item_ends(len_ref)
    base = lax.axis_index("tm") * (2 * own_rows) + half * own_rows
    start = base + (m - 1) * T
    edge, ahead = boundary(ends, start)
    alone = edge >= start + T
    block = half * (own_rows // T) + m - 1
    top = 2 * (own_rows // T)
    new, old = m & 1, 1 - (m & 1)

    def norm_rows(alone):
        place = pl.multiple_of(jnp.clip(block, 0, top - 1) * T, T)
        mix = mix_ref[pl.ds(place, T), :]
        mix = jnp.where(block < 0, prev_ref[...], jnp.where(block >= top, next_ref[0:T, :], mix))
        mixed = split(mix)
        hidden = mm(cat([mixed[0], mixed[1], mixed[0], ones_block(T)], 1), weights[...])
        hidden_ref[...] = hidden
        row_b, row_a = item_rows(ahead, items)
        rows = iota((ROWS, LANES), 0) + (start - edge)
        for c in range(4):
            slope = vec(1, c)
            keep = 1.0 - slope
            scale_b = table_ref[1, pl.ds(row_b, 1), :] * vec(2, c)
            shift_b = vec(3, c) - table_ref[0, pl.ds(row_b, 1), :] * scale_b
            scale_a = table_ref[1, pl.ds(row_a, 1), :] * vec(2, c)
            shift_a = vec(3, c) - table_ref[0, pl.ds(row_a, 1), :] * scale_a
            for i in range(0, T, ROWS):
                x = hidden[i : i + ROWS, column(c)]
                act = x * (slope + keep * sigmoid(x))
                if alone:
                    value = act * scale_b + shift_b
                else:
                    after = rows + i >= 0
                    value = act * jnp.where(after, scale_a, scale_b) + jnp.where(after, shift_a, shift_b)
                ring[new, i : i + ROWS, column(c)] = value

    pl.when(alone)(lambda: norm_rows(True))
    pl.when(jnp.logical_not(alone))(lambda: norm_rows(False))

    begin = start - STEP
    edge2, ahead2 = boundary(ends, begin)
    plain = edge2 >= begin + T + STEP
    refs = (sums, squares, counts, onehot)

    def filtered(c, i, lower_weight, upper_weight):
        lower = ring[old, i : i + ROWS, column(c)]
        upper = ring[new, i : i + ROWS, column(c)]
        if i < STEP:
            middle = ring[old, i + STEP : i + STEP + ROWS, column(c)]
        else:
            middle = ring[new, i - STEP : i - STEP + ROWS, column(c)]
        return lower_weight * lower + vec(5, c) * middle + upper_weight * upper + vec(7, c)

    @pl.when((m > 0) & plain)
    def _():
        in_low = jnp.where(m > 1, 1.0, 0.0)
        in_high = jnp.where(m < last, 1.0, 0.0)
        number = STEP * (in_low + in_high)
        all_sums, all_squares = [], []
        for c in range(4):
            slope = vec(8, c)
            keep = 1.0 - slope
            acts, halves = [], [None, None]
            for i in range(0, T, ROWS):
                depth = filtered(c, i, vec(4, c), vec(6, c))
                depth_ref[i : i + ROWS, column(c)] = depth
                act = depth * (slope + keep * sigmoid(depth))
                acts.append(act)
                halves[i // STEP] = plus(halves[i // STEP], fold(act))
            total = in_low * colsum(halves[0]) + in_high * colsum(halves[1])
            mean = total / number
            halves = [None, None]
            for i, act in enumerate(acts):
                away = act - mean
                halves[i * ROWS // STEP] = plus(halves[i * ROWS // STEP], fold(away * away))
            all_sums.append(total)
            all_squares.append(in_low * colsum(halves[0]) + in_high * colsum(halves[1]))
        put_entry(refs, 4, 2 * (m - 1), all_sums, all_squares, number, lane_items(ahead2, 0)[0])

    @pl.when((m > 0) & jnp.logical_not(plain))
    def _():
        low = jnp.where(m == 1, STEP, 0)
        high = jnp.where(m == last, STEP, T)
        rows = iota((ROWS, LANES), 0) + (begin - edge2)
        acts = []
        for c in range(4):
            slope = vec(8, c)
            pieces = []
            for i in range(0, T, ROWS):
                offset = rows + i
                lower_weight = jnp.where((offset >= 0) & (offset < STEP), 0.0, vec(4, c))
                upper_weight = jnp.where((offset < 0) & (offset >= -STEP), 0.0, vec(6, c))
                depth = filtered(c, i, lower_weight, upper_weight)
                depth_ref[i : i + ROWS, column(c)] = depth
                pieces.append(depth * (slope + (1.0 - slope) * sigmoid(depth)))
            acts.append(cat(pieces, 0))
        row = iota((T, LANES), 0)
        own = (row >= low) & (row < high)
        offset = row + (begin - edge2)
        n_before = jnp.clip(edge2 - begin, low, high) - low
        n_after = (high - low - n_before).astype(F32)
        general_entries(
            refs, acts, own & (offset >= 0), own & (offset < 0), n_after, n_before.astype(F32), m - 1, ahead2
        )

    @pl.when(m == last)
    def _():
        put_statistics(msg_ref, sums[...], squares[...], counts[...], onehot[...])


def mask_kernel(
    len_ref, msg_in_ref, *refs,
):
    depth_refs = refs[: TM // STEP]
    (
        mix_ref, skip_ref, enc_ref, cot_ref, wave_cot_ref, wave_next_ref, edge_next_ref, basis_ref, vec_ref,
        b_out_ref, slope_skip_ref, own_ref, core_ref, x_ref, far_ref,
        block_ref, grad_skip_ref, grad_enc_ref, send_ref, wave_ref, r_ref, up_ref, down_ref, keep_ref, give_ref,
        msg_ref, table_ref,
        gathered, sems, w_out, w_out_t, w_mask, w_mask_t, decode, basis_back, select_hi, select_lo, normed_ref,
        pull_ref, carry, acc_out, acc_mask, acc_basis, acc_vec,
        acc_small, entries, onehot,
    ) = refs[TM // STEP :]
    j = pl.program_id(0)
    last = pl.num_programs(0) - 1
    items = len_ref.shape[0]
    me = lax.axis_index("src")
    half = me & 1
    side = me >> 1
    own_rows = (last + 1) * TM

    def vec(row, c):
        return vec_ref[row : row + 1, column(c)]

    @pl.when(j == 0)
    def _():
        copies = [
            pltpu.make_async_copy(ref, gathered.at[half ^ k], sems.at[k])
            for k, ref in enumerate((own_ref, core_ref, x_ref, far_ref))
        ]
        for copy in copies:
            copy.start()
        merge_statistics(msg_in_ref, table_ref)
        for ref in (acc_out, acc_mask, acc_basis, acc_vec, acc_small, carry, entries):
            ref[...] = jnp.zeros_like(ref)
        basis = split(basis_ref[...])
        b_hi, b_lo = basis
        col = iota((L, 2 * LANES), 1)
        row = iota((L, 2 * LANES), 0)
        spread = ((col & 7) == (row & 7)) & ((col >> 7) == (row >> 3))
        spread = spread.astype(F32).astype(BF16)
        wide = (mm_tn(b_hi, spread).astype(BF16), mm_tn(b_lo, spread).astype(BF16))
        for n in range(2):
            decode[n] = two_of([part[n * 256 : (n + 1) * 256] for part in wide], 0)
        for c in range(2):
            row = iota((LANES, L), 0) - 48 * c
            col = iota((LANES, L), 1)
            with_hi = ((row == col) | (row == col + 32)).astype(F32).astype(BF16)
            with_lo = (row == col + 16).astype(F32).astype(BF16)
            back = mm(with_hi, b_hi) + mm(with_lo, b_lo)
            basis_back[:, c * HIDDEN : (c + 1) * HIDDEN] = back.astype(BF16)
            row = iota((2 * LANES, LANES), 0)
            col = iota((2 * LANES, LANES), 1) - 48 * c
            place = (row & 7) + ((row >> 7) << 3)
            select_hi[c] = ((col == place) | (col == place + 16)).astype(F32).astype(BF16)
            select_lo[c] = (col == place + 32).astype(F32).astype(BF16)
        for copy in copies:
            copy.wait()
        for s in range(4):
            cut = column(s)
            for k in range(2):
                part = gathered[s, column(k), :]
                hi, lo = split(part)
                for place, value in ((0, hi), (256, hi), (512, lo)):
                    place = place + (s >> 1) * 768 + (s & 1) * 128
                    w_out[place : place + 128, column(k)] = value
                hi, lo = split(part.T)
                for place, value in ((0, hi), (256, hi), (512, lo)):
                    w_out_t[place + k * 128 : place + (k + 1) * 128, cut] = value
                part = gathered[s, column(2 + k), :]
                wide = slice(s * 256 + k * LANES, s * 256 + (k + 1) * LANES)
                w_mask[0:384, wide] = two_of(split(part * -LOG2E), 0)
                w_mask[384:512, wide] = bias_rows(vec_ref[11 + k : 12 + k, cut] * -LOG2E, 128)
                hi, lo = split(part.T)
                for place in (0, 256):
                    w_mask_t[s >> 1, s & 1, place + k * 128 : place + (k + 1) * 128, 0:128] = hi
                    w_mask_t[s >> 1, s & 1, place + k * 128 : place + (k + 1) * 128, 128:256] = lo

    ends = item_ends(len_ref)
    start = lax.axis_index("tm") * (2 * own_rows) + half * own_rows + j * TM
    edge, ahead = boundary(ends, start)
    row_b, row_a = item_rows(ahead, items)
    offset = iota((TM, LANES), 0) + (start - edge)

    after = offset >= 0
    inv_b, inv_a = table_ref[1, pl.ds(row_b, 1), :], table_ref[1, pl.ds(row_a, 1), :]
    shift_b, shift_a = -inv_b * table_ref[0, pl.ds(row_b, 1), :], -inv_a * table_ref[0, pl.ds(row_a, 1), :]
    inv = jnp.where(after, inv_a, inv_b)
    shift = jnp.where(after, shift_a, shift_b)
    norms = [[], []], [[], []]
    for c in range(4):
        slope = vec(8, c)
        keep = 1.0 - slope
        his, los = [], []
        for i in range(0, TM, ROWS):
            rows = slice(i, i + ROWS)
            depth = depth_refs[i // STEP][i % STEP : i % STEP + ROWS, column(c)]
            s = sigmoid(depth)
            part = keep * s
            mild = slope + part
            normed = depth * mild * inv[rows] + shift[rows]
            normed_ref[rows, column(c)] = normed
            pull_ref[rows, column(c)] = mild + part * (depth * (1.0 - s))
            hi, lo = split(normed * vec(9, c) + vec(10, c))
            his.append(hi)
            los.append(lo)
        norms[c >> 1][0].append(cat(his, 0))
        norms[c >> 1][1].append(cat(los, 0))
    branch = [
        mm(cat(his + los + his, 1), w_out[768 * k : 768 * (k + 1), :]) for k, (his, los) in enumerate(norms)
    ]
    branch = branch[0] + branch[1]
    slope_skip = slope_skip_ref[...]
    keep = 1.0 - slope_skip
    totals, skips, actives = [], [], []
    for i in range(0, TM, ROWS):
        rows = slice(i, i + ROWS)
        block = mix_ref[rows, :] + (branch[rows, 0:128] + b_out_ref[:, 0:128])
        block_ref[rows, :] = block
        send_ref[rows, 0:128] = block
        total = skip_ref[rows, :] + (branch[rows, 128:256] + b_out_ref[:, 128:256])
        s = sigmoid(total)
        part = keep * s
        mild = slope_skip + part
        rest = total * (1.0 - s)
        totals.append(rest)
        skips.append(mild + part * rest)
        actives.append(split(total * mild))
    a_hi, a_lo = cat([a for a, _ in actives], 0), cat([a for _, a in actives], 0)
    query = cat([a_hi, a_lo, a_hi, ones_block(TM)], 1)

    lane_frame = iota((16, LANES), 1) >> 3
    frame = iota((16, LANES), 0)
    here = jnp.where(lane_frame == frame, 1.0, 0.0)
    coming = jnp.where(lane_frame == ((frame + 1) & 15), 1.0, 0.0)
    final_row = frame == 15
    packed = None
    waves = [wave_cot_ref[0:1, :], wave_cot_ref[1:2, :]]
    finals = [
        jnp.where((half == 1) & (j == last), edge_next_ref[T + c : T + c + 1, :], wave_next_ref[c : c + 1, :])
        for c in range(2)
    ]
    for c in range(2):
        wave = jnp.where(side == 0, waves[c], waves[1 - c])
        final = jnp.where(side == 0, finals[c], finals[1 - c])
        for part, select in zip(split(cat([wave, final], 1)), (select_hi, select_lo)):
            part = part.astype(F32)
            lines = [part[:, column(q)] for q in range(TM // 16 + 1)]
            pieces = []
            for q in range(TM // 16):
                following = jnp.where(final_row, lines[q + 1], lines[q]) * coming
                pieces.append(cat([lines[q] * here, following], 1).astype(BF16))
            packed = plus(packed, mm(cat(pieces, 0), select[c]))
    lane = iota((1, LANES), 1)
    lane = jnp.where(lane < 48, lane, lane - 48)
    packed = jnp.where((offset == -1) & ((lane & 15) >= 8), 0.0, packed).astype(BF16)

    decoded = [None, None]
    back = [None, None]
    masked, grads_hi, grads_lo = [[], []], [], []
    chunks = [[slice(c * HIDDEN + n * 256, c * HIDDEN + (n + 1) * 256) for c in range(2)] for n in range(2)]
    all_grads = [[mm(packed, basis_back[:, chunk]) for chunk in pair] for pair in chunks]
    all_logits = [[mm(query, w_mask[:, chunk]) for chunk in pair] for pair in chunks]
    for n in range(2):
        logits, grads = all_logits[n], all_grads[n]
        blocks = [[[], []] for _ in range(4)]
        for b in range(2):
            col = column(2 * n + b)
            bias_sum = None
            pieces = [[[], []] for _ in range(4)]
            for i in range(0, TM, ROWS):
                rows = slice(i, i + ROWS)
                enc = enc_ref[rows, col]
                grad_enc = None
                for c in range(2):
                    mask = 1.0 / (1.0 + jnp.exp2(logits[c][rows, column(b)]))
                    grad = grads[c][rows, column(b)]
                    grad_enc = plus(grad_enc, grad * mask)
                    value = mask * enc
                    for k, part in enumerate(split(value)):
                        pieces[c][k].append(part)
                    grad_logits = grad * value * (1.0 - mask)
                    if c == 0:
                        bias_sum = plus(bias_sum, fold(grad_logits))
                    for k, part in enumerate(split(grad_logits)):
                        pieces[2 + c][k].append(part)
                grad_enc_ref[rows, col] = grad_enc
                send_ref[rows, 256 + (2 * n + b) * 128 : 256 + (2 * n + b + 1) * 128] = grad_enc
            acc_vec[2:3, (2 * n + b) * 128 : (2 * n + b + 1) * 128] += colsum(bias_sum)
            for block, piece in zip(blocks, pieces):
                for k in range(2):
                    block[k].append(cat(piece[k], 0))
        for c in range(2):
            hi, lo = blocks[c]
            masked[c].append(cat(hi + lo, 1))
            decoded[c] = plus(decoded[c], mm(cat(hi + lo + hi, 1), decode[n]))
            hi, lo = blocks[2 + c]
            back[c] = plus(back[c], mm(cat(hi + lo, 1), w_mask_t[c, n]))
            if c == 0:
                grads_hi = grads_hi + hi
                grads_lo = grads_lo + lo
    back = back[0] + back[1]
    own_grads = cat(grads_hi + grads_lo, 1)

    pieces, along, cot_sum, skip_sum = [], None, None, None
    for k, i in enumerate(range(0, TM, ROWS)):
        rows = slice(i, i + ROWS)
        grad_active = back[rows, 0:128] + back[rows, 128:256]
        grad_skip = grad_active * skips[k]
        along = plus(along, fold(grad_active * totals[k]))
        grad_skip_ref[rows, :] = grad_skip
        send_ref[rows, 128:256] = grad_skip
        cot = cot_ref[rows, :]
        cot_sum = plus(cot_sum, fold(cot))
        skip_sum = plus(skip_sum, fold(grad_skip))
        pieces.append(split(cat([cot, grad_skip], 1)))
    acc_small[0:1, :] += colsum(along)
    acc_small[1:2, :] += colsum(cot_sum)
    acc_small[2:3, :] += colsum(skip_sum)
    g_hi, g_lo = cat([p for p, _ in pieces], 0), cat([p for _, p in pieces], 0)
    r_ref[...] = mm(three((g_hi, g_lo), 1), w_out_t[...])

    first_row = iota((8, LANES), 0) == 0
    waves = []
    for c in range(2):
        tail = decoded[c][:, 128:256]
        shifted = pltpu.roll(tail, 1, 0)
        shifted = cat([jnp.where(first_row, carry[c : c + 1, :], shifted[0:8]), shifted[8:]], 0)
        carry[c : c + 1, :] = tail[TM - 1 : TM, :]
        value = decoded[c][:, 0:128] + jnp.where(offset == 0, 0.0, shifted)
        lines = []
        for q in range(TM // 16):
            line = value[q * 16 : (q + 1) * 16] * here
            lines.append(colsum(line[0:8] + line[8:16]))
        waves.append(cat(lines, 1))
    wave_ref[0:1, :] = jnp.where(side == 0, waves[0], waves[1])
    wave_ref[1:2, :] = jnp.where(side == 0, waves[1], waves[0])

    @pl.when(j == 0)
    def _():
        down_ref[...] = r_ref[0:128, :]

    @pl.when(j == last)
    def _():
        up_ref[0:128, :] = r_ref[TM - 128 : TM, :]
        up_ref[128:136, :] = jnp.zeros((8, HIDDEN), F32)
        up_ref[128:129, 0:128] = jnp.where(side == 0, carry[0:1, :], carry[1:2, :])
        up_ref[129:130, 0:128] = jnp.where(side == 0, carry[1:2, :], carry[0:1, :])

    own_norms = cat(norms[0][0] + norms[0][1] + norms[0][0], 1)

    def weight_gradients(rows):
        for n in range(2):
            for c in range(2):
                values = masked[c][n]
                acc_basis[c, :, 256 * n : 256 * (n + 1)] += mm_tn(
                    cat([packed[rows]] * 2, 0), cat([values[rows, 0:256], values[rows, 256:512]], 0)
                )
            yield
        acc_mask[...] += mm_tn(
            three((a_hi[rows], a_lo[rows]), 0), two_of((own_grads[rows, 0:512], own_grads[rows, 512:1024]), 0)
        )
        yield
        acc_out[...] += mm_tn(
            cat([own_norms[rows, 256 * k : 256 * (k + 1)] for k in range(3)], 0), two_of((g_hi[rows], g_lo[rows]), 0)
        )
        yield

    for k in range(TM // T):
        rows = slice(k * T, (k + 1) * T)
        begin = start + k * T
        edge2, ahead2 = boundary(ends, begin)
        plain = edge2 >= begin + T + STEP
        entry = 2 * (j * (TM // T) + k)
        hot_b, hot_a = lane_items(ahead2, items)
        onehot[pl.ds(entry, 1), :] = hot_b
        onehot[pl.ds(entry + 1, 1), :] = hot_a
        row_b2, row_a2 = item_rows(ahead2, items)

        @pl.when(plain)
        def _():
            products = weight_gradients(rows)
            inverse = table_ref[1, pl.ds(row_b2, 1), :]
            lines = [[None] * 8, [None] * 8]
            for c in range(4):
                next(products)
                taps = vec(4, c) + vec(5, c) + vec(6, c)
                level = vec(7, c) + vec(3, c) * taps
                sums = [None] * 8
                for i in range(k * T, (k + 1) * T, ROWS):
                    cut = slice(i, i + ROWS)
                    r, normed, pull = r_ref[cut, column(c)], normed_ref[cut, column(c)], pull_ref[cut, column(c)]
                    depth = depth_refs[i // STEP][i % STEP : i % STEP + ROWS, column(c)] - level
                    pull_r, pull_n = pull * r, pull * normed
                    values = (
                        r, r * normed, pull_r, pull, pull_n, pull_r * depth, pull * depth, pull_n * depth,
                    )
                    sums = [plus(s, fold(value)) for s, value in zip(sums, values)]
                sums = [colsum(s) for s in sums]
                if c < 2:
                    acc_vec[0:1, column(c)] += sums[1]
                    acc_vec[1:2, column(c)] += sums[0]
                gain, flat = vec(9, c), vec(2, c) * taps * inverse
                scales = (gain, gain, flat * gain, flat, flat, inverse * gain, inverse, inverse)
                lines[c >> 1] = [plus(line, s * scale) for line, s, scale in zip(lines[c >> 1], sums, scales)]
            for i in range(8):
                entries[i, pl.ds(entry, 1), :] = lines[0][i] + lines[1][i]

        @pl.when(jnp.logical_not(plain))
        def _():
            products = weight_gradients(rows)
            place = iota((ROWS, LANES), 0) + (begin - k * T - edge2)
            inv_b, inv_a = table_ref[1, pl.ds(row_b2, 1), :], table_ref[1, pl.ds(row_a2, 1), :]
            before, behind = [None] * 8, [None] * 8
            for c in range(4):
                next(products)
                sum_r, sum_rn = None, None
                for i in range(k * T, (k + 1) * T, ROWS):
                    cut = slice(i, i + ROWS)
                    offset = place + i
                    after = offset >= 0
                    taps = jnp.where(after & (offset < STEP), 0.0, vec(4, c)) + vec(5, c)
                    taps = taps + jnp.where((offset < 0) & (offset >= -STEP), 0.0, vec(6, c))
                    r, normed = r_ref[cut, column(c)], normed_ref[cut, column(c)]
                    pull = pull_ref[cut, column(c)] * jnp.where(after, inv_a, inv_b)
                    depth = depth_refs[i // STEP][i % STEP : i % STEP + ROWS, column(c)]
                    flat = pull * (vec(2, c) * taps)
                    cross = pull * (depth - vec(7, c) - vec(3, c) * taps)
                    r_normed = r * normed
                    sum_r, sum_rn = plus(sum_r, fold(r)), plus(sum_rn, fold(r_normed))
                    q = r * vec(9, c)
                    values = (
                        q, q * normed, flat * q, flat, flat * normed, cross * q, cross, cross * normed,
                    )
                    before = [plus(s, fold(jnp.where(after, 0.0, value))) for s, value in zip(before, values)]
                    behind = [plus(s, fold(jnp.where(after, value, 0.0))) for s, value in zip(behind, values)]
                if c < 2:
                    acc_vec[0:1, column(c)] += colsum(sum_rn)
                    acc_vec[1:2, column(c)] += colsum(sum_r)
            for i in range(8):
                entries[i, pl.ds(entry, 1), :] = colsum(before[i])
                entries[i, pl.ds(entry + 1, 1), :] = colsum(behind[i])

    @pl.when(j == last)
    def _():
        hot = onehot[...]
        lines = [colsum(hot * jnp.sum(entries[i], axis=1, keepdims=True)) for i in range(8)]
        msg = cat(lines, 0)
        for i in range(msg_ref.shape[0]):
            msg_ref[i] = msg
        for ref, h in ((keep_ref, half), (give_ref, 1 - half)):
            own = pl.ds(pl.multiple_of(h * 128, 128), 128)
            ref[0:128, :] = acc_out[own, 0:128]
            ref[128:256, :] = acc_out[own, 128:256]
            for k in range(2):
                pair = pl.ds(pl.multiple_of(h * 256 + k * 128, 128), 128)
                ref[256 + 128 * k : 384 + 128 * k, :] = acc_mask[:, pair]
            bias = acc_vec[2:3, pl.ds(pl.multiple_of(h * 256, 256), 256)]
            ref[512:520, :] = cat(
                [
                    bias[:, 0:128], bias[:, 128:256], acc_vec[0:1, own], acc_vec[1:2, own],
                    acc_small[0:3, :], jnp.zeros((1, LANES), F32),
                ], 0,
            )
            for k in range(4):
                cut = column(k)
                ref[520 + 16 * k : 536 + 16 * k, :] = (acc_basis[0, 0:16, cut] + acc_basis[0, 32:48, cut]) + (
                    acc_basis[1, 48:64, cut] + acc_basis[1, 80:96, cut]
                )


def back_kernel(
    len_ref, msg_in_ref, depth_ref, r_a_ref, r_b_ref, low_ref, high_ref, hidden_ref, mix_ref, cot_ref,
    vec_ref, table_in_ref, table_mid_ref, own_ref, core_ref, x_ref, far_ref,
    grad_mix_ref, send_ref, keep_ref, give_ref, edge_ref,
    gathered, sems, table, weights, ring, acc_w, acc_vec,
):
    j = pl.program_id(0)
    last = pl.num_programs(0) - 1
    items = len_ref.shape[0]
    me = lax.axis_index("src")
    half = me & 1
    side = me >> 1
    own_rows = last * T

    def vec(row, c):
        return vec_ref[row : row + 1, column(c)]

    ends = item_ends(len_ref)

    @pl.when(j == 0)
    def _():
        copies = [
            pltpu.make_async_copy(ref.at[pl.ds(0, 128)], gathered.at[half ^ k], sems.at[k])
            for k, ref in enumerate((own_ref, core_ref, x_ref, far_ref))
        ]
        for copy in copies:
            copy.start()
        totals = 0.5 * jnp.sum(msg_in_ref[...], axis=0)
        lane = iota((1, LANES), 1)
        number = jnp.zeros((1, LANES), jnp.int32)
        for k in range(items):
            number = jnp.where(lane == k, len_ref[k], number)
        number = jnp.maximum(number.astype(F32) * HIDDEN, 1.0)
        m1 = totals[0:1] / number
        m2 = totals[1:2] / number
        p1 = (totals[2:3] - m1 * totals[3:4] - m2 * totals[4:5]) / number
        p2 = (totals[5:6] - m1 * totals[6:7] - m2 * totals[7:8]) / number
        padded = table.shape[1]
        for i, value in enumerate((m1, m2, p1, p2)):
            table[i] = to_rows(value, padded)
        acc_w[...] = jnp.zeros_like(acc_w)
        acc_vec[...] = jnp.zeros_like(acc_vec)
        edge_ref[...] = low_ref[128:136, 0:128]
        for copy in copies:
            copy.wait()
        for s in range(4):
            cut = column(s)
            hi, lo = split(gathered[s].T)
            for place in (0, 256):
                place = place + (s >> 1) * 512 + (s & 1) * 128
                weights[place : place + 128, 0:128] = hi
                weights[place : place + 128, 128:256] = lo

    base = lax.axis_index("tm") * (2 * own_rows) + half * own_rows
    new, old = j & 1, 1 - (j & 1)

    def chooser(begin, alone, edge, ahead):
        row_b, row_a = item_rows(ahead, items)

        def pick(ref, i):
            value_b = ref[i, pl.ds(row_b, 1), :]
            return value_b, value_b if alone else ref[i, pl.ds(row_a, 1), :]

        def choose(pair, i):
            if alone:
                return pair[0]
            return jnp.where(iota((ROWS, LANES), 0) + (begin - edge) + i >= 0, pair[1], pair[0])

        return pick, choose

    begin = base + j * T - STEP
    edge, ahead = boundary(ends, begin)
    alone = edge >= begin + T

    def filter_rows(alone):
        pick, choose = chooser(begin, alone, edge, ahead)
        means, inverses = pick(table_mid_ref, 0), pick(table_mid_ref, 1)
        firsts, seconds = pick(table, 0), pick(table, 1)
        shifts = tuple(-a * b for a, b in zip(means, inverses))
        firsts = tuple(a * b for a, b in zip(firsts, inverses))
        seconds = tuple(a * b for a, b in zip(seconds, inverses))
        for c in range(4):
            slope, gain = vec(8, c), vec(9, c)
            keep = 1.0 - slope
            halves = [None, None]
            for i in range(0, T, ROWS):
                if i < STEP:
                    r = jnp.where(j == 0, low_ref[i : i + ROWS, column(c)], r_a_ref[i : i + ROWS, column(c)])
                else:
                    cut = slice(i - STEP, i - STEP + ROWS)
                    r = jnp.where(j == last, high_ref[cut, column(c)], r_b_ref[cut, column(c)])
                depth = depth_ref[i : i + ROWS, column(c)]
                s = sigmoid(depth)
                u = depth * (1.0 - s)
                part = keep * s
                mild = slope + part
                inv = choose(inverses, i)
                normed = depth * mild * inv + choose(shifts, i)
                grad_act = r * (gain * inv) - choose(firsts, i) - normed * choose(seconds, i)
                if c < 2:
                    halves[i // STEP] = plus(halves[i // STEP], fold(grad_act * u))
                ring[new, i : i + ROWS, column(c)] = grad_act * (mild + part * u)
            if c < 2:
                in_low = jnp.where(j > 0, 1.0, 0.0)
                in_high = jnp.where(j < last, 1.0, 0.0)
                acc_vec[8:9, column(c)] += in_low * colsum(halves[0]) + in_high * colsum(halves[1])

    pl.when(alone)(lambda: filter_rows(True))
    pl.when(jnp.logical_not(alone))(lambda: filter_rows(False))

    start = base + (j - 1) * T
    edge2, ahead2 = boundary(ends, start)
    plain = edge2 >= start + T + STEP

    def norm_rows(plain):
        pick, choose = chooser(start, plain, edge2, ahead2)
        means, inverses = pick(table_in_ref, 0), pick(table_in_ref, 1)
        firsts, seconds = pick(table, 2), pick(table, 3)
        shifts = tuple(-a * b for a, b in zip(means, inverses))
        firsts = tuple(a * b for a, b in zip(firsts, inverses))
        seconds = tuple(a * b for a, b in zip(seconds, inverses))
        rows = iota((ROWS, LANES), 0) + (start - edge2)
        his, los = [[], [], [], []], [[], [], [], []]
        for c in range(4):
            slope, gain, bias = vec(1, c), vec(2, c), vec(3, c)
            keep = 1.0 - slope
            sums = [None] * 8
            for i in range(0, T, ROWS):
                cut = slice(i, i + ROWS)
                grad_low, grad_high = ring[old, cut, column(c)], ring[new, cut, column(c)]
                if i < STEP:
                    grad_mid = ring[old, i + STEP : i + STEP + ROWS, column(c)]
                else:
                    grad_mid = ring[new, i - STEP : i - STEP + ROWS, column(c)]
                if not plain:
                    offset = rows + i
                    grad_low = jnp.where((offset >= 0) & (offset < STEP), 0.0, grad_low)
                    grad_high = jnp.where((offset < 0) & (offset >= -STEP), 0.0, grad_high)
                grad_norm = vec(5, c) * grad_mid + vec(4, c) * grad_high + vec(6, c) * grad_low
                hidden = hidden_ref[cut, column(c)]
                s = sigmoid(hidden)
                u = hidden * (1.0 - s)
                part = keep * s
                mild = slope + part
                inv = choose(inverses, i)
                normed = hidden * mild * inv + choose(shifts, i)
                grad_act = grad_norm * (gain * inv) - choose(firsts, i) - normed * choose(seconds, i)
                grad_hidden = grad_act * (mild + part * u)
                if c < 2:
                    norm = normed * gain + bias
                    values = (
                        grad_hidden, grad_act * u, grad_norm * normed, grad_norm, norm * grad_high, norm * grad_mid,
                        norm * grad_low, grad_mid,
                    )
                    sums = [plus(s, fold(value)) for s, value in zip(sums, values)]
                hi, lo = split(grad_hidden)
                his[c].append(hi)
                los[c].append(lo)
            if c < 2:
                acc_vec[0:8, column(c)] += cat([colsum(s) for s in sums], 0)
        hi, lo = [cat(p, 0) for p in his], [cat(p, 0) for p in los]
        own = mm(cat(hi[0:2] + lo[0:2], 1), weights[0:512, :])
        back = own + mm(cat(hi[2:4] + lo[2:4], 1), weights[512:1024, :])
        grad_mix = cot_ref[...] + (back[:, 0:128] + back[:, 128:256])
        grad_mix_ref[...] = grad_mix
        send_ref[...] = grad_mix
        mixed = cat(split(mix_ref[...]), 1)
        acc_w[...] += mm_tn(cat([cat(hi[0:2], 1), cat(lo[0:2], 1)], 1), mixed)

    pl.when((j > 0) & plain)(lambda: norm_rows(True))
    pl.when((j > 0) & jnp.logical_not(plain))(lambda: norm_rows(False))

    @pl.when(j == last)
    def _():
        for ref, h in ((keep_ref, half), (give_ref, 1 - half)):
            own = pl.ds(pl.multiple_of(h * 128, 128), 128)
            rest = pl.ds(pl.multiple_of(256 + h * 128, 128), 128)
            ref[0:128, :] = (acc_w[own, 0:128] + (acc_w[own, 128:256] + acc_w[rest, 0:128])).T
            ref[128:144, :] = acc_vec[:, own]


def pass_kernel(len_ref, got_ref, block_in, skip_in, enc_in, block_ref, skip_ref, enc_ref):
    block_ref[...] = got_ref[:, 0:128]
    skip_ref[...] = got_ref[:, 128:256]
    enc_ref[...] = got_ref[:, 256:768]


def merge_kernel(len_ref, got_ref, mix_in, mine_ref, other_ref, edge_ref, edge_other_ref, mix_ref, wave_ref):
    me = lax.axis_index("src")
    half = me & 1
    mix_ref[...] = got_ref[...]
    width = mine_ref.shape[1]
    frames = width // STRIDE
    base = lax.axis_index("tm") * (2 * frames)
    ends = item_ends(len_ref)
    lane = iota((2, LANES), 1)
    for part, edge, h in ((mine_ref, edge_ref, half), (other_ref, edge_other_ref, 1 - half)):
        place = base + h * frames
        new = place == 0
        for end in ends:
            new = new | (end == place)
        place = pl.multiple_of(h * width, width)
        wave_ref[:, pl.ds(place, width)] = part[...]
        first = part[:, 0:128] + jnp.where((lane < STRIDE) & jnp.logical_not(new), edge[0:2, :], 0.0)
        wave_ref[:, pl.ds(place, LANES)] = first


def last_kernel(
    a_ref, b_ref, c_ref, d_ref, w_in, b_in, slope_in, gain_in, beta_in, w_depth, b_depth, slope_mid,
    gain_mid, beta_mid, w_out, b_out, slope_skip, w_mask, b_mask, basis,
):
    late = a_ref[...] + b_ref[...]
    w_in[...] = late[0:128]
    for ref, row in (
        (b_in, 128), (slope_in, 129), (gain_in, 130), (beta_in, 131), (b_depth, 135), (slope_mid, 136),
    ):
        ref[...] = late[row : row + 1]
    w_depth[...] = late[132:135]
    early = c_ref[...] + d_ref[...]
    w_out[:, 0:128] = early[0:128]
    w_out[:, 128:256] = early[128:256]
    w_mask[:, 0:128] = early[256:384]
    w_mask[:, 128:256] = early[384:512]
    b_mask[:, 0:128] = early[512:513]
    b_mask[:, 128:256] = early[513:514]
    gain_mid[...] = early[514:515]
    beta_mid[...] = early[515:516]
    slope_skip[...] = early[516:517]
    b_out[:, 0:128] = early[517:518]
    b_out[:, 128:256] = early[518:519]
    for k in range(4):
        basis[:, column(k)] = early[520 + 16 * k : 536 + 16 * k]


def local(
    mix_in, skip_in, encoded, lengths, w_in, b_in, slope_in, gain_in, beta_in, w_depth, b_depth, slope_mid, gain_mid,
    beta_mid, w_out, b_out, slope_skip, w_mask, b_mask, basis, cot_out, cot_wave,
):
    n_tm, n_src = lax.axis_size("tm"), lax.axis_size("src")
    devices = n_tm * n_src
    frames = mix_in.shape[0]
    own_rows = frames // 2
    items = lengths.shape[0]
    padded = -(-items // 8) * 8
    tiles = own_rows // T
    tiles_m = own_rows // TM
    up = [(i, i + 1) for i in range(n_tm - 1)]
    down = [(j, i) for i, j in up]
    swap = [(i, i ^ 1) for i in range(n_src)]
    cross = [(i, i ^ 2) for i in range(n_src)]

    def half():
        return lax.axis_index("src") & 1

    def struct(*shape):
        return jax.ShapeDtypeStruct(shape, F32)

    def whole(*shape):
        zeros = (0,) * len(shape)
        return pl.BlockSpec(shape, lambda i, n: zeros)

    anywhere = pl.BlockSpec(memory_space=pl.ANY)

    def vmem(*shape):
        return pltpu.VMEM(shape, F32)

    def vmem16(*shape):
        return pltpu.VMEM(shape, BF16)

    def call(kernel, name, grid, in_specs, out_specs, out_shape, scratch, us, **kw):
        return pl.pallas_call(
            kernel,
            grid_spec=pltpu.PrefetchScalarGridSpec(
                num_scalar_prefetch=1, grid=(grid,), in_specs=in_specs, out_specs=out_specs, scratch_shapes=scratch
            ),
            out_shape=out_shape,
            compiler_params=pltpu.CompilerParams(
                vmem_limit_bytes=VMEM, dimension_semantics=("arbitrary",)
            ),
            cost_estimate=pl.CostEstimate(flops=0, bytes_accessed=us * 3_600_000, transcendentals=0),
            name=name,
            **kw,
        )

    msg_shape = (devices, 8, LANES)
    message = struct(*msg_shape)

    def exchange(msg):
        return lax.all_to_all(msg, ("tm", "src"), 0, 0)

    def line(vector):
        return vector.reshape(1, -1)

    def fixed(*shape):
        return pl.BlockSpec(shape, lambda i: (0,) * len(shape))

    n1 = frames // T1
    vectors = (
        line(b_in), line(slope_in), line(gain_in), line(beta_in), w_depth, line(b_depth), line(slope_mid),
        line(gain_mid), line(beta_mid), line(b_mask),
    )
    pack, wide, low, high = pl.pallas_call(
        prep_kernel,
        grid=(1,),
        in_specs=[
            fixed(T, 128), pl.BlockSpec((T, 128), lambda i: (frames // T - 1, 0)), fixed(2, LANES), fixed(128, 128),
            fixed(128, 256), fixed(128, 256), *[fixed(*v.shape) for v in vectors],
        ],
        out_specs=[fixed(PACK_IN, 128), fixed(512, 128), fixed(T + 8, 128), fixed(T, 128)],
        out_shape=[struct(PACK_IN, 128), struct(512, 128), struct(T + 8, 128), struct(T, 128)],
        compiler_params=pltpu.CompilerParams(vmem_limit_bytes=VMEM),
        name="prep",
    )(mix_in, mix_in, cot_wave, w_in, w_out, w_mask, *vectors)
    pack_x = lax.ppermute(pack, "src", cross)
    pack_core = lax.ppermute(pack, "src", swap)
    mix_prev = lax.ppermute(high, "tm", up)
    mix_next = lax.ppermute(low, "tm", down)
    msg1 = call(
        first_kernel, "first", 2,
        [pl.BlockSpec((frames // 2, 128), lambda i, n: (i, 0)), whole(128, 128), whole(1, 128), whole(1, 128)],
        whole(*msg_shape), message,
        [vmem(1, 2 * n1, 128), vmem(1, 2 * n1, 128), vmem(2 * n1, 128), vmem(2 * n1, 128)], 4,
    )(lengths, mix_in, w_in, line(b_in), line(slope_in))
    msg1, pack_x, pack_core, mix_prev, mix_next = lax.optimization_barrier(
        (msg1, pack_x, pack_core, mix_prev, mix_next)
    )
    pack_far = lax.ppermute(pack_x, "src", swap)
    packs = (pack, pack_core, pack_x, pack_far)
    msg1 = exchange(msg1)
    wide_x = lax.ppermute(wide, "src", cross)
    wide_core = lax.ppermute(wide, "src", swap)
    wide_far = lax.ppermute(wide_x, "src", swap)
    wides = (wide, wide_core, wide_x, wide_far)

    entries = -(-2 * (tiles + 1) // 8) * 8
    hidden, depth, msg2, vec, table_in = call(
        depth_kernel, "depth", tiles + 2,
        [
            whole(*msg_shape),
            whole(frames, 128), whole(T, 128), whole(T + 8, 128), anywhere, anywhere, anywhere, anywhere,
        ],
        [
            pl.BlockSpec((T, HIDDEN), lambda i, n: (i, 0)),
            pl.BlockSpec((T, HIDDEN), lambda i, n: (jnp.maximum(i - 1, 0), 0)),
            whole(*msg_shape), whole(NVEC, HIDDEN), whole(2, padded, LANES),
        ],
        [
            struct(own_rows + 2 * T, HIDDEN), struct(own_rows + T, HIDDEN), message, struct(NVEC, HIDDEN),
            struct(2, padded, LANES),
        ],
        [
            vmem(4, PACK_IN, 128), pltpu.SemaphoreType.DMA((4,)), vmem16(512, HIDDEN), vmem(2, T, HIDDEN),
            vmem(4, entries, 128), vmem(4, entries, 128), vmem(entries, 128), vmem(entries, 128),
        ], 8,
    )(lengths, msg1, mix_in, mix_prev, mix_next, *packs)
    msg2 = exchange(msg2)

    def half_rows(width):
        return pl.BlockSpec((TM, width), lambda i, n: (half() * tiles_m + i, 0))

    def rows_m(width):
        return pl.BlockSpec((TM, width), lambda i, n: (i, 0))

    def depth_piece(k):
        return pl.BlockSpec((STEP, HIDDEN), lambda i, n: (TM // STEP * i + 1 + k, 0))

    pieces = TM // STEP
    (block_out, grad_skip, grad_enc, send, wave_half, r, r_up, r_down, keep, give, msg3, table_mid) = call(
        mask_kernel, "mask", tiles_m,
        [
            whole(*msg_shape), *[depth_piece(k) for k in range(pieces)],
            half_rows(128), half_rows(128), half_rows(HIDDEN), half_rows(128),
            pl.BlockSpec((2, TM * STRIDE), lambda i, n: (0, half() * tiles_m + i)),
            pl.BlockSpec(
                (2, LANES),
                lambda i, n: (0, jnp.minimum((half() * tiles_m + i + 1) * (TM // 16), (2 * tiles_m) * (TM // 16) - 1)),
            ),
            whole(T + 8, 128), whole(L, HIDDEN), whole(NVEC, HIDDEN), whole(1, 256), whole(1, 128),
            anywhere, anywhere, anywhere, anywhere,
        ],
        [
            half_rows(128), half_rows(128), half_rows(HIDDEN), rows_m(768),
            pl.BlockSpec((2, TM * STRIDE), lambda i, n: (0, i)),
            rows_m(HIDDEN), whole(136, HIDDEN), whole(128, HIDDEN), whole(EARLY, 128), whole(EARLY, 128),
            whole(*msg_shape), whole(2, padded, LANES),
        ],
        [
            struct(frames, 128), struct(frames, 128), struct(frames, HIDDEN), struct(own_rows, 768),
            struct(2, own_rows * STRIDE), struct(own_rows, HIDDEN), struct(136, HIDDEN), struct(128, HIDDEN),
            struct(EARLY, 128), struct(EARLY, 128), message, struct(2, padded, LANES),
        ],
        [
            vmem(4, 512, 128), pltpu.SemaphoreType.DMA((4,)), vmem16(1536, 256), vmem16(768, HIDDEN),
            vmem16(512, 1024), vmem16(2, 2, 512, 256), vmem16(2, 768, 256), vmem16(128, 1024), vmem16(2, 256, 128),
            vmem16(2, 256, 128), vmem(TM, HIDDEN), vmem(TM, HIDDEN), vmem(8, 128), vmem(256, 256), vmem(128, HIDDEN),
            vmem(2, 128, HIDDEN), vmem(8, HIDDEN), vmem(8, 128),
            vmem(8, 2 * tiles, 128), vmem(2 * tiles, 128),
        ], 28,
    )(
        lengths, msg2, *[depth] * pieces, mix_in, skip_in, encoded, cot_out, cot_wave, cot_wave, mix_next, basis.T, vec,
        line(b_out), line(slope_skip), *wides,
    )

    both = ("tm", "src")
    later, earlier = [], []
    for i in range(n_tm):
        for s in range(n_src):
            here = i * n_src + s
            there = here + 1 if s % 2 == 0 else (i + 1) * n_src + s - 1
            if s % 2 == 0 or i + 1 < n_tm:
                later.append((here, there))
                earlier.append((there, here))
    hops = [[(i, i ^ (1 << bit)) for i in range(n_tm)] for bit in range(n_tm.bit_length() - 1)]
    early = keep + lax.ppermute(give, "src", swap)
    got_low = lax.ppermute(r_up, both, later)
    got_high = lax.ppermute(r_down, both, earlier)
    msg3 = exchange(msg3)
    early_other = lax.ppermute(early, "tm", hops[0])
    msg3, got_low, got_high, early, early_other, send, wave_half = lax.optimization_barrier(
        (msg3, got_low, got_high, early, early_other, send, wave_half)
    )
    early = early + early_other
    early_other = lax.ppermute(early, "tm", hops[-1])
    got = lax.ppermute(send, "src", swap)
    wave_other = lax.ppermute(wave_half, "src", swap)

    def rows(width):
        return pl.BlockSpec((T, width), lambda i, n: (i, 0))

    def own_tile(width):
        return pl.BlockSpec((T, width), lambda i, n: (half() * tiles + jnp.maximum(i - 1, 0), 0))

    def other_rows(width):
        return pl.BlockSpec((own_rows // 2, width), lambda i, n: ((1 - half()) * 2 + i, 0))

    grad_mix, mix_send, keep, give, edge = call(
        back_kernel, "back", tiles + 1,
        [
            whole(*msg_shape), rows(HIDDEN),
            pl.BlockSpec((STEP, HIDDEN), lambda i, n: (jnp.maximum(2 * i - 1, 0), 0)),
            pl.BlockSpec((STEP, HIDDEN), lambda i, n: (jnp.minimum(2 * i, 2 * tiles - 1), 0)),
            whole(136, HIDDEN), whole(128, HIDDEN),
            pl.BlockSpec((T, HIDDEN), lambda i, n: (jnp.maximum(i, 1), 0)), own_tile(128), own_tile(128),
            whole(NVEC, HIDDEN), whole(2, padded, LANES), whole(2, padded, LANES),
            anywhere, anywhere, anywhere, anywhere,
        ],
        [
            own_tile(128), pl.BlockSpec((T, 128), lambda i, n: (jnp.maximum(i - 1, 0), 0)),
            whole(144, 128), whole(144, 128), whole(8, 128),
        ],
        [
            struct(frames, 128), struct(own_rows, 128), struct(144, 128), struct(144, 128), struct(8, 128),
        ],
        [
            vmem(4, 128, 128), pltpu.SemaphoreType.DMA((4,)), vmem(4, padded, LANES), vmem16(1024, 256),
            vmem(2, T, HIDDEN), vmem(512, 256), vmem(16, HIDDEN),
        ], 13,
    )(
        lengths, msg3, depth, r, r, got_low, got_high, hidden, mix_in, cot_out, vec, table_in, table_mid, *packs,
    )

    grad_mix, mix_send, keep, give, edge, early, early_other = lax.optimization_barrier(
        (grad_mix, mix_send, keep, give, edge, early, early_other)
    )
    late = keep + lax.ppermute(give, "src", swap)
    mix_got = lax.ppermute(mix_send, "src", swap)
    edge_other = lax.ppermute(edge, "src", swap)
    late_other = lax.ppermute(late, "tm", hops[-1])
    early = early + early_other
    early_other = lax.ppermute(early, "tm", hops[1])
    block_out, grad_skip, grad_enc = call(
        pass_kernel, "pass", 2,
        [pl.BlockSpec((own_rows // 2, 768), lambda i, n: (i, 0)), anywhere, anywhere, anywhere],
        [other_rows(128), other_rows(128), other_rows(HIDDEN)],
        [struct(frames, 128), struct(frames, 128), struct(frames, HIDDEN)], [], 4,
        input_output_aliases={2: 0, 3: 1, 4: 2},
    )(lengths, got, block_out, grad_skip, grad_enc)
    late, late_other, block_out, grad_skip, grad_enc = lax.optimization_barrier(
        (late, late_other, block_out, grad_skip, grad_enc)
    )
    late = late + late_other
    late_other = lax.ppermute(late, "tm", hops[0])
    wave_width = own_rows * STRIDE
    grad_mix, wave = call(
        merge_kernel, "merge", 1,
        [
            whole(own_rows, 128), anywhere, whole(2, wave_width), whole(2, wave_width), whole(8, 128), whole(8, 128),
        ],
        [pl.BlockSpec((own_rows, 128), lambda i, n: (1 - half(), 0)), whole(2, 2 * wave_width)],
        [struct(frames, 128), struct(2, 2 * wave_width)], [], 2,
        input_output_aliases={2: 0},
    )(lengths, mix_got, grad_mix, wave_half, wave_other, edge, edge_other)
    late, late_other, grad_mix, wave = lax.optimization_barrier((late, late_other, grad_mix, wave))
    for hop in hops[1:-1]:
        late = late + late_other
        late_other = lax.ppermute(late, "tm", hop)
    for hop in hops[2:-1]:
        early = early + early_other
        early_other = lax.ppermute(early, "tm", hop)

    outs = pl.pallas_call(
        last_kernel,
        in_specs=[pl.BlockSpec(memory_space=pltpu.VMEM)] * 4,
        out_shape=[
            struct(128, 128), struct(1, 128), struct(1, 128), struct(1, 128), struct(1, 128), struct(3, 128),
            struct(1, 128), struct(1, 128), struct(1, 128), struct(1, 128), struct(128, 256), struct(1, 256),
            struct(1, 128), struct(128, 256), struct(1, 256), struct(L, HIDDEN),
        ],
        compiler_params=pltpu.CompilerParams(vmem_limit_bytes=VMEM),
        name="last",
    )(late, late_other, early, early_other)
    outs = [o.reshape(-1) if o.shape[0] == 1 else o for o in outs[:-1]] + [outs[-1].T]
    return (block_out, wave, grad_mix, grad_skip, grad_enc, *outs)


def solution(mesh):
    frames, channels = P("tm", None), P("src")
    in_specs = (
        frames, frames, frames, P(), P(None, "src"), channels, channels, channels, channels, P(None, "src"), channels,
        channels, channels, channels, P("src", None), P(), P(), P(None, "src"), channels, P(), frames, P(None, "tm"),
    )
    out_specs = (
        frames, P(None, "tm"), frames, frames, frames, P(None, "src"), channels, channels, channels, channels,
        P(None, "src"), channels, channels, channels, channels, P("src", None), P(), P(), P(None, "src"), channels,
        P(),
    )
    return jax.shard_map(local, mesh=mesh, in_specs=in_specs, out_specs=out_specs, check_vma=False)
```

time: 192 us -> 163 us (0.85)
  waiting for transfers between devices: 37 us -> 21.9 us
  blocking collectives: 0 us -> 13.9 us
  local copies, waits for them, and re-layouts: 15.5 us -> 5.23 us
  Pallas kernels: 93.2 us -> 84 us
  starting transfers between devices: 37.5 us -> 30.2 us
    ppermute x9 -> x12, waiting for transfers between devices: 31.4 us -> 3.44 us  [the longest x1 2.59 us: local(): late_other = lax.ppermute(late, 'tm', hop)]
    all_to_all x0 -> x1, blocking collectives: none -> 13.9 us  [exchange(): return lax.all_to_all(msg, ('tm', 'src'), 0, 0)]
    pallas_call x5 -> x8, Pallas kernels: 93.2 us -> 84 us  [the longest x1 35 us: local(): call(mask_kernel, 'mask', tiles_m, [whole(*msg_shape), *[depth_piece(k) f...]
    all_to_all x3 -> x2, waiting for transfers between devices: 5.58 us -> 14.8 us  [exchange(): return lax.all_to_all(msg, ('tm', 'src'), 0, 0)]
    all_to_all x3 -> x2, starting transfers between devices: 16.7 us -> 8.95 us  [exchange(): return lax.all_to_all(msg, ('tm', 'src'), 0, 0)]
    unnamed x34 -> x30, local copies, waits for them, and re-layouts: 10.3 us -> 5.23 us
    add x4, other arithmetic: 1.06 us -> 3.54 us  [the longest x2 1.79 us: local(): late = late + late_other]
    concatenate x1 -> x0, local copies, waits for them, and re-layouts: 2.38 us -> none  [local(): jnp.concatenate([w_in, vectors, w_out[:, :128], w_out[:, 128:], w_mask[:,...]
  transfers between devices with their start and end apart: 22 -> 24, of which waited for: 9 -> 7; matrix products, arithmetic and copies ran while one was open for 4% -> 3% of each run, Pallas kernels for 16% -> 28%
where the time goes in v2:
time: 163 us; the launch traced here: 162 us
  Pallas kernels  84 us (52%)
  starting transfers between devices  30.2 us (19%)
  waiting for transfers between devices  21.9 us (13%)
  blocking collectives  13.9 us (9%)
  other arithmetic  5.44 us (3%)
  local copies, waits for them, and re-layouts  5.23 us (3%)
    pallas_call x1, Pallas kernels, local(): call(mask_kernel, 'mask', tiles_m, [whole(*msg_shape), *[depth_piece(k) f...  35 us
    pallas_call x1, Pallas kernels, local(): call(back_kernel, 'back', tiles + 1, [whole(*msg_shape), rows(HIDDEN), pl...  17 us
    all_to_all x2, waiting for transfers between devices, exchange(): return lax.all_to_all(msg, ('tm', 'src'), 0, 0)  14.8 us
    all_to_all x1, blocking collectives, exchange(): return lax.all_to_all(msg, ('tm', 'src'), 0, 0)  13.9 us
    pallas_call x1, Pallas kernels, local(): call(depth_kernel, 'depth', tiles + 2, [whole(*msg_shape), whole(frames,...  13.5 us
    all_to_all x2, starting transfers between devices, exchange(): return lax.all_to_all(msg, ('tm', 'src'), 0, 0)  8.95 us
    pallas_call x1, Pallas kernels, local(): call(first_kernel, 'first', 2, [pl.BlockSpec((frames // 2, 128), lambda i...  5.91 us
    ppermute x1, starting transfers between devices, local(): mix_prev = lax.ppermute(high, 'tm', up)  5.51 us
  transfers between devices with their start and end apart: 24, of which 7 were waited for; matrix products, arithmetic and copies ran while one was open for 3% of the time, Pallas kernels for 28%

profile of v2, /device:TPU:0, one launch (start us, length us, event | category | flops | bytes accessed | tf_op | source)
XLA Modules:
  0.0 161.7 jit_solution(8281582028523329849)
XLA Ops:
  0.7 2.1 %prep.1 = (f32[144,128]{1,0:T(8,128)}, f32[512,128]{1,0:T(8,128)}, f32[264,128]{1,0:T(8,128)}, f32[256,128]{1,0:T(8,128)}) custom-call(f32[4096,128]{1,0:T(8,128)} %mix_ref.5, f32[4096,128]{1,0:T(8,128)} %mix_ref.5, f32[2,32768]{1,0:T(2,128)} %refs_9_.1, f32[128,128]{1,0:T(8,128)} %w_in_ref.3, f32[128,256]{1,0:T(8,128)} %w_out_ref.1, f32[128,256]{1,0:T(8,128)} %w_mask_ref.1, ...), custom_call_target="tpu_custom_call" | custom-call | tf_op jit(solution)/shard_map/prep/pallas_call | solution.py:1071
  2.7 1.3 collective-permute-start.3
  4.0 5.5 %collective-permute-start.2 = (f32[256,128]{1,0:T(8,128)}, f32[256,128]{1,0:T(8,128)S(1)}, u32[]{:S(2)}, u32[]{:S(2)}) collective-permute-start(f32[256,128]{1,0:T(8,128)} %get-tuple-element.97), channel_id=1, source_target_pairs={{0,4},{4,8},{8,12},{12,16},{16,20},{20,24},{24,28},{1,5},{5,9},{9,... | collective-permute-start | bytes 393224 | tf_op jit(solution)/shard_map/ppermute | solution.py:1085
  9.6 2.1 %collective-permute-start = (f32[144,128]{1,0:T(8,128)}, f32[144,128]{1,0:T(8,128)S(1)}, u32[]{:S(2)}, u32[]{:S(2)}) collective-permute-start(f32[144,128]{1,0:T(8,128)} %get-tuple-element.96.own_ref), channel_id=1, source_target_pairs={{0,2},{1,3},{2,0},{3,1},{4,6},{5,7},{6,4},{7,5},{8,10},{9,11},{10,... | collective-permute-start | bytes 221192 | tf_op jit(solution)/shard_map/ppermute | solution.py:1083
  11.7 5.9 %first.1 = f32[32,8,128]{2,1,0:T(8,128)} custom-call(s32[5]{0:T(128)} %len_ref.11, f32[4096,128]{1,0:T(8,128)} %mix_ref.5, f32[128,128]{1,0:T(8,128)} %w_in_ref.3, f32[1,128]{1,0:T(1,128)} %bitcast.26, f32[1,128]{1,0:T(1,128)} %bitcast.28), custom_call_target="tpu_custom_call" | custom-call | bytes 14400000 | tf_op jit(solution)/shard_map/first/pallas_call | solution.py:1087
  18.3 6.2 %all-to-all-start = ((f32[32,8,128]{2,1,0:T(8,128)}), f32[32,8,128]{2,1,0:T(8,128)S(1)}, u32[]{:S(2)}, u32[]{:S(2)}) async-start(f32[32,8,128]{2,1,0:T(8,128)} %first.1), calls=%async_computation | async-start | bytes 262144 | tf_op jit(solution)/shard_map/all_to_all | solution.py:1058
  26.0 6.8 %all-to-all-done.msg_in_ref = f32[32,8,128]{2,1,0:T(8,128)S(1)} async-done(((f32[32,8,128]{2,1,0:T(8,128)}), f32[32,8,128]{2,1,0:T(8,128)S(1)}, u32[]{:S(2)}, u32[]{:S(2)}) %all-to-all-start) | async-done | bytes 131104 | tf_op jit(solution)/shard_map/all_to_all | solution.py:1058
  33.4 13.5 %depth.1 = (f32[2560,512]{1,0:T(8,128)}, f32[2304,512]{1,0:T(8,128)}, f32[32,8,128]{2,1,0:T(8,128)}, f32[16,512]{1,0:T(8,128)}, f32[2,8,128]{2,1,0:T(8,128)}) custom-call(s32[5]{0:T(128)} %len_ref.11, f32[32,8,128]{2,1,0:T(8,128)} %copy-done.2, f32[4096,128]{1,0:T(8,128)} %mix_ref.5, f32[256,128]{1,0:T(8,128)} %copy-done.9, f32[264,128]{1,0:T(8,128)} %copy-done, ...), custom_call_target="tpu_custom_call" | custom-call | bytes 28800000 | tf_op jit(solution)/shard_map/depth/pallas_call | solution.py:1105
  47.0 2.8 %all-to-all-start.1 = ((f32[32,8,128]{2,1,0:T(8,128)}), f32[32,8,128]{2,1,0:T(8,128)S(1)}, u32[]{:S(2)}, u32[]{:S(2)}) async-start(f32[32,8,128]{2,1,0:T(8,128)} %get-tuple-element.104), calls=%async_computation.1 | async-start | bytes 262144 | tf_op jit(solution)/shard_map/all_to_all | solution.py:1058
  49.8 8.0 %all-to-all-done.1.msg_in_ref = f32[32,8,128]{2,1,0:T(8,128)S(1)} async-done(((f32[32,8,128]{2,1,0:T(8,128)}), f32[32,8,128]{2,1,0:T(8,128)S(1)}, u32[]{:S(2)}, u32[]{:S(2)}) %all-to-all-start.1) | async-done | bytes 131104 | tf_op jit(solution)/shard_map/all_to_all | solution.py:1058
  58.5 35.0 %mask.1 = (f32[4096,128]{1,0:T(8,128)}, f32[4096,128]{1,0:T(8,128)}, f32[4096,512]{1,0:T(8,128)}, f32[2048,768]{1,0:T(8,128)}, f32[2,16384]{1,0:T(2,128)}, /*ind...) custom-call(s32[5]{0:T(128)} %len_ref.11, ...), custom_call_target="tpu_custom_call" | custom-call | bytes 100800000 | tf_op jit(solution)/shard_map/mask/pallas_call | solution.py:1137
  93.5 1.8 %collective-permute-done.10 = f32[584,128]{1,0:T(8,128)S(1)} collective-permute-done((f32[584,128]{1,0:T(8,128)}, f32[584,128]{1,0:T(8,128)S(1)}, u32[]{:S(2)}, u32[]{:S(2)}) %collective-permute-start.10) | collective-permute-done | bytes 299040 | tf_op jit(solution)/shard_map/ppermute | solution.py:1183
  96.4 2.0 %collective-permute-start.8 = (f32[136,512]{1,0:T(8,128)}, f32[136,512]{1,0:T(8,128)S(1)}, u32[]{:S(2)}, u32[]{:S(2)}) collective-permute-start(f32[136,512]{1,0:T(8,128)} %get-tuple-element.109), channel_id=1, source_target_pairs={{0,1},{1,4},{2,3},{3,6},{4,5},{5,8},{6,7},{7,10},{8,9},{9,12},{10,... | collective-permute-start | bytes 835592 | tf_op jit(solution)/shard_map/ppermute | solution.py:1184
  98.4 1.3 collective-permute-start.9
  99.7 13.9 %all_to_all.15.msg_in_ref = f32[32,8,128]{2,1,0:T(8,128)} all-to-all(f32[32,8,128]{2,1,0:T(8,128)} %get-tuple-element.108), channel_id=1, replica_groups=mesh['tm'=8,'src'=4] {'tm','src'}, dimensions={0} | all-to-all | bytes 262144 | tf_op jit(solution)/shard_map/all_to_all | solution.py:1058
  115.3 17.0 %back.1 = (f32[4096,128]{1,0:T(8,128)}, f32[2048,128]{1,0:T(8,128)}, f32[144,128]{1,0:T(8,128)}, f32[144,128]{1,0:T(8,128)}, f32[8,128]{1,0:T(8,128)}) custom-call(s32[5]{0:T(128)} %len_ref.11, f32[32,8,128]{2,1,0:T(8,128)} %all_to_all.15.msg_in_ref, f32[2304,512]{1,0:T(8,128)} %get-tuple-element.105.refs_0_.refs_1_.refs_2_.refs_3_.depth_ref, ...), custom_call_target="tpu_custom_call" | custom-call | bytes 46800000 | tf_op jit(solution)/shard_map/back/pallas_call | solution.py:1205
  132.5 1.7 %add.23.c_ref = f32[584,128]{1,0:T(8,128)} add(f32[584,128]{1,0:T(8,128)S(1)} %add.19, f32[584,128]{1,0:T(8,128)} %collective-permute-done.12) | non-fusion elementwise | flops 74752 | bytes 897024 | tf_op jit(solution)/shard_map/add | solution.py:1238
  135.6 1.3 collective-permute-done.13
  137.7 1.8 %collective-permute-start.14 = (f32[144,128]{1,0:T(8,128)S(1)}, f32[144,128]{1,0:T(8,128)S(1)}, u32[]{:S(2)}, u32[]{:S(2)}) collective-permute-start(f32[144,128]{1,0:T(8,128)S(1)} %add.20), channel_id=1, source_target_pairs={{0,16},{4,20},{8,24},{12,28},{16,0},{20,4},{24,8},{28,12},{1,17},{... | collective-permute-start | bytes 221192 | tf_op jit(solution)/shard_map/ppermute | solution.py:1237
  139.6 5.5 %pass.1 = (f32[4096,128]{1,0:T(8,128)}, f32[4096,128]{1,0:T(8,128)}, f32[4096,512]{1,0:T(8,128)}) custom-call(s32[5]{0:T(128)} %len_ref.11, f32[2048,768]{1,0:T(8,128)} %collective-permute-done.15.got_ref, f32[4096,128]{1,0:T(8,128)} %get-tuple-element.132.block_in, ...), custom_call_target="tpu_custom_call", output_to_operand_aliasing={{0}: (2, {}), {1}: (3, {}), {2}: (4, {})} | custom-call | bytes 14400000 | tf_op jit(solution)/shard_map/pass/pallas_call | solution.py:1240
  149.1 3.1 %merge.1 = (f32[4096,128]{1,0:T(8,128)}, f32[2,32768]{1,0:T(2,128)}) custom-call(s32[5]{0:T(128)} %len_ref.11, f32[2048,128]{1,0:T(8,128)} %collective-permute-done.17.got_ref, f32[4096,128]{1,0:T(8,128)} %get-tuple-element.142.mix_in, f32[2,16384]{1,0:T(2,128)} %get-tuple-element.143.mine_ref, ...), custom_call_target="tpu_custom_call", output_to_operand_aliasing={{0}: (2, {})} | custom-call | bytes 7200000 | tf_op jit(solution)/shard_map/merge/pallas_call | solution.py:1253
  153.7 2.7 %collective-permute-start.20 = (f32[144,128]{1,0:T(8,128)S(1)}, f32[144,128]{1,0:T(8,128)S(1)}, u32[]{:S(2)}, u32[]{:S(2)}) collective-permute-start(f32[144,128]{1,0:T(8,128)S(1)} %add.22.a_ref), channel_id=1, source_target_pairs={{0,8},{4,12},{8,0},{12,4},{16,24},{20,28},{24,16},{28,20},{1,9},{5... | collective-permute-start | bytes 221192 | tf_op jit(solution)/shard_map/ppermute | solution.py:1265
  156.4 2.6 %collective-permute-done.20.b_ref = f32[144,128]{1,0:T(8,128)S(1)} collective-permute-done((f32[144,128]{1,0:T(8,128)S(1)}, f32[144,128]{1,0:T(8,128)S(1)}, u32[]{:S(2)}, u32[]{:S(2)}) %collective-permute-start.20) | collective-permute-done | bytes 73760 | tf_op jit(solution)/shard_map/ppermute | solution.py:1265
  159.6 1.9 %last.1 = (f32[128,128]{1,0:T(8,128)}, f32[1,128]{1,0:T(1,128)}, f32[1,128]{1,0:T(1,128)}, f32[1,128]{1,0:T(1,128)}, f32[1,128]{1,0:T(1,128)}, /*index=5*/f32[3,...) custom-call(f32[144,128]{1,0:T(8,128)} %copy-done.6, ...), custom_call_target="tpu_custom_call" | custom-call | tf_op jit(solution)/shard_map/last/pallas_call | solution.py:1270
  (69 shorter events, 15.1 us)
Async XLA Ops:
  2.7 15.0 %collective-permute-start.3 = (f32[264,128]{1,0:T(8,128)}, f32[264,128]{1,0:T(8,128)S(1)}, u32[]{:S(2)}, u32[]{:S(2)}) collective-permute-start(f32[264,128]{1,0:T(8,128)} %get-tuple-element.98), channel_id=1, source_target_pairs={{4,0},{8,4},{12,8},{16,12},{20,16},{24,20},{28,24},{5,1},{9,5},{13... | collective-permute-start | bytes 405512 | tf_op jit(solution)/shard_map/ppermute | solution.py:1086
  4.0 13.7 %collective-permute-start.2 = (f32[256,128]{1,0:T(8,128)}, f32[256,128]{1,0:T(8,128)S(1)}, u32[]{:S(2)}, u32[]{:S(2)}) collective-permute-start(f32[256,128]{1,0:T(8,128)} %get-tuple-element.97), channel_id=1, source_target_pairs={{0,4},{4,8},{8,12},{12,16},{16,20},{20,24},{24,28},{1,5},{5,9},{9,... | collective-permute-start | bytes 393224 | tf_op jit(solution)/shard_map/ppermute | solution.py:1085
  9.5 8.1 %collective-permute-start.1 = (f32[144,128]{1,0:T(8,128)}, f32[144,128]{1,0:T(8,128)S(1)}, u32[]{:S(2)}, u32[]{:S(2)}) collective-permute-start(f32[144,128]{1,0:T(8,128)} %get-tuple-element.96.own_ref), channel_id=1, source_target_pairs={{0,1},{1,0},{2,3},{3,2},{4,5},{5,4},{6,7},{7,6},{8,9},{9,8},{10,11... | collective-permute-start | bytes 221192 | tf_op jit(solution)/shard_map/ppermute | solution.py:1084
  9.6 8.1 %collective-permute-start = (f32[144,128]{1,0:T(8,128)}, f32[144,128]{1,0:T(8,128)S(1)}, u32[]{:S(2)}, u32[]{:S(2)}) collective-permute-start(f32[144,128]{1,0:T(8,128)} %get-tuple-element.96.own_ref), channel_id=1, source_target_pairs={{0,2},{1,3},{2,0},{3,1},{4,6},{5,7},{6,4},{7,5},{8,10},{9,11},{10,... | collective-permute-start | bytes 221192 | tf_op jit(solution)/shard_map/ppermute | solution.py:1083
  11.6 13.5 %collective-permute-start.6 = (f32[512,128]{1,0:T(8,128)}, f32[512,128]{1,0:T(8,128)}, u32[]{:S(2)}, u32[]{:S(2)}) collective-permute-start(f32[512,128]{1,0:T(8,128)} %get-tuple-element.107.refs_15_), channel_id=1, source_target_pairs={{0,2},{1,3},{2,0},{3,1},{4,6},{5,7},{6,4},{7,5},{8,10},{9,11},{10,... | collective-permute-start | bytes 786440 | tf_op jit(solution)/shard_map/ppermute | solution.py:1099
  18.3 14.4 %all-to-all-start = ((f32[32,8,128]{2,1,0:T(8,128)}), f32[32,8,128]{2,1,0:T(8,128)S(1)}, u32[]{:S(2)}, u32[]{:S(2)}) async-start(f32[32,8,128]{2,1,0:T(8,128)} %first.1), calls=%async_computation | async-start | bytes 262144 | tf_op jit(solution)/shard_map/all_to_all | solution.py:1058
  24.5 1.5 collective-permute-start.4
  24.8 24.9 %collective-permute-start.5 = (f32[512,128]{1,0:T(8,128)}, f32[512,128]{1,0:T(8,128)}, u32[]{:S(2)}, u32[]{:S(2)}) collective-permute-start(f32[512,128]{1,0:T(8,128)} %get-tuple-element.107.refs_15_), channel_id=1, source_target_pairs={{0,1},{1,0},{2,3},{3,2},{4,5},{5,4},{6,7},{7,6},{8,9},{9,8},{10,11... | collective-permute-start | bytes 786440 | tf_op jit(solution)/shard_map/ppermute | solution.py:1100
  25.1 24.7 %collective-permute-start.7 = (f32[512,128]{1,0:T(8,128)}, f32[512,128]{1,0:T(8,128)}, u32[]{:S(2)}, u32[]{:S(2)}) collective-permute-start(f32[512,128]{1,0:T(8,128)} %collective-permute-done.6.refs_17_), channel_id=1, source_target_pairs={{0,1},{1,0},{2,3},{3,2},{4,5},{5,4},{6,7},{7,6},{8,9},{9,8},{10,11... | collective-permute-start | bytes 786440 | tf_op jit(solution)/shard_map/ppermute | solution.py:1101
  47.0 10.8 %all-to-all-start.1 = ((f32[32,8,128]{2,1,0:T(8,128)}), f32[32,8,128]{2,1,0:T(8,128)S(1)}, u32[]{:S(2)}, u32[]{:S(2)}) async-start(f32[32,8,128]{2,1,0:T(8,128)} %get-tuple-element.104), calls=%async_computation.1 | async-start | bytes 262144 | tf_op jit(solution)/shard_map/all_to_all | solution.py:1058
  93.4 1.9 %collective-permute-start.10 = (f32[584,128]{1,0:T(8,128)}, f32[584,128]{1,0:T(8,128)S(1)}, u32[]{:S(2)}, u32[]{:S(2)}) collective-permute-start(f32[584,128]{1,0:T(8,128)} %get-tuple-element.112), channel_id=1, source_target_pairs={{0,1},{1,0},{2,3},{3,2},{4,5},{5,4},{6,7},{7,6},{8,9},{9,8},{10,11... | collective-permute-start | bytes 897032 | tf_op jit(solution)/shard_map/ppermute | solution.py:1183
  96.3 17.3 %collective-permute-start.11 = (f32[584,128]{1,0:T(8,128)S(1)}, f32[584,128]{1,0:T(8,128)S(1)}, u32[]{:S(2)}, u32[]{:S(2)}) collective-permute-start(f32[584,128]{1,0:T(8,128)S(1)} %add.18), channel_id=1, source_target_pairs={{0,4},{4,0},{8,12},{12,8},{16,20},{20,16},{24,28},{28,24},{1,5},{5... | collective-permute-start | bytes 897032 | tf_op jit(solution)/shard_map/ppermute | solution.py:1187
  96.4 17.2 %collective-permute-start.8 = (f32[136,512]{1,0:T(8,128)}, f32[136,512]{1,0:T(8,128)S(1)}, u32[]{:S(2)}, u32[]{:S(2)}) collective-permute-start(f32[136,512]{1,0:T(8,128)} %get-tuple-element.109), channel_id=1, source_target_pairs={{0,1},{1,4},{2,3},{3,6},{4,5},{5,8},{6,7},{7,10},{8,9},{9,12},{10,... | collective-permute-start | bytes 835592 | tf_op jit(solution)/shard_map/ppermute | solution.py:1184
  98.4 15.2 %collective-permute-start.9 = (f32[128,512]{1,0:T(8,128)}, f32[128,512]{1,0:T(8,128)S(1)}, u32[]{:S(2)}, u32[]{:S(2)}) collective-permute-start(f32[128,512]{1,0:T(8,128)} %get-tuple-element.110), channel_id=1, source_target_pairs={{1,0},{4,1},{3,2},{6,3},{5,4},{8,5},{7,6},{10,7},{9,8},{12,9},{11,... | collective-permute-start | bytes 786440 | tf_op jit(solution)/shard_map/ppermute | solution.py:1185
  114.4 25.2 %collective-permute-start.15 = (f32[2048,768]{1,0:T(8,128)}, f32[2048,768]{1,0:T(8,128)}, u32[]{:S(2)}, u32[]{:S(2)}) collective-permute-start(f32[2048,768]{1,0:T(8,128)} %get-tuple-element.131), channel_id=1, source_target_pairs={{0,1},{1,0},{2,3},{3,2},{4,5},{5,4},{6,7},{7,6},{8,9},{9,8},{10,11... | collective-permute-start | bytes 18874376 | tf_op jit(solution)/shard_map/ppermute | solution.py:1193
  114.7 17.7 %collective-permute-start.12 = (f32[584,128]{1,0:T(8,128)S(1)}, f32[584,128]{1,0:T(8,128)}, u32[]{:S(2)}, u32[]{:S(2)}) collective-permute-start(f32[584,128]{1,0:T(8,128)S(1)} %add.19), channel_id=1, source_target_pairs={{0,16},{4,20},{8,24},{12,28},{16,0},{20,4},{24,8},{28,12},{1,17},{... | collective-permute-start | bytes 897032 | tf_op jit(solution)/shard_map/ppermute | solution.py:1192
  132.3 16.2 %collective-permute-start.17 = (f32[2048,128]{1,0:T(8,128)}, f32[2048,128]{1,0:T(8,128)}, u32[]{:S(2)}, u32[]{:S(2)}) collective-permute-start(f32[2048,128]{1,0:T(8,128)} %get-tuple-element.141), channel_id=1, source_target_pairs={{0,1},{1,0},{2,3},{3,2},{4,5},{5,4},{6,7},{7,6},{8,9},{9,8},{10,11... | collective-permute-start | bytes 3145736 | tf_op jit(solution)/shard_map/ppermute | solution.py:1235
  134.2 22.2 %collective-permute-start.21 = (f32[584,128]{1,0:T(8,128)}, f32[584,128]{1,0:T(8,128)S(1)}, u32[]{:S(2)}, u32[]{:S(2)}) collective-permute-start(f32[584,128]{1,0:T(8,128)} %add.23.c_ref), channel_id=1, source_target_pairs={{0,8},{4,12},{8,0},{12,4},{16,24},{20,28},{24,16},{28,20},{1,9},{5... | collective-permute-start | bytes 897032 | tf_op jit(solution)/shard_map/ppermute | solution.py:1239
  135.4 1.5 collective-permute-start.13
  137.7 7.3 %collective-permute-start.14 = (f32[144,128]{1,0:T(8,128)S(1)}, f32[144,128]{1,0:T(8,128)S(1)}, u32[]{:S(2)}, u32[]{:S(2)}) collective-permute-start(f32[144,128]{1,0:T(8,128)S(1)} %add.20), channel_id=1, source_target_pairs={{0,16},{4,20},{8,24},{12,28},{16,0},{20,4},{24,8},{28,12},{1,17},{... | collective-permute-start | bytes 221192 | tf_op jit(solution)/shard_map/ppermute | solution.py:1237
  139.6 8.1 %collective-permute-start.18 = (f32[2,16384]{1,0:T(2,128)}, f32[2,16384]{1,0:T(2,128)}, u32[]{:S(2)}, u32[]{:S(2)}) collective-permute-start(f32[2,16384]{1,0:T(2,128)} %get-tuple-element.143.mine_ref), channel_id=1, source_target_pairs={{0,1},{1,0},{2,3},{3,2},{4,5},{5,4},{6,7},{7,6},{8,9},{9,8},{10,11... | collective-permute-start | bytes 393224 | tf_op jit(solution)/shard_map/ppermute | solution.py:1194
  146.6 5.6 %collective-permute-start.16 = (f32[144,128]{1,0:T(8,128)S(1)}, f32[144,128]{1,0:T(8,128)S(1)}, u32[]{:S(2)}, u32[]{:S(2)}) collective-permute-start(f32[144,128]{1,0:T(8,128)S(1)} %add.21), channel_id=1, source_target_pairs={{0,4},{4,0},{8,12},{12,8},{16,20},{20,16},{24,28},{28,24},{1,5},{5... | collective-permute-start | bytes 221192 | tf_op jit(solution)/shard_map/ppermute | solution.py:1251
  147.3 1.2 collective-permute-start.19
  153.7 5.3 %collective-permute-start.20 = (f32[144,128]{1,0:T(8,128)S(1)}, f32[144,128]{1,0:T(8,128)S(1)}, u32[]{:S(2)}, u32[]{:S(2)}) collective-permute-start(f32[144,128]{1,0:T(8,128)S(1)} %add.22.a_ref), channel_id=1, source_target_pairs={{0,8},{4,12},{8,0},{12,4},{16,24},{20,28},{24,16},{28,20},{1,9},{5... | collective-permute-start | bytes 221192 | tf_op jit(solution)/shard_map/ppermute | solution.py:1265
  (15 other events, 66.9 us)

commit v3 on v2

--- a/solution.py
+++ b/solution.py
@@ -23,7 +23,7 @@
 PACK_IN = 128 + NVEC
 PACK = PACK_IN + 512
 EARLY = 584
-VMEM = 63 * 2**20 + 2**19
+VMEM = 64 * 2**20 - 2**15
 LOG2E = 1.4426950408889634
 
 
@@ -396,16 +396,61 @@
         put_statistics(msg_ref, sums[...], squares[...], counts[...], onehot[...])
 
 
+def cotangent_kernel(len_ref, wave_cot_ref, wave_next_ref, edge_next_ref, after_ref, packed_ref):
+    j = pl.program_id(0)
+    last = pl.num_programs(0) - 1
+    me = lax.axis_index("src")
+    half = me & 1
+    side = me >> 1
+    own_rows = (last + 1) * TM
+    start = lax.axis_index("tm") * (2 * own_rows) + half * own_rows + j * TM
+    edge, _ = boundary(item_ends(len_ref), start)
+    offset = iota((TM, LANES), 0) + (start - edge)
+    selects_hi, selects_lo = [], []
+    for c in range(2):
+        row = iota((2 * LANES, LANES), 0)
+        col = iota((2 * LANES, LANES), 1) - 48 * c
+        place = (row & 7) + ((row >> 7) << 3)
+        selects_hi.append(((col == place) | (col == place + 16)).astype(F32).astype(BF16))
+        selects_lo.append((col == place + 32).astype(F32).astype(BF16))
+
+    lane_frame = iota((16, LANES), 1) >> 3
+    frame = iota((16, LANES), 0)
+    here = jnp.where(lane_frame == frame, 1.0, 0.0)
+    coming = jnp.where(lane_frame == ((frame + 1) & 15), 1.0, 0.0)
+    final_row = frame == 15
+    packed = None
+    waves = [wave_cot_ref[0:1, :], wave_cot_ref[1:2, :]]
+    finals = [
+        jnp.where((half == 1) & (j == last), edge_next_ref[T + c : T + c + 1, :], wave_next_ref[c : c + 1, :])
+        for c in range(2)
+    ]
+    for c in range(2):
+        wave = jnp.where(side == 0, waves[c], waves[1 - c])
+        final = jnp.where(side == 0, finals[c], finals[1 - c])
+        for part, select in zip(split(cat([wave, final], 1)), (selects_hi, selects_lo)):
+            part = part.astype(F32)
+            lines = [part[:, column(q)] for q in range(TM // 16 + 1)]
+            pieces = []
+            for q in range(TM // 16):
+                following = jnp.where(final_row, lines[q + 1], lines[q]) * coming
+                pieces.append(cat([lines[q] * here, following], 1).astype(BF16))
+            packed = plus(packed, mm(cat(pieces, 0), select[c]))
+    lane = iota((1, LANES), 1)
+    lane = jnp.where(lane < 48, lane, lane - 48)
+    packed_ref[...] = jnp.where((offset == -1) & ((lane & 15) >= 8), 0.0, packed).astype(BF16)
+
+
 def mask_kernel(
     len_ref, msg_in_ref, *refs,
 ):
     depth_refs = refs[: TM // STEP]
     (
-        mix_ref, skip_ref, enc_ref, cot_ref, wave_cot_ref, wave_next_ref, edge_next_ref, basis_ref, vec_ref,
+        mix_ref, skip_ref, enc_ref, cot_ref, packed_ref, basis_ref, vec_ref,
         b_out_ref, slope_skip_ref, own_ref, core_ref, x_ref, far_ref,
         block_ref, grad_skip_ref, grad_enc_ref, send_ref, wave_ref, r_ref, up_ref, down_ref, keep_ref, give_ref,
         msg_ref, table_ref,
-        gathered, sems, w_out, w_out_t, w_mask, w_mask_t, decode, basis_back, select_hi, select_lo, normed_ref,
+        gathered, sems, w_out, w_out_t, w_mask, w_mask_t, decode, basis_back, normed_ref,
         pull_ref, carry, acc_out, acc_mask, acc_basis, acc_vec,
         acc_small, entries, onehot,
     ) = refs[TM // STEP :]
@@ -447,11 +492,6 @@
             with_lo = (row == col + 16).astype(F32).astype(BF16)
             back = mm(with_hi, b_hi) + mm(with_lo, b_lo)
             basis_back[:, c * HIDDEN : (c + 1) * HIDDEN] = back.astype(BF16)
-            row = iota((2 * LANES, LANES), 0)
-            col = iota((2 * LANES, LANES), 1) - 48 * c
-            place = (row & 7) + ((row >> 7) << 3)
-            select_hi[c] = ((col == place) | (col == place + 16)).astype(F32).astype(BF16)
-            select_lo[c] = (col == place + 32).astype(F32).astype(BF16)
         for copy in copies:
             copy.wait()
         for s in range(4):
@@ -480,6 +520,12 @@
     row_b, row_a = item_rows(ahead, items)
     offset = iota((TM, LANES), 0) + (start - edge)
 
+    lane_frame = iota((16, LANES), 1) >> 3
+    here = jnp.where(lane_frame == iota((16, LANES), 0), 1.0, 0.0)
+    packed = packed_ref[...]
+
+    chunks = [[slice(c * HIDDEN + n * 256, c * HIDDEN + (n + 1) * 256) for c in range(2)] for n in range(2)]
+    all_grads = [[None, None], [None, None]]
     after = offset >= 0
     inv_b, inv_a = table_ref[1, pl.ds(row_b, 1), :], table_ref[1, pl.ds(row_a, 1), :]
     shift_b, shift_a = -inv_b * table_ref[0, pl.ds(row_b, 1), :], -inv_a * table_ref[0, pl.ds(row_a, 1), :]
@@ -504,6 +550,7 @@
             los.append(lo)
         norms[c >> 1][0].append(cat(his, 0))
         norms[c >> 1][1].append(cat(los, 0))
+        all_grads[c >> 1][c & 1] = mm(packed, basis_back[:, chunks[c >> 1][c & 1]])
     branch = [
         mm(cat(his + los + his, 1), w_out[768 * k : 768 * (k + 1), :]) for k, (his, los) in enumerate(norms)
     ]
@@ -527,46 +574,38 @@
     a_hi, a_lo = cat([a for a, _ in actives], 0), cat([a for _, a in actives], 0)
     query = cat([a_hi, a_lo, a_hi, ones_block(TM)], 1)
 
-    lane_frame = iota((16, LANES), 1) >> 3
-    frame = iota((16, LANES), 0)
-    here = jnp.where(lane_frame == frame, 1.0, 0.0)
-    coming = jnp.where(lane_frame == ((frame + 1) & 15), 1.0, 0.0)
-    final_row = frame == 15
-    packed = None
-    waves = [wave_cot_ref[0:1, :], wave_cot_ref[1:2, :]]
-    finals = [
-        jnp.where((half == 1) & (j == last), edge_next_ref[T + c : T + c + 1, :], wave_next_ref[c : c + 1, :])
-        for c in range(2)
-    ]
-    for c in range(2):
-        wave = jnp.where(side == 0, waves[c], waves[1 - c])
-        final = jnp.where(side == 0, finals[c], finals[1 - c])
-        for part, select in zip(split(cat([wave, final], 1)), (select_hi, select_lo)):
-            part = part.astype(F32)
-            lines = [part[:, column(q)] for q in range(TM // 16 + 1)]
-            pieces = []
-            for q in range(TM // 16):
-                following = jnp.where(final_row, lines[q + 1], lines[q]) * coming
-                pieces.append(cat([lines[q] * here, following], 1).astype(BF16))
-            packed = plus(packed, mm(cat(pieces, 0), select[c]))
-    lane = iota((1, LANES), 1)
-    lane = jnp.where(lane < 48, lane, lane - 48)
-    packed = jnp.where((offset == -1) & ((lane & 15) >= 8), 0.0, packed).astype(BF16)
-
     decoded = [None, None]
     back = [None, None]
     masked, grads_hi, grads_lo = [[], []], [], []
-    chunks = [[slice(c * HIDDEN + n * 256, c * HIDDEN + (n + 1) * 256) for c in range(2)] for n in range(2)]
-    all_grads = [[mm(packed, basis_back[:, chunk]) for chunk in pair] for pair in chunks]
-    all_logits = [[mm(query, w_mask[:, chunk]) for chunk in pair] for pair in chunks]
+    all_logits = [[mm(query, w_mask[:, chunk]) for chunk in chunks[0]], [None, None]]
+
+    def logits_of(c):
+        all_logits[1][c] = mm(query, w_mask[:, chunks[1][c]])
+
+    def decode_of(n, c):
+        hi, lo = all_blocks[n][c]
+        decoded[c] = plus(decoded[c], mm(cat(hi + lo + hi, 1), decode[n]))
+
+    def back_of(n, c):
+        hi, lo = all_blocks[n][2 + c]
+        back[c] = plus(back[c], mm(cat(hi + lo, 1), w_mask_t[c, n]))
+
+    all_blocks = [[[[], []] for _ in range(4)] for _ in range(2)]
     for n in range(2):
+        if n == 0:
+            waiting = [functools.partial(logits_of, c) for c in range(2)]
+        else:
+            waiting = [functools.partial(f, 0, c) for f in (back_of, decode_of) for c in range(2)]
+        every = 2 * (TM // ROWS) // len(waiting)
         logits, grads = all_logits[n], all_grads[n]
-        blocks = [[[], []] for _ in range(4)]
+        blocks = all_blocks[n]
         for b in range(2):
             col = column(2 * n + b)
             bias_sum = None
             pieces = [[[], []] for _ in range(4)]
-            for i in range(0, TM, ROWS):
+            for k, i in enumerate(range(0, TM, ROWS)):
+                if (b * (TM // ROWS) + k) % every == 0 and waiting:
+                    waiting.pop(0)()
                 rows = slice(i, i + ROWS)
                 enc = enc_ref[rows, col]
                 grad_enc = None
@@ -575,28 +614,27 @@
                     grad = grads[c][rows, column(b)]
                     grad_enc = plus(grad_enc, grad * mask)
                     value = mask * enc
-                    for k, part in enumerate(split(value)):
-                        pieces[c][k].append(part)
+                    for h, part in enumerate(split(value)):
+                        pieces[c][h].append(part)
                     grad_logits = grad * value * (1.0 - mask)
                     if c == 0:
                         bias_sum = plus(bias_sum, fold(grad_logits))
-                    for k, part in enumerate(split(grad_logits)):
-                        pieces[2 + c][k].append(part)
+                    for h, part in enumerate(split(grad_logits)):
+                        pieces[2 + c][h].append(part)
                 grad_enc_ref[rows, col] = grad_enc
                 send_ref[rows, 256 + (2 * n + b) * 128 : 256 + (2 * n + b + 1) * 128] = grad_enc
             acc_vec[2:3, (2 * n + b) * 128 : (2 * n + b + 1) * 128] += colsum(bias_sum)
             for block, piece in zip(blocks, pieces):
-                for k in range(2):
-                    block[k].append(cat(piece[k], 0))
+                for h in range(2):
+                    block[h].append(cat(piece[h], 0))
         for c in range(2):
-            hi, lo = blocks[c]
-            masked[c].append(cat(hi + lo, 1))
-            decoded[c] = plus(decoded[c], mm(cat(hi + lo + hi, 1), decode[n]))
-            hi, lo = blocks[2 + c]
-            back[c] = plus(back[c], mm(cat(hi + lo, 1), w_mask_t[c, n]))
-            if c == 0:
-                grads_hi = grads_hi + hi
-                grads_lo = grads_lo + lo
+            masked[c].append(cat(blocks[c][0] + blocks[c][1], 1))
+        grads_hi = grads_hi + blocks[2][0]
+        grads_lo = grads_lo + blocks[2][1]
+    for c in range(2):
+        back_of(1, c)
+    for c in range(2):
+        decode_of(1, c)
     back = back[0] + back[1]
     own_grads = cat(grads_hi + grads_lo, 1)
 
@@ -769,8 +807,8 @@
 
 def back_kernel(
     len_ref, msg_in_ref, depth_ref, r_a_ref, r_b_ref, low_ref, high_ref, hidden_ref, mix_ref, cot_ref,
-    vec_ref, table_in_ref, table_mid_ref, own_ref, core_ref, x_ref, far_ref,
-    grad_mix_ref, send_ref, keep_ref, give_ref, edge_ref,
+    vec_ref, table_in_ref, table_mid_ref, own_ref, core_ref, x_ref, far_ref, got_ref, block_in, skip_in, enc_in,
+    grad_mix_ref, send_ref, keep_ref, give_ref, edge_ref, block_ref, skip_ref, enc_ref,
     gathered, sems, table, weights, ring, acc_w, acc_vec,
 ):
     j = pl.program_id(0)
@@ -819,6 +857,10 @@
                 place = place + (s >> 1) * 512 + (s & 1) * 128
                 weights[place : place + 128, 0:128] = hi
                 weights[place : place + 128, 128:256] = lo
+
+    block_ref[...] = got_ref[:, 0:128]
+    skip_ref[...] = got_ref[:, 128:256]
+    enc_ref[...] = got_ref[:, 256:768]
 
     base = lax.axis_index("tm") * (2 * own_rows) + half * own_rows
     new, old = j & 1, 1 - (j & 1)
@@ -948,12 +990,6 @@
             ref[128:144, :] = acc_vec[:, own]
 
 
-def pass_kernel(len_ref, got_ref, block_in, skip_in, enc_in, block_ref, skip_ref, enc_ref):
-    block_ref[...] = got_ref[:, 0:128]
-    skip_ref[...] = got_ref[:, 128:256]
-    enc_ref[...] = got_ref[:, 256:768]
-
-
 def merge_kernel(len_ref, got_ref, mix_in, mine_ref, other_ref, edge_ref, edge_other_ref, mix_ref, wave_ref):
     me = lax.axis_index("src")
     half = me & 1
@@ -974,18 +1010,27 @@
         wave_ref[:, pl.ds(place, LANES)] = first
 
 
-def last_kernel(
-    a_ref, b_ref, c_ref, d_ref, w_in, b_in, slope_in, gain_in, beta_in, w_depth, b_depth, slope_mid,
+def total_of(refs):
+    values = [ref[...] for ref in refs]
+    while len(values) > 1:
+        values = [a + b for a, b in zip(values[0::2], values[1::2])]
+    return values[0]
+
+
+def last_kernel(count, early_ref, early_other_ref, *refs):
+    lates = refs[:count]
+    (
+        w_in, b_in, slope_in, gain_in, beta_in, w_depth, b_depth, slope_mid,
     gain_mid, beta_mid, w_out, b_out, slope_skip, w_mask, b_mask, basis,
-):
-    late = a_ref[...] + b_ref[...]
+    ) = refs[count:]
+    late = total_of(lates)
     w_in[...] = late[0:128]
     for ref, row in (
         (b_in, 128), (slope_in, 129), (gain_in, 130), (beta_in, 131), (b_depth, 135), (slope_mid, 136),
     ):
         ref[...] = late[row : row + 1]
     w_depth[...] = late[132:135]
-    early = c_ref[...] + d_ref[...]
+    early = early_ref[...] + early_other_ref[...]
     w_out[:, 0:128] = early[0:128]
     w_out[:, 128:256] = early[128:256]
     w_mask[:, 0:128] = early[256:384]
@@ -1133,18 +1178,25 @@
     def depth_piece(k):
         return pl.BlockSpec((STEP, HIDDEN), lambda i, n: (TM // STEP * i + 1 + k, 0))
 
+    packed = call(
+        cotangent_kernel, "cotangent", tiles_m,
+        [
+            pl.BlockSpec((2, TM * STRIDE), lambda i, n: (0, half() * tiles_m + i)),
+            pl.BlockSpec(
+                (2, LANES),
+                lambda i, n: (0, jnp.minimum((half() * tiles_m + i + 1) * (TM // 16), (2 * tiles_m) * (TM // 16) - 1)),
+            ),
+            whole(T + 8, 128), anywhere,
+        ],
+        rows_m(128), jax.ShapeDtypeStruct((own_rows, 128), BF16), [], 6,
+    )(lengths, cot_wave, cot_wave, mix_next, vec)
     pieces = TM // STEP
     (block_out, grad_skip, grad_enc, send, wave_half, r, r_up, r_down, keep, give, msg3, table_mid) = call(
         mask_kernel, "mask", tiles_m,
         [
             whole(*msg_shape), *[depth_piece(k) for k in range(pieces)],
             half_rows(128), half_rows(128), half_rows(HIDDEN), half_rows(128),
-            pl.BlockSpec((2, TM * STRIDE), lambda i, n: (0, half() * tiles_m + i)),
-            pl.BlockSpec(
-                (2, LANES),
-                lambda i, n: (0, jnp.minimum((half() * tiles_m + i + 1) * (TM // 16), (2 * tiles_m) * (TM // 16) - 1)),
-            ),
-            whole(T + 8, 128), whole(L, HIDDEN), whole(NVEC, HIDDEN), whole(1, 256), whole(1, 128),
+            rows_m(128), whole(L, HIDDEN), whole(NVEC, HIDDEN), whole(1, 256), whole(1, 128),
             anywhere, anywhere, anywhere, anywhere,
         ],
         [
@@ -1160,13 +1212,12 @@
         ],
         [
             vmem(4, 512, 128), pltpu.SemaphoreType.DMA((4,)), vmem16(1536, 256), vmem16(768, HIDDEN),
-            vmem16(512, 1024), vmem16(2, 2, 512, 256), vmem16(2, 768, 256), vmem16(128, 1024), vmem16(2, 256, 128),
-            vmem16(2, 256, 128), vmem(TM, HIDDEN), vmem(TM, HIDDEN), vmem(8, 128), vmem(256, 256), vmem(128, HIDDEN),
+            vmem16(512, 1024), vmem16(2, 2, 512, 256), vmem16(2, 768, 256), vmem16(128, 1024), vmem(TM, HIDDEN), vmem(TM, HIDDEN), vmem(8, 128), vmem(256, 256), vmem(128, HIDDEN),
             vmem(2, 128, HIDDEN), vmem(8, HIDDEN), vmem(8, 128),
             vmem(8, 2 * tiles, 128), vmem(2 * tiles, 128),
         ], 28,
     )(
-        lengths, msg2, *[depth] * pieces, mix_in, skip_in, encoded, cot_out, cot_wave, cot_wave, mix_next, basis.T, vec,
+        lengths, msg2, *[depth] * pieces, mix_in, skip_in, encoded, cot_out, packed, basis.T, vec,
         line(b_out), line(slope_skip), *wides,
     )
 
@@ -1184,14 +1235,15 @@
     got_low = lax.ppermute(r_up, both, later)
     got_high = lax.ppermute(r_down, both, earlier)
     msg3 = exchange(msg3)
+    early, send, wave_half = lax.optimization_barrier((early, send, wave_half))
     early_other = lax.ppermute(early, "tm", hops[0])
-    msg3, got_low, got_high, early, early_other, send, wave_half = lax.optimization_barrier(
-        (msg3, got_low, got_high, early, early_other, send, wave_half)
+    got = lax.ppermute(send, "src", swap)
+    wave_other = lax.ppermute(wave_half, "src", swap)
+    msg3, got_low, got_high, early, early_other, got, wave_other = lax.optimization_barrier(
+        (msg3, got_low, got_high, early, early_other, got, wave_other)
     )
     early = early + early_other
     early_other = lax.ppermute(early, "tm", hops[-1])
-    got = lax.ppermute(send, "src", swap)
-    wave_other = lax.ppermute(wave_half, "src", swap)
 
     def rows(width):
         return pl.BlockSpec((T, width), lambda i, n: (i, 0))
@@ -1200,9 +1252,9 @@
         return pl.BlockSpec((T, width), lambda i, n: (half() * tiles + jnp.maximum(i - 1, 0), 0))
 
     def other_rows(width):
-        return pl.BlockSpec((own_rows // 2, width), lambda i, n: ((1 - half()) * 2 + i, 0))
-
-    grad_mix, mix_send, keep, give, edge = call(
+        return pl.BlockSpec((T, width), lambda i, n: ((1 - half()) * tiles + jnp.minimum(i, tiles - 1), 0))
+
+    grad_mix, mix_send, keep, give, edge, block_out, grad_skip, grad_enc = call(
         back_kernel, "back", tiles + 1,
         [
             whole(*msg_shape), rows(HIDDEN),
@@ -1212,72 +1264,73 @@
             pl.BlockSpec((T, HIDDEN), lambda i, n: (jnp.maximum(i, 1), 0)), own_tile(128), own_tile(128),
             whole(NVEC, HIDDEN), whole(2, padded, LANES), whole(2, padded, LANES),
             anywhere, anywhere, anywhere, anywhere,
+            pl.BlockSpec((T, 768), lambda i, n: (jnp.minimum(i, tiles - 1), 0)), anywhere, anywhere, anywhere,
         ],
         [
             own_tile(128), pl.BlockSpec((T, 128), lambda i, n: (jnp.maximum(i - 1, 0), 0)),
-            whole(144, 128), whole(144, 128), whole(8, 128),
+            whole(144, 128), whole(144, 128), whole(8, 128), other_rows(128), other_rows(128), other_rows(HIDDEN),
         ],
         [
             struct(frames, 128), struct(own_rows, 128), struct(144, 128), struct(144, 128), struct(8, 128),
+            struct(frames, 128), struct(frames, 128), struct(frames, HIDDEN),
         ],
         [
             vmem(4, 128, 128), pltpu.SemaphoreType.DMA((4,)), vmem(4, padded, LANES), vmem16(1024, 256),
             vmem(2, T, HIDDEN), vmem(512, 256), vmem(16, HIDDEN),
         ], 13,
+        input_output_aliases={18: 5, 19: 6, 20: 7},
     )(
-        lengths, msg3, depth, r, r, got_low, got_high, hidden, mix_in, cot_out, vec, table_in, table_mid, *packs,
+        lengths, msg3, depth, r, r, got_low, got_high, hidden, mix_in, cot_out, vec, table_in, table_mid, *packs, got,
+        block_out, grad_skip, grad_enc,
     )
 
-    grad_mix, mix_send, keep, give, edge, early, early_other = lax.optimization_barrier(
-        (grad_mix, mix_send, keep, give, edge, early, early_other)
+    grad_mix, mix_send, keep, give, edge, early_other = lax.optimization_barrier(
+        (grad_mix, mix_send, keep, give, edge, early_other)
     )
     late = keep + lax.ppermute(give, "src", swap)
     mix_got = lax.ppermute(mix_send, "src", swap)
     edge_other = lax.ppermute(edge, "src", swap)
-    late_other = lax.ppermute(late, "tm", hops[-1])
+    late, early, early_other = lax.optimization_barrier((late, early, early_other))
+    late_other = lax.ppermute(late, "tm", hops[0])
     early = early + early_other
-    early_other = lax.ppermute(early, "tm", hops[1])
-    block_out, grad_skip, grad_enc = call(
-        pass_kernel, "pass", 2,
-        [pl.BlockSpec((own_rows // 2, 768), lambda i, n: (i, 0)), anywhere, anywhere, anywhere],
-        [other_rows(128), other_rows(128), other_rows(HIDDEN)],
-        [struct(frames, 128), struct(frames, 128), struct(frames, HIDDEN)], [], 4,
-        input_output_aliases={2: 0, 3: 1, 4: 2},
-    )(lengths, got, block_out, grad_skip, grad_enc)
-    late, late_other, block_out, grad_skip, grad_enc = lax.optimization_barrier(
-        (late, late_other, block_out, grad_skip, grad_enc)
+    for hop in hops[1:-1]:
+        early_other = lax.ppermute(early, "tm", hop)
+        if hop is not hops[-2]:
+            early = early + early_other
+    late, late_other, early, mix_got, edge_other = lax.optimization_barrier(
+        (late, late_other, early, mix_got, edge_other)
     )
     late = late + late_other
-    late_other = lax.ppermute(late, "tm", hops[0])
+    lates = [late]
+    for k in range(1, n_tm // 2):
+        lates.append(lax.ppermute(late, "tm", [(i, i ^ (2 * k)) for i in range(n_tm)]))
     wave_width = own_rows * STRIDE
+    late, mix_got, edge_other = lax.optimization_barrier((late, mix_got, edge_other))
     grad_mix, wave = call(
         merge_kernel, "merge", 1,
         [
             whole(own_rows, 128), anywhere, whole(2, wave_width), whole(2, wave_width), whole(8, 128), whole(8, 128),
         ],
         [pl.BlockSpec((own_rows, 128), lambda i, n: (1 - half(), 0)), whole(2, 2 * wave_width)],
-        [struct(frames, 128), struct(2, 2 * wave_width)], [], 2,
+        [struct(frames, 128), struct(2, 2 * wave_width)], [], 3,
         input_output_aliases={2: 0},
     )(lengths, mix_got, grad_mix, wave_half, wave_other, edge, edge_other)
-    late, late_other, grad_mix, wave = lax.optimization_barrier((late, late_other, grad_mix, wave))
-    for hop in hops[1:-1]:
-        late = late + late_other
-        late_other = lax.ppermute(late, "tm", hop)
-    for hop in hops[2:-1]:
-        early = early + early_other
-        early_other = lax.ppermute(early, "tm", hop)
-
+    *lates, grad_mix, wave = lax.optimization_barrier((*lates, grad_mix, wave))
+
+    parts = (early, early_other, *lates)
+    shapes = (
+        (128, 128), (1, 128), (1, 128), (1, 128), (1, 128), (3, 128), (1, 128), (1, 128), (1, 128), (1, 128), (128, 256),
+        (1, 256), (1, 128), (128, 256), (1, 256), (L, HIDDEN),
+    )
     outs = pl.pallas_call(
-        last_kernel,
-        in_specs=[pl.BlockSpec(memory_space=pltpu.VMEM)] * 4,
-        out_shape=[
-            struct(128, 128), struct(1, 128), struct(1, 128), struct(1, 128), struct(1, 128), struct(3, 128),
-            struct(1, 128), struct(1, 128), struct(1, 128), struct(1, 128), struct(128, 256), struct(1, 256),
-            struct(1, 128), struct(128, 256), struct(1, 256), struct(L, HIDDEN),
-        ],
+        functools.partial(last_kernel, len(lates)),
+        grid=(1,),
+        in_specs=[fixed(*part.shape) for part in parts],
+        out_specs=[fixed(*shape) for shape in shapes],
+        out_shape=[struct(*shape) for shape in shapes],
         compiler_params=pltpu.CompilerParams(vmem_limit_bytes=VMEM),
         name="last",
-    )(late, late_other, early, early_other)
+    )(*parts)
     outs = [o.reshape(-1) if o.shape[0] == 1 else o for o in outs[:-1]] + [outs[-1].T]
     return (block_out, wave, grad_mix, grad_skip, grad_enc, *outs)
 

time: 163 us -> 155 us (0.951)
  blocking collectives: 13.9 us -> 0 us
  waiting for transfers between devices: 21.9 us -> 28.7 us
  starting transfers between devices: 30.2 us -> 36.9 us
  local copies, waits for them, and re-layouts: 5.23 us -> 0.02 us
  Pallas kernels: 84 us -> 82 us
    all_to_all x1 -> x0, blocking collectives: 13.9 us -> none  [exchange(): return lax.all_to_all(msg, ('tm', 'src'), 0, 0)]
    all_to_all x2 -> x3, starting transfers between devices: 8.95 us -> 14.9 us  [exchange(): return lax.all_to_all(msg, ('tm', 'src'), 0, 0)]
    unnamed x30 -> x10, local copies, waits for them, and re-layouts: 5.23 us -> 0.02 us
    pallas_call x1, Pallas kernels: 35 us -> 31.6 us  [local(): call(mask_kernel, 'mask', tiles_m, [whole(*msg_shape), *[depth_piece(k) f...]
    all_to_all x2 -> x3, waiting for transfers between devices: 14.8 us -> 17.8 us  [exchange(): return lax.all_to_all(msg, ('tm', 'src'), 0, 0)]
    ppermute x1, waiting for transfers between devices: 0.01 us -> 2.35 us  [local(): late_other = lax.ppermute(late, 'tm', hops[0])]
    pallas_call x1, Pallas kernels: 17 us -> 19.2 us  [local(): call(back_kernel, 'back', tiles + 1, [whole(*msg_shape), rows(HIDDEN), pl...]
    ppermute x3 -> x4, starting transfers between devices: 5.67 us -> 5.47 us  [the longest x3 4.39 us: local(): lax.ppermute(late, 'tm', [(i, i ^ 2 * k) for i in range(n_tm)])]
  transfers between devices with their start and end apart: 24 -> 26, of which waited for: 7 -> 9; matrix products, arithmetic and copies ran while one was open for 3% -> 2% of each run, Pallas kernels for 28% -> 30%
where the time goes in v3:
time: 155 us; the launch traced here: 154 us
  Pallas kernels  82 us (53%)
  starting transfers between devices  36.9 us (24%)
  waiting for transfers between devices  28.7 us (19%)
  other arithmetic  5.31 us (3%)
    pallas_call x1, Pallas kernels, local(): call(mask_kernel, 'mask', tiles_m, [whole(*msg_shape), *[depth_piece(k) f...  31.6 us
    pallas_call x1, Pallas kernels, local(): call(back_kernel, 'back', tiles + 1, [whole(*msg_shape), rows(HIDDEN), pl...  19.2 us
    all_to_all x3, waiting for transfers between devices, exchange(): return lax.all_to_all(msg, ('tm', 'src'), 0, 0)  17.8 us
    all_to_all x3, starting transfers between devices, exchange(): return lax.all_to_all(msg, ('tm', 'src'), 0, 0)  14.9 us
    pallas_call x1, Pallas kernels, local(): call(depth_kernel, 'depth', tiles + 2, [whole(*msg_shape), whole(frames,...  13.6 us
    ppermute x1, starting transfers between devices, local(): mix_prev = lax.ppermute(high, 'tm', up)  6.17 us
    pallas_call x1, Pallas kernels, local(): call(first_kernel, 'first', 2, [pl.BlockSpec((frames // 2, 128), lambda i...  5.9 us
    pallas_call x1, Pallas kernels, local(): call(cotangent_kernel, 'cotangent', tiles_m, [pl.BlockSpec((2, TM * STRID...  4.66 us
  transfers between devices with their start and end apart: 26, of which 9 were waited for; matrix products, arithmetic and copies ran while one was open for 2% of the time, Pallas kernels for 30%

profile of v3, /device:TPU:0, one launch (start us, length us, event | category | flops | bytes accessed | tf_op | source)
XLA Modules:
  0.0 154.0 jit_solution(17557536952611981437)
XLA Ops:
  0.7 2.1 %prep.1 = (f32[144,128]{1,0:T(8,128)}, f32[512,128]{1,0:T(8,128)}, f32[264,128]{1,0:T(8,128)}, f32[256,128]{1,0:T(8,128)}) custom-call(f32[4096,128]{1,0:T(8,128)} %mix_ref.5, f32[4096,128]{1,0:T(8,128)} %mix_ref.5, f32[2,32768]{1,0:T(2,128)} %wave_next_ref.1, f32[128,128]{1,0:T(8,128)} %w_in_ref.3, f32[128,256]{1,0:T(8,128)} %w_out_ref.1, ...), custom_call_target="tpu_custom_call" | custom-call | tf_op jit(solution)/shard_map/prep/pallas_call | solution.py:1116
  4.0 6.2 %collective-permute-start.2 = (f32[256,128]{1,0:T(8,128)}, f32[256,128]{1,0:T(8,128)}, u32[]{:S(2)}, u32[]{:S(2)}) collective-permute-start(f32[256,128]{1,0:T(8,128)} %get-tuple-element.106), channel_id=1, source_target_pairs={{0,4},{4,8},{8,12},{12,16},{16,20},{20,24},{24,28},{1,5},{5,9},{9,... | collective-permute-start | bytes 393224 | tf_op jit(solution)/shard_map/ppermute | solution.py:1130
  10.2 2.0 %collective-permute-start = (f32[144,128]{1,0:T(8,128)}, f32[144,128]{1,0:T(8,128)}, u32[]{:S(2)}, u32[]{:S(2)}) collective-permute-start(f32[144,128]{1,0:T(8,128)} %get-tuple-element.105.own_ref), channel_id=1, source_target_pairs={{0,2},{1,3},{2,0},{3,1},{4,6},{5,7},{6,4},{7,5},{8,10},{9,11},{10,... | collective-permute-start | bytes 221192 | tf_op jit(solution)/shard_map/ppermute | solution.py:1128
  12.2 5.9 %first.1 = f32[32,8,128]{2,1,0:T(8,128)} custom-call(s32[5]{0:T(128)} %len_ref.11, f32[4096,128]{1,0:T(8,128)} %mix_ref.5, f32[128,128]{1,0:T(8,128)} %w_in_ref.3, f32[1,128]{1,0:T(1,128)} %bitcast.26, f32[1,128]{1,0:T(1,128)} %bitcast.28), custom_call_target="tpu_custom_call" | custom-call | bytes 14400000 | tf_op jit(solution)/shard_map/first/pallas_call | solution.py:1132
  18.1 5.8 %all-to-all-start = ((f32[32,8,128]{2,1,0:T(8,128)}), f32[32,8,128]{2,1,0:T(8,128)}, u32[]{:S(2)}, u32[]{:S(2)}) async-start(f32[32,8,128]{2,1,0:T(8,128)} %first.1), calls=%async_computation | async-start | bytes 262144 | tf_op jit(solution)/shard_map/all_to_all | solution.py:1103
  25.7 6.5 %all-to-all-done.msg_in_ref = f32[32,8,128]{2,1,0:T(8,128)} async-done(((f32[32,8,128]{2,1,0:T(8,128)}), f32[32,8,128]{2,1,0:T(8,128)}, u32[]{:S(2)}, u32[]{:S(2)}) %all-to-all-start) | async-done | bytes 131104 | tf_op jit(solution)/shard_map/all_to_all | solution.py:1103
  32.2 13.6 %depth.1 = (f32[2560,512]{1,0:T(8,128)}, f32[2304,512]{1,0:T(8,128)}, f32[32,8,128]{2,1,0:T(8,128)}, f32[16,512]{1,0:T(8,128)}, f32[2,8,128]{2,1,0:T(8,128)}) custom-call(s32[5]{0:T(128)} %len_ref.11, f32[32,8,128]{2,1,0:T(8,128)} %all-to-all-done.msg_in_ref, f32[4096,128]{1,0:T(8,128)} %mix_ref.5, f32[256,128]{1,0:T(8,128)} %collective-permute-done.2.prev_ref, ...), custom_call_target="tpu_custom_call" | custom-call | bytes 28800000 | tf_op jit(solution)/shard_map/depth/pallas_call | solution.py:1150
  45.8 3.5 %all-to-all-start.1 = ((f32[32,8,128]{2,1,0:T(8,128)}), f32[32,8,128]{2,1,0:T(8,128)}, u32[]{:S(2)}, u32[]{:S(2)}) async-start(f32[32,8,128]{2,1,0:T(8,128)} %get-tuple-element.113), calls=%async_computation.1 | async-start | bytes 262144 | tf_op jit(solution)/shard_map/all_to_all | solution.py:1103
  49.3 4.7 %cotangent.1.refs_8_ = bf16[2048,128]{1,0:T(8,128)(2,1)} custom-call(s32[5]{0:T(128)} %len_ref.11, f32[2,32768]{1,0:T(2,128)} %wave_next_ref.1, f32[2,32768]{1,0:T(2,128)} %wave_next_ref.1, f32[264,128]{1,0:T(8,128)} %collective-permute-done.3.next_ref.edge_next_ref, f32[16,512]{1,0:T(8,128)} %get-tuple-element.115.after_ref.refs_10_.vec_ref), custom_call_target="tpu_custom_call" | custom-call | bytes 21600000 | tf_op jit(solution)/shard_map/cotangent/pallas_call | solution.py:1181
  54.0 3.4 %all-to-all-done.1.msg_in_ref = f32[32,8,128]{2,1,0:T(8,128)} async-done(((f32[32,8,128]{2,1,0:T(8,128)}), f32[32,8,128]{2,1,0:T(8,128)}, u32[]{:S(2)}, u32[]{:S(2)}) %all-to-all-start.1) | async-done | bytes 131104 | tf_op jit(solution)/shard_map/all_to_all | solution.py:1103
  57.3 31.6 %mask.1 = (f32[4096,128]{1,0:T(8,128)}, f32[4096,128]{1,0:T(8,128)}, f32[4096,512]{1,0:T(8,128)}, f32[2048,768]{1,0:T(8,128)}, f32[2,16384]{1,0:T(2,128)}, /*ind...) custom-call(s32[5]{0:T(128)} %len_ref.11, ...), custom_call_target="tpu_custom_call" | custom-call | bytes 100800000 | tf_op jit(solution)/shard_map/mask/pallas_call | solution.py:1194
  89.0 1.8 %collective-permute-done.10 = f32[584,128]{1,0:T(8,128)S(1)} collective-permute-done((f32[584,128]{1,0:T(8,128)}, f32[584,128]{1,0:T(8,128)S(1)}, u32[]{:S(2)}, u32[]{:S(2)}) %collective-permute-start.10) | collective-permute-done | bytes 299040 | tf_op jit(solution)/shard_map/ppermute | solution.py:1234
  92.9 1.8 %collective-permute-start.8 = (f32[136,512]{1,0:T(8,128)}, f32[136,512]{1,0:T(8,128)S(1)}, u32[]{:S(2)}, u32[]{:S(2)}) collective-permute-start(f32[136,512]{1,0:T(8,128)} %get-tuple-element.118), channel_id=1, source_target_pairs={{0,1},{1,4},{2,3},{3,6},{4,5},{5,8},{6,7},{7,10},{8,9},{9,12},{10,... | collective-permute-start | bytes 835592 | tf_op jit(solution)/shard_map/ppermute | solution.py:1235
  96.0 5.6 %all-to-all-start.2 = ((f32[32,8,128]{2,1,0:T(8,128)}), f32[32,8,128]{2,1,0:T(8,128)S(1)}, u32[]{:S(2)}, u32[]{:S(2)}) async-start(f32[32,8,128]{2,1,0:T(8,128)} %get-tuple-element.117), calls=%async_computation.2 | async-start | bytes 262144 | tf_op jit(solution)/shard_map/all_to_all | solution.py:1103
  101.7 7.9 %all-to-all-done.2.msg_in_ref = f32[32,8,128]{2,1,0:T(8,128)S(1)} async-done(((f32[32,8,128]{2,1,0:T(8,128)}), f32[32,8,128]{2,1,0:T(8,128)S(1)}, u32[]{:S(2)}, u32[]{:S(2)}) %all-to-all-start.2) | async-done | bytes 131104 | tf_op jit(solution)/shard_map/all_to_all | solution.py:1103
  111.4 19.2 %back.1 = (f32[4096,128]{1,0:T(8,128)}, f32[2048,128]{1,0:T(8,128)}, f32[144,128]{1,0:T(8,128)}, f32[144,128]{1,0:T(8,128)}, f32[8,128]{1,0:T(8,128)}, /*index=5...) custom-call(s32[5]{0:T(128)} %len_ref.11, ...), custom_call_target="tpu_custom_call", output_to_operand_aliasing={{5}: (18, {}), {6}: (19, {}), {7}: (20, {})} | custom-call | bytes 46800000 | tf_op jit(solution)/shard_map/back/pallas_call | solution.py:1257
  131.2 2.1 %collective-permute-done.15 = f32[144,128]{1,0:T(8,128)S(1)} collective-permute-done((f32[144,128]{1,0:T(8,128)}, f32[144,128]{1,0:T(8,128)S(1)}, u32[]{:S(2)}, u32[]{:S(2)}) %collective-permute-start.15) | collective-permute-done | bytes 73760 | tf_op jit(solution)/shard_map/ppermute | solution.py:1290
  134.2 1.8 %add.18.early_ref = f32[584,128]{1,0:T(8,128)} add(f32[584,128]{1,0:T(8,128)} %add.16, f32[584,128]{1,0:T(8,128)} %collective-permute-done.14) | non-fusion elementwise | flops 74752 | bytes 897024 | tf_op jit(solution)/shard_map/add | solution.py:1295
  139.1 2.3 %collective-permute-done.16 = f32[144,128]{1,0:T(8,128)S(1)} collective-permute-done((f32[144,128]{1,0:T(8,128)S(1)}, f32[144,128]{1,0:T(8,128)S(1)}, u32[]{:S(2)}, u32[]{:S(2)}) %collective-permute-start.16) | collective-permute-done | bytes 73760 | tf_op jit(solution)/shard_map/ppermute | solution.py:1294
  142.1 2.6 %collective-permute-start.21 = (f32[144,128]{1,0:T(8,128)}, f32[144,128]{1,0:T(8,128)}, u32[]{:S(2)}, u32[]{:S(2)}) collective-permute-start(f32[144,128]{1,0:T(8,128)} %add.19.refs_0_), channel_id=1, source_target_pairs={{0,24},{4,28},{8,16},{12,20},{16,8},{20,12},{24,0},{28,4},{1,25},{... | collective-permute-start | bytes 221192 | tf_op jit(solution)/shard_map/ppermute | solution.py:1306
  144.7 1.8 %collective-permute-start.19 = (f32[144,128]{1,0:T(8,128)}, f32[144,128]{1,0:T(8,128)}, u32[]{:S(2)}, u32[]{:S(2)}) collective-permute-start(f32[144,128]{1,0:T(8,128)} %add.19.refs_0_), channel_id=1, source_target_pairs={{0,8},{4,12},{8,0},{12,4},{16,24},{20,28},{24,16},{28,20},{1,9},{5... | collective-permute-start | bytes 221192 | tf_op jit(solution)/shard_map/ppermute | solution.py:1306
  146.5 3.1 %merge.1 = (f32[4096,128]{1,0:T(8,128)}, f32[2,32768]{1,0:T(2,128)}) custom-call(s32[5]{0:T(128)} %len_ref.11, f32[2048,128]{1,0:T(8,128)} %collective-permute-done.17.got_ref, f32[4096,128]{1,0:T(8,128)} %get-tuple-element.159.mix_in, f32[2,16384]{1,0:T(2,128)} %get-tuple-element.126.mine_ref, ...), custom_call_target="tpu_custom_call", output_to_operand_aliasing={{0}: (2, {})} | custom-call | bytes 10800000 | tf_op jit(solution)/shard_map/merge/pallas_call | solution.py:1309
  149.6 2.3 %collective-permute-done.20.refs_2_ = f32[144,128]{1,0:T(8,128)} collective-permute-done((f32[144,128]{1,0:T(8,128)}, f32[144,128]{1,0:T(8,128)}, u32[]{:S(2)}, u32[]{:S(2)}) %collective-permute-start.20) | collective-permute-done | bytes 73760 | tf_op jit(solution)/shard_map/ppermute | solution.py:1306
  151.9 1.9 %last.1 = (f32[128,128]{1,0:T(8,128)}, f32[1,128]{1,0:T(1,128)}, f32[1,128]{1,0:T(1,128)}, f32[1,128]{1,0:T(1,128)}, f32[1,128]{1,0:T(1,128)}, /*index=5*/f32[3,...) custom-call(f32[584,128]{1,0:T(8,128)} %add.18.early_ref, ...), custom_call_target="tpu_custom_call" | custom-call | tf_op jit(solution)/shard_map/last/pallas_call | solution.py:1325
  (51 shorter events, 13.6 us)
Async XLA Ops:
  2.7 15.4 %collective-permute-start.3 = (f32[264,128]{1,0:T(8,128)}, f32[264,128]{1,0:T(8,128)}, u32[]{:S(2)}, u32[]{:S(2)}) collective-permute-start(f32[264,128]{1,0:T(8,128)} %get-tuple-element.107), channel_id=1, source_target_pairs={{4,0},{8,4},{12,8},{16,12},{20,16},{24,20},{28,24},{5,1},{9,5},{13... | collective-permute-start | bytes 405512 | tf_op jit(solution)/shard_map/ppermute | solution.py:1131
  4.0 14.1 %collective-permute-start.2 = (f32[256,128]{1,0:T(8,128)}, f32[256,128]{1,0:T(8,128)}, u32[]{:S(2)}, u32[]{:S(2)}) collective-permute-start(f32[256,128]{1,0:T(8,128)} %get-tuple-element.106), channel_id=1, source_target_pairs={{0,4},{4,8},{8,12},{12,16},{16,20},{20,24},{24,28},{1,5},{5,9},{9,... | collective-permute-start | bytes 393224 | tf_op jit(solution)/shard_map/ppermute | solution.py:1130
  10.2 7.9 %collective-permute-start.1 = (f32[144,128]{1,0:T(8,128)}, f32[144,128]{1,0:T(8,128)}, u32[]{:S(2)}, u32[]{:S(2)}) collective-permute-start(f32[144,128]{1,0:T(8,128)} %get-tuple-element.105.own_ref), channel_id=1, source_target_pairs={{0,1},{1,0},{2,3},{3,2},{4,5},{5,4},{6,7},{7,6},{8,9},{9,8},{10,11... | collective-permute-start | bytes 221192 | tf_op jit(solution)/shard_map/ppermute | solution.py:1129
  10.2 7.9 %collective-permute-start = (f32[144,128]{1,0:T(8,128)}, f32[144,128]{1,0:T(8,128)}, u32[]{:S(2)}, u32[]{:S(2)}) collective-permute-start(f32[144,128]{1,0:T(8,128)} %get-tuple-element.105.own_ref), channel_id=1, source_target_pairs={{0,2},{1,3},{2,0},{3,1},{4,6},{5,7},{6,4},{7,5},{8,10},{9,11},{10,... | collective-permute-start | bytes 221192 | tf_op jit(solution)/shard_map/ppermute | solution.py:1128
  12.2 12.4 %collective-permute-start.6 = (f32[512,128]{1,0:T(8,128)}, f32[512,128]{1,0:T(8,128)}, u32[]{:S(2)}, u32[]{:S(2)}) collective-permute-start(f32[512,128]{1,0:T(8,128)} %get-tuple-element.116.refs_13_), channel_id=1, source_target_pairs={{0,2},{1,3},{2,0},{3,1},{4,6},{5,7},{6,4},{7,5},{8,10},{9,11},{10,... | collective-permute-start | bytes 786440 | tf_op jit(solution)/shard_map/ppermute | solution.py:1144
  18.1 14.1 %all-to-all-start = ((f32[32,8,128]{2,1,0:T(8,128)}), f32[32,8,128]{2,1,0:T(8,128)}, u32[]{:S(2)}, u32[]{:S(2)}) async-start(f32[32,8,128]{2,1,0:T(8,128)} %first.1), calls=%async_computation | async-start | bytes 262144 | tf_op jit(solution)/shard_map/all_to_all | solution.py:1103
  24.2 29.7 %collective-permute-start.5 = (f32[512,128]{1,0:T(8,128)}, f32[512,128]{1,0:T(8,128)}, u32[]{:S(2)}, u32[]{:S(2)}) collective-permute-start(f32[512,128]{1,0:T(8,128)} %get-tuple-element.116.refs_13_), channel_id=1, source_target_pairs={{0,1},{1,0},{2,3},{3,2},{4,5},{5,4},{6,7},{7,6},{8,9},{9,8},{10,11... | collective-permute-start | bytes 786440 | tf_op jit(solution)/shard_map/ppermute | solution.py:1145
  24.6 29.4 %collective-permute-start.7 = (f32[512,128]{1,0:T(8,128)}, f32[512,128]{1,0:T(8,128)}, u32[]{:S(2)}, u32[]{:S(2)}) collective-permute-start(f32[512,128]{1,0:T(8,128)} %collective-permute-done.6.refs_15_), channel_id=1, source_target_pairs={{0,1},{1,0},{2,3},{3,2},{4,5},{5,4},{6,7},{7,6},{8,9},{9,8},{10,11... | collective-permute-start | bytes 786440 | tf_op jit(solution)/shard_map/ppermute | solution.py:1146
  45.8 11.5 %all-to-all-start.1 = ((f32[32,8,128]{2,1,0:T(8,128)}), f32[32,8,128]{2,1,0:T(8,128)}, u32[]{:S(2)}, u32[]{:S(2)}) async-start(f32[32,8,128]{2,1,0:T(8,128)} %get-tuple-element.113), calls=%async_computation.1 | async-start | bytes 262144 | tf_op jit(solution)/shard_map/all_to_all | solution.py:1103
  88.9 1.9 %collective-permute-start.10 = (f32[584,128]{1,0:T(8,128)}, f32[584,128]{1,0:T(8,128)S(1)}, u32[]{:S(2)}, u32[]{:S(2)}) collective-permute-start(f32[584,128]{1,0:T(8,128)} %get-tuple-element.121), channel_id=1, source_target_pairs={{0,1},{1,0},{2,3},{3,2},{4,5},{5,4},{6,7},{7,6},{8,9},{9,8},{10,11... | collective-permute-start | bytes 897032 | tf_op jit(solution)/shard_map/ppermute | solution.py:1234
  91.8 17.8 %collective-permute-start.12 = (f32[2048,768]{1,0:T(8,128)}, f32[2048,768]{1,0:T(8,128)}, u32[]{:S(2)}, u32[]{:S(2)}) collective-permute-start(f32[2048,768]{1,0:T(8,128)} %get-tuple-element.125), channel_id=1, source_target_pairs={{0,1},{1,0},{2,3},{3,2},{4,5},{5,4},{6,7},{7,6},{8,9},{9,8},{10,11... | collective-permute-start | bytes 18874376 | tf_op jit(solution)/shard_map/ppermute | solution.py:1240
  92.0 17.6 %collective-permute-start.11 = (f32[584,128]{1,0:T(8,128)S(1)}, f32[584,128]{1,0:T(8,128)S(1)}, u32[]{:S(2)}, u32[]{:S(2)}) collective-permute-start(f32[584,128]{1,0:T(8,128)S(1)} %add.15), channel_id=1, source_target_pairs={{0,4},{4,0},{8,12},{12,8},{16,20},{20,16},{24,28},{28,24},{1,5},{5... | collective-permute-start | bytes 897032 | tf_op jit(solution)/shard_map/ppermute | solution.py:1239
  92.9 16.7 %collective-permute-start.8 = (f32[136,512]{1,0:T(8,128)}, f32[136,512]{1,0:T(8,128)S(1)}, u32[]{:S(2)}, u32[]{:S(2)}) collective-permute-start(f32[136,512]{1,0:T(8,128)} %get-tuple-element.118), channel_id=1, source_target_pairs={{0,1},{1,4},{2,3},{3,6},{4,5},{5,8},{6,7},{7,10},{8,9},{9,12},{10,... | collective-permute-start | bytes 835592 | tf_op jit(solution)/shard_map/ppermute | solution.py:1235
  94.7 14.9 %collective-permute-start.9 = (f32[128,512]{1,0:T(8,128)}, f32[128,512]{1,0:T(8,128)S(1)}, u32[]{:S(2)}, u32[]{:S(2)}) collective-permute-start(f32[128,512]{1,0:T(8,128)} %get-tuple-element.119), channel_id=1, source_target_pairs={{1,0},{4,1},{3,2},{6,3},{5,4},{8,5},{7,6},{10,7},{9,8},{12,9},{11,... | collective-permute-start | bytes 786440 | tf_op jit(solution)/shard_map/ppermute | solution.py:1236
  96.0 13.6 %all-to-all-start.2 = ((f32[32,8,128]{2,1,0:T(8,128)}), f32[32,8,128]{2,1,0:T(8,128)S(1)}, u32[]{:S(2)}, u32[]{:S(2)}) async-start(f32[32,8,128]{2,1,0:T(8,128)} %get-tuple-element.117), calls=%async_computation.2 | async-start | bytes 262144 | tf_op jit(solution)/shard_map/all_to_all | solution.py:1103
  101.6 8.0 %collective-permute-start.13 = (f32[2,16384]{1,0:T(2,128)}, f32[2,16384]{1,0:T(2,128)S(1)}, u32[]{:S(2)}, u32[]{:S(2)}) collective-permute-start(f32[2,16384]{1,0:T(2,128)} %get-tuple-element.126.mine_ref), channel_id=1, source_target_pairs={{0,1},{1,0},{2,3},{3,2},{4,5},{5,4},{6,7},{7,6},{8,9},{9,8},{10,11... | collective-permute-start | bytes 393224 | tf_op jit(solution)/shard_map/ppermute | solution.py:1241
  110.6 20.0 %collective-permute-start.14 = (f32[584,128]{1,0:T(8,128)}, f32[584,128]{1,0:T(8,128)}, u32[]{:S(2)}, u32[]{:S(2)}) collective-permute-start(f32[584,128]{1,0:T(8,128)} %add.16), channel_id=1, source_target_pairs={{0,16},{4,20},{8,24},{12,28},{16,0},{20,4},{24,8},{28,12},{1,17},{... | collective-permute-start | bytes 897032 | tf_op jit(solution)/shard_map/ppermute | solution.py:1246
  130.6 10.8 %collective-permute-start.17 = (f32[2048,128]{1,0:T(8,128)}, f32[2048,128]{1,0:T(8,128)}, u32[]{:S(2)}, u32[]{:S(2)}) collective-permute-start(f32[2048,128]{1,0:T(8,128)} %get-tuple-element.152), channel_id=1, source_target_pairs={{0,1},{1,0},{2,3},{3,2},{4,5},{5,4},{6,7},{7,6},{8,9},{9,8},{10,11... | collective-permute-start | bytes 3145736 | tf_op jit(solution)/shard_map/ppermute | solution.py:1291
  130.7 2.6 %collective-permute-start.15 = (f32[144,128]{1,0:T(8,128)}, f32[144,128]{1,0:T(8,128)S(1)}, u32[]{:S(2)}, u32[]{:S(2)}) collective-permute-start(f32[144,128]{1,0:T(8,128)} %get-tuple-element.147), channel_id=1, source_target_pairs={{0,1},{1,0},{2,3},{3,2},{4,5},{5,4},{6,7},{7,6},{8,9},{9,8},{10,11... | collective-permute-start | bytes 221192 | tf_op jit(solution)/shard_map/ppermute | solution.py:1290
  136.0 15.9 %collective-permute-start.22 = (f32[584,128]{1,0:T(8,128)}, f32[584,128]{1,0:T(8,128)}, u32[]{:S(2)}, u32[]{:S(2)}) collective-permute-start(f32[584,128]{1,0:T(8,128)} %add.18.early_ref), channel_id=1, source_target_pairs={{0,8},{4,12},{8,0},{12,4},{16,24},{20,28},{24,16},{28,20},{1,9},{5... | collective-permute-start | bytes 897032 | tf_op jit(solution)/shard_map/ppermute | solution.py:1297
  137.1 4.4 %collective-permute-start.16 = (f32[144,128]{1,0:T(8,128)S(1)}, f32[144,128]{1,0:T(8,128)S(1)}, u32[]{:S(2)}, u32[]{:S(2)}) collective-permute-start(f32[144,128]{1,0:T(8,128)S(1)} %add.17), channel_id=1, source_target_pairs={{0,4},{4,0},{8,12},{12,8},{16,20},{20,16},{24,28},{28,24},{1,5},{5... | collective-permute-start | bytes 221192 | tf_op jit(solution)/shard_map/ppermute | solution.py:1294
  142.1 7.5 %collective-permute-start.21 = (f32[144,128]{1,0:T(8,128)}, f32[144,128]{1,0:T(8,128)}, u32[]{:S(2)}, u32[]{:S(2)}) collective-permute-start(f32[144,128]{1,0:T(8,128)} %add.19.refs_0_), channel_id=1, source_target_pairs={{0,24},{4,28},{8,16},{12,20},{16,8},{20,12},{24,0},{28,4},{1,25},{... | collective-permute-start | bytes 221192 | tf_op jit(solution)/shard_map/ppermute | solution.py:1306
  144.7 7.2 %collective-permute-start.20 = (f32[144,128]{1,0:T(8,128)}, f32[144,128]{1,0:T(8,128)}, u32[]{:S(2)}, u32[]{:S(2)}) collective-permute-start(f32[144,128]{1,0:T(8,128)} %add.19.refs_0_), channel_id=1, source_target_pairs={{0,16},{4,20},{8,24},{12,28},{16,0},{20,4},{24,8},{28,12},{1,17},{... | collective-permute-start | bytes 221192 | tf_op jit(solution)/shard_map/ppermute | solution.py:1306
  144.7 7.2 %collective-permute-start.19 = (f32[144,128]{1,0:T(8,128)}, f32[144,128]{1,0:T(8,128)}, u32[]{:S(2)}, u32[]{:S(2)}) collective-permute-start(f32[144,128]{1,0:T(8,128)} %add.19.refs_0_), channel_id=1, source_target_pairs={{0,8},{4,12},{8,0},{12,4},{16,24},{20,28},{24,16},{28,20},{1,9},{5... | collective-permute-start | bytes 221192 | tf_op jit(solution)/shard_map/ppermute | solution.py:1306
  (7 other events, 12.4 us)

commit v4 on v3

--- a/solution.py
+++ b/solution.py
@@ -256,7 +256,7 @@
 def depth_kernel(
     len_ref, msg_in_ref, mix_ref, prev_ref, next_ref, own_ref, core_ref, x_ref, far_ref,
     hidden_ref, depth_ref, msg_ref, vec_ref, table_ref,
-    gathered, sems, weights, ring, sums, squares, counts, onehot,
+    gathered, weights, ring, sums, squares, counts, onehot,
 ):
     m = pl.program_id(0)
     last = pl.num_programs(0) - 1
@@ -267,17 +267,11 @@
 
     @pl.when(m == 0)
     def _():
-        copies = [
-            pltpu.make_async_copy(ref, gathered.at[half ^ k], sems.at[k])
-            for k, ref in enumerate((own_ref, core_ref, x_ref, far_ref))
-        ]
-        for copy in copies:
-            copy.start()
+        for k, ref in enumerate((own_ref, core_ref, x_ref, far_ref)):
+            gathered[half ^ k] = ref[...]
         merge_statistics(msg_in_ref, table_ref)
         for ref in (sums, squares, counts, onehot):
             ref[...] = jnp.zeros_like(ref)
-        for copy in copies:
-            copy.wait()
         for s in range(4):
             cut = column(s)
             weights[0:384, cut] = two_of(split(gathered[s, 0:128, :]), 0)
@@ -449,8 +443,8 @@
         mix_ref, skip_ref, enc_ref, cot_ref, packed_ref, basis_ref, vec_ref,
         b_out_ref, slope_skip_ref, own_ref, core_ref, x_ref, far_ref,
         block_ref, grad_skip_ref, grad_enc_ref, send_ref, wave_ref, r_ref, up_ref, down_ref, keep_ref, give_ref,
-        msg_ref, table_ref,
-        gathered, sems, w_out, w_out_t, w_mask, w_mask_t, decode, basis_back, normed_ref,
+        msg_ref, table_ref, w_out_t,
+        gathered, w_out, w_mask, w_mask_t, decode, basis_back, normed_ref,
         pull_ref, carry, acc_out, acc_mask, acc_basis, acc_vec,
         acc_small, entries, onehot,
     ) = refs[TM // STEP :]
@@ -467,12 +461,8 @@
 
     @pl.when(j == 0)
     def _():
-        copies = [
-            pltpu.make_async_copy(ref, gathered.at[half ^ k], sems.at[k])
-            for k, ref in enumerate((own_ref, core_ref, x_ref, far_ref))
-        ]
-        for copy in copies:
-            copy.start()
+        for k, ref in enumerate((own_ref, core_ref, x_ref, far_ref)):
+            gathered[half ^ k] = ref[...]
         merge_statistics(msg_in_ref, table_ref)
         for ref in (acc_out, acc_mask, acc_basis, acc_vec, acc_small, carry, entries):
             ref[...] = jnp.zeros_like(ref)
@@ -492,8 +482,6 @@
             with_lo = (row == col + 16).astype(F32).astype(BF16)
             back = mm(with_hi, b_hi) + mm(with_lo, b_lo)
             basis_back[:, c * HIDDEN : (c + 1) * HIDDEN] = back.astype(BF16)
-        for copy in copies:
-            copy.wait()
         for s in range(4):
             cut = column(s)
             for k in range(2):
@@ -674,12 +662,14 @@
 
     @pl.when(j == 0)
     def _():
-        down_ref[...] = r_ref[0:128, :]
+        down_ref[:, 0:128] = cot_ref[0:128, :]
+        down_ref[:, 128:256] = grad_skip_ref[0:128, :]
 
     @pl.when(j == last)
     def _():
-        up_ref[0:128, :] = r_ref[TM - 128 : TM, :]
-        up_ref[128:136, :] = jnp.zeros((8, HIDDEN), F32)
+        up_ref[0:128, 0:128] = cot_ref[TM - 128 : TM, :]
+        up_ref[0:128, 128:256] = grad_skip_ref[TM - 128 : TM, :]
+        up_ref[128:136, :] = jnp.zeros((8, 256), F32)
         up_ref[128:129, 0:128] = jnp.where(side == 0, carry[0:1, :], carry[1:2, :])
         up_ref[129:130, 0:128] = jnp.where(side == 0, carry[1:2, :], carry[0:1, :])
 
@@ -807,9 +797,9 @@
 
 def back_kernel(
     len_ref, msg_in_ref, depth_ref, r_a_ref, r_b_ref, low_ref, high_ref, hidden_ref, mix_ref, cot_ref,
-    vec_ref, table_in_ref, table_mid_ref, own_ref, core_ref, x_ref, far_ref, got_ref, block_in, skip_in, enc_in,
+    vec_ref, table_in_ref, table_mid_ref, w_out_t, own_ref, core_ref, x_ref, far_ref, got_ref, block_in, skip_in, enc_in,
     grad_mix_ref, send_ref, keep_ref, give_ref, edge_ref, block_ref, skip_ref, enc_ref,
-    gathered, sems, table, weights, ring, acc_w, acc_vec,
+    gathered, table, weights, ring, halo, acc_w, acc_vec,
 ):
     j = pl.program_id(0)
     last = pl.num_programs(0) - 1
@@ -826,12 +816,8 @@
 
     @pl.when(j == 0)
     def _():
-        copies = [
-            pltpu.make_async_copy(ref.at[pl.ds(0, 128)], gathered.at[half ^ k], sems.at[k])
-            for k, ref in enumerate((own_ref, core_ref, x_ref, far_ref))
-        ]
-        for copy in copies:
-            copy.start()
+        for k, ref in enumerate((own_ref, core_ref, x_ref, far_ref)):
+            gathered[half ^ k] = ref[...]
         totals = 0.5 * jnp.sum(msg_in_ref[...], axis=0)
         lane = iota((1, LANES), 1)
         number = jnp.zeros((1, LANES), jnp.int32)
@@ -848,8 +834,8 @@
         acc_w[...] = jnp.zeros_like(acc_w)
         acc_vec[...] = jnp.zeros_like(acc_vec)
         edge_ref[...] = low_ref[128:136, 0:128]
-        for copy in copies:
-            copy.wait()
+        for k, part in enumerate((low_ref[0:128, :], high_ref[...])):
+            halo[k] = mm(three(split(part), 1), w_out_t[...])
         for s in range(4):
             cut = column(s)
             hi, lo = split(gathered[s].T)
@@ -896,10 +882,10 @@
             halves = [None, None]
             for i in range(0, T, ROWS):
                 if i < STEP:
-                    r = jnp.where(j == 0, low_ref[i : i + ROWS, column(c)], r_a_ref[i : i + ROWS, column(c)])
+                    r = jnp.where(j == 0, halo[0, i : i + ROWS, column(c)], r_a_ref[i : i + ROWS, column(c)])
                 else:
                     cut = slice(i - STEP, i - STEP + ROWS)
-                    r = jnp.where(j == last, high_ref[cut, column(c)], r_b_ref[cut, column(c)])
+                    r = jnp.where(j == last, halo[1, cut, column(c)], r_b_ref[cut, column(c)])
                 depth = depth_ref[i : i + ROWS, column(c)]
                 s = sigmoid(depth)
                 u = depth * (1.0 - s)
@@ -1151,7 +1137,7 @@
         depth_kernel, "depth", tiles + 2,
         [
             whole(*msg_shape),
-            whole(frames, 128), whole(T, 128), whole(T + 8, 128), anywhere, anywhere, anywhere, anywhere,
+            whole(frames, 128), whole(T, 128), whole(T + 8, 128), *[whole(PACK_IN, 128)] * 4,
         ],
         [
             pl.BlockSpec((T, HIDDEN), lambda i, n: (i, 0)),
@@ -1163,7 +1149,7 @@
             struct(2, padded, LANES),
         ],
         [
-            vmem(4, PACK_IN, 128), pltpu.SemaphoreType.DMA((4,)), vmem16(512, HIDDEN), vmem(2, T, HIDDEN),
+            vmem(4, PACK_IN, 128), vmem16(512, HIDDEN), vmem(2, T, HIDDEN),
             vmem(4, entries, 128), vmem(4, entries, 128), vmem(entries, 128), vmem(entries, 128),
         ], 8,
     )(lengths, msg1, mix_in, mix_prev, mix_next, *packs)
@@ -1191,27 +1177,28 @@
         rows_m(128), jax.ShapeDtypeStruct((own_rows, 128), BF16), [], 6,
     )(lengths, cot_wave, cot_wave, mix_next, vec)
     pieces = TM // STEP
-    (block_out, grad_skip, grad_enc, send, wave_half, r, r_up, r_down, keep, give, msg3, table_mid) = call(
+    (block_out, grad_skip, grad_enc, send, wave_half, r, r_up, r_down, keep, give, msg3, table_mid, w_out_t) = call(
         mask_kernel, "mask", tiles_m,
         [
             whole(*msg_shape), *[depth_piece(k) for k in range(pieces)],
             half_rows(128), half_rows(128), half_rows(HIDDEN), half_rows(128),
             rows_m(128), whole(L, HIDDEN), whole(NVEC, HIDDEN), whole(1, 256), whole(1, 128),
-            anywhere, anywhere, anywhere, anywhere,
+            *[whole(512, 128)] * 4,
         ],
         [
             half_rows(128), half_rows(128), half_rows(HIDDEN), rows_m(768),
             pl.BlockSpec((2, TM * STRIDE), lambda i, n: (0, i)),
-            rows_m(HIDDEN), whole(136, HIDDEN), whole(128, HIDDEN), whole(EARLY, 128), whole(EARLY, 128),
-            whole(*msg_shape), whole(2, padded, LANES),
+            rows_m(HIDDEN), whole(136, 256), whole(128, 256), whole(EARLY, 128), whole(EARLY, 128),
+            whole(*msg_shape), whole(2, padded, LANES), whole(768, HIDDEN),
         ],
         [
             struct(frames, 128), struct(frames, 128), struct(frames, HIDDEN), struct(own_rows, 768),
-            struct(2, own_rows * STRIDE), struct(own_rows, HIDDEN), struct(136, HIDDEN), struct(128, HIDDEN),
+            struct(2, own_rows * STRIDE), struct(own_rows, HIDDEN), struct(136, 256), struct(128, 256),
             struct(EARLY, 128), struct(EARLY, 128), message, struct(2, padded, LANES),
+            jax.ShapeDtypeStruct((768, HIDDEN), BF16),
         ],
         [
-            vmem(4, 512, 128), pltpu.SemaphoreType.DMA((4,)), vmem16(1536, 256), vmem16(768, HIDDEN),
+            vmem(4, 512, 128), vmem16(1536, 256),
             vmem16(512, 1024), vmem16(2, 2, 512, 256), vmem16(2, 768, 256), vmem16(128, 1024), vmem(TM, HIDDEN), vmem(TM, HIDDEN), vmem(8, 128), vmem(256, 256), vmem(128, HIDDEN),
             vmem(2, 128, HIDDEN), vmem(8, HIDDEN), vmem(8, 128),
             vmem(8, 2 * tiles, 128), vmem(2 * tiles, 128),
@@ -1260,10 +1247,10 @@
             whole(*msg_shape), rows(HIDDEN),
             pl.BlockSpec((STEP, HIDDEN), lambda i, n: (jnp.maximum(2 * i - 1, 0), 0)),
             pl.BlockSpec((STEP, HIDDEN), lambda i, n: (jnp.minimum(2 * i, 2 * tiles - 1), 0)),
-            whole(136, HIDDEN), whole(128, HIDDEN),
+            whole(136, 256), whole(128, 256),
             pl.BlockSpec((T, HIDDEN), lambda i, n: (jnp.maximum(i, 1), 0)), own_tile(128), own_tile(128),
-            whole(NVEC, HIDDEN), whole(2, padded, LANES), whole(2, padded, LANES),
-            anywhere, anywhere, anywhere, anywhere,
+            whole(NVEC, HIDDEN), whole(2, padded, LANES), whole(2, padded, LANES), whole(768, HIDDEN),
+            *[whole(128, 128)] * 4,
             pl.BlockSpec((T, 768), lambda i, n: (jnp.minimum(i, tiles - 1), 0)), anywhere, anywhere, anywhere,
         ],
         [
@@ -1275,28 +1262,30 @@
             struct(frames, 128), struct(frames, 128), struct(frames, HIDDEN),
         ],
         [
-            vmem(4, 128, 128), pltpu.SemaphoreType.DMA((4,)), vmem(4, padded, LANES), vmem16(1024, 256),
-            vmem(2, T, HIDDEN), vmem(512, 256), vmem(16, HIDDEN),
+            vmem(4, 128, 128), vmem(4, padded, LANES), vmem16(1024, 256),
+            vmem(2, T, HIDDEN), vmem(2, 128, HIDDEN), vmem(512, 256), vmem(16, HIDDEN),
         ], 13,
-        input_output_aliases={18: 5, 19: 6, 20: 7},
+        input_output_aliases={19: 5, 20: 6, 21: 7},
     )(
-        lengths, msg3, depth, r, r, got_low, got_high, hidden, mix_in, cot_out, vec, table_in, table_mid, *packs, got,
+        lengths, msg3, depth, r, r, got_low, got_high, hidden, mix_in, cot_out, vec, table_in, table_mid, w_out_t, *packs, got,
         block_out, grad_skip, grad_enc,
     )
 
     grad_mix, mix_send, keep, give, edge, early_other = lax.optimization_barrier(
         (grad_mix, mix_send, keep, give, edge, early_other)
     )
-    late = keep + lax.ppermute(give, "src", swap)
-    mix_got = lax.ppermute(mix_send, "src", swap)
-    edge_other = lax.ppermute(edge, "src", swap)
-    late, early, early_other = lax.optimization_barrier((late, early, early_other))
-    late_other = lax.ppermute(late, "tm", hops[0])
+    late_give = lax.ppermute(give, "src", swap)
     early = early + early_other
     for hop in hops[1:-1]:
         early_other = lax.ppermute(early, "tm", hop)
         if hop is not hops[-2]:
             early = early + early_other
+    late_give, early = lax.optimization_barrier((late_give, early))
+    late = keep + late_give
+    late, edge, mix_send = lax.optimization_barrier((late, edge, mix_send))
+    late_other = lax.ppermute(late, "tm", hops[0])
+    mix_got = lax.ppermute(mix_send, "src", swap)
+    edge_other = lax.ppermute(edge, "src", swap)
     late, late_other, early, mix_got, edge_other = lax.optimization_barrier(
         (late, late_other, early, mix_got, edge_other)
     )

time: 155 us -> 149 us (0.961)
  waiting for transfers between devices: 28.7 us -> 19.6 us
  starting transfers between devices: 36.9 us -> 41.5 us
  Pallas kernels: 82 us -> 79.9 us
    all_to_all x3, waiting for transfers between devices: 17.8 us -> 10.7 us  [exchange(): return lax.all_to_all(msg, ('tm', 'src'), 0, 0)]
    ppermute x1, starting transfers between devices: 0.78 us -> 4.41 us  [local(): early_other = lax.ppermute(early, 'tm', hops[-1])]
    all_to_all x3, starting transfers between devices: 14.9 us -> 11.8 us  [exchange(): return lax.all_to_all(msg, ('tm', 'src'), 0, 0)]
    ppermute x1, waiting for transfers between devices: 2.1 us -> 0.01 us  [local(): late_give = lax.ppermute(give, 'src', swap)]
    ppermute x1, starting transfers between devices: 0.1 us -> 1.69 us  [local(): wave_other = lax.ppermute(wave_half, 'src', swap)]
  transfers between devices with their start and end apart: 26 -> 26, of which waited for: 9 -> 9; matrix products, arithmetic and copies ran while one was open for 2% -> 2% of each run, Pallas kernels for 30% -> 31%
where the time goes in v4:
time: 149 us; the launch traced here: 148 us
  Pallas kernels  79.9 us (54%)
  starting transfers between devices  41.5 us (28%)
  waiting for transfers between devices  19.6 us (13%)
  other arithmetic  5.21 us (3%)
    pallas_call x1, Pallas kernels, local(): call(mask_kernel, 'mask', tiles_m, [whole(*msg_shape), *[depth_piece(k) f...  30.7 us
    pallas_call x1, Pallas kernels, local(): call(back_kernel, 'back', tiles + 1, [whole(*msg_shape), rows(HIDDEN), pl...  18.7 us
    pallas_call x1, Pallas kernels, local(): call(depth_kernel, 'depth', tiles + 2, [whole(*msg_shape), whole(frames,...  12.8 us
    all_to_all x3, starting transfers between devices, exchange(): return lax.all_to_all(msg, ('tm', 'src'), 0, 0)  11.8 us
    all_to_all x3, waiting for transfers between devices, exchange(): return lax.all_to_all(msg, ('tm', 'src'), 0, 0)  10.7 us
    ppermute x1, starting transfers between devices, local(): mix_prev = lax.ppermute(high, 'tm', up)  6.16 us
    pallas_call x1, Pallas kernels, local(): call(first_kernel, 'first', 2, [pl.BlockSpec((frames // 2, 128), lambda i...  5.9 us
    pallas_call x1, Pallas kernels, local(): call(cotangent_kernel, 'cotangent', tiles_m, [pl.BlockSpec((2, TM * STRID...  4.66 us
  transfers between devices with their start and end apart: 26, of which 9 were waited for; matrix products, arithmetic and copies ran while one was open for 2% of the time, Pallas kernels for 31%

profile of v4, /device:TPU:0, one launch (start us, length us, event | category | flops | bytes accessed | tf_op | source)
XLA Modules:
  0.0 147.8 jit_solution(14789546476644654365)
XLA Ops:
  0.7 2.1 %prep.1 = (f32[144,128]{1,0:T(8,128)}, f32[512,128]{1,0:T(8,128)}, f32[264,128]{1,0:T(8,128)}, f32[256,128]{1,0:T(8,128)}) custom-call(f32[4096,128]{1,0:T(8,128)} %mix_ref.5, f32[4096,128]{1,0:T(8,128)} %mix_ref.5, f32[2,32768]{1,0:T(2,128)} %wave_next_ref.1, f32[128,128]{1,0:T(8,128)} %w_in_ref.3, f32[128,256]{1,0:T(8,128)} %w_out_ref.1, ...), custom_call_target="tpu_custom_call" | custom-call | tf_op jit(solution)/shard_map/prep/pallas_call | solution.py:1102
  4.0 6.2 %collective-permute-start.2 = (f32[256,128]{1,0:T(8,128)}, f32[256,128]{1,0:T(8,128)}, u32[]{:S(2)}, u32[]{:S(2)}) collective-permute-start(f32[256,128]{1,0:T(8,128)} %get-tuple-element.109), channel_id=1, source_target_pairs={{0,4},{4,8},{8,12},{12,16},{16,20},{20,24},{24,28},{1,5},{5,9},{9,... | collective-permute-start | bytes 393224 | tf_op jit(solution)/shard_map/ppermute | solution.py:1116
  10.2 2.0 %collective-permute-start = (f32[144,128]{1,0:T(8,128)}, f32[144,128]{1,0:T(8,128)}, u32[]{:S(2)}, u32[]{:S(2)}) collective-permute-start(f32[144,128]{1,0:T(8,128)} %get-tuple-element.108.own_ref), channel_id=1, source_target_pairs={{0,2},{1,3},{2,0},{3,1},{4,6},{5,7},{6,4},{7,5},{8,10},{9,11},{10,... | collective-permute-start | bytes 221192 | tf_op jit(solution)/shard_map/ppermute | solution.py:1114
  12.2 5.9 %first.1 = f32[32,8,128]{2,1,0:T(8,128)} custom-call(s32[5]{0:T(128)} %len_ref.11, f32[4096,128]{1,0:T(8,128)} %mix_ref.5, f32[128,128]{1,0:T(8,128)} %w_in_ref.3, f32[1,128]{1,0:T(1,128)} %bitcast.26, f32[1,128]{1,0:T(1,128)} %bitcast.28), custom_call_target="tpu_custom_call" | custom-call | bytes 14400000 | tf_op jit(solution)/shard_map/first/pallas_call | solution.py:1118
  18.1 5.7 %all-to-all-start = ((f32[32,8,128]{2,1,0:T(8,128)}), f32[32,8,128]{2,1,0:T(8,128)}, u32[]{:S(2)}, u32[]{:S(2)}) async-start(f32[32,8,128]{2,1,0:T(8,128)} %first.1), calls=%async_computation | async-start | bytes 262144 | tf_op jit(solution)/shard_map/all_to_all | solution.py:1089
  25.5 6.5 %all-to-all-done.msg_in_ref = f32[32,8,128]{2,1,0:T(8,128)} async-done(((f32[32,8,128]{2,1,0:T(8,128)}), f32[32,8,128]{2,1,0:T(8,128)}, u32[]{:S(2)}, u32[]{:S(2)}) %all-to-all-start) | async-done | bytes 131104 | tf_op jit(solution)/shard_map/all_to_all | solution.py:1089
  32.0 12.8 %depth.1 = (f32[2560,512]{1,0:T(8,128)}, f32[2304,512]{1,0:T(8,128)}, f32[32,8,128]{2,1,0:T(8,128)}, f32[16,512]{1,0:T(8,128)}, f32[2,8,128]{2,1,0:T(8,128)}) custom-call(s32[5]{0:T(128)} %len_ref.11, f32[32,8,128]{2,1,0:T(8,128)} %all-to-all-done.msg_in_ref, f32[4096,128]{1,0:T(8,128)} %mix_ref.5, f32[256,128]{1,0:T(8,128)} %collective-permute-done.2.prev_ref, ...), custom_call_target="tpu_custom_call" | custom-call | bytes 28800000 | tf_op jit(solution)/shard_map/depth/pallas_call | solution.py:1136
  44.8 3.5 %all-to-all-start.1 = ((f32[32,8,128]{2,1,0:T(8,128)}), f32[32,8,128]{2,1,0:T(8,128)}, u32[]{:S(2)}, u32[]{:S(2)}) async-start(f32[32,8,128]{2,1,0:T(8,128)} %get-tuple-element.116), calls=%async_computation.1 | async-start | bytes 262144 | tf_op jit(solution)/shard_map/all_to_all | solution.py:1089
  48.3 4.7 %cotangent.1.refs_8_ = bf16[2048,128]{1,0:T(8,128)(2,1)} custom-call(s32[5]{0:T(128)} %len_ref.11, f32[2,32768]{1,0:T(2,128)} %wave_next_ref.1, f32[2,32768]{1,0:T(2,128)} %wave_next_ref.1, f32[264,128]{1,0:T(8,128)} %collective-permute-done.3.next_ref.edge_next_ref, f32[16,512]{1,0:T(8,128)} %get-tuple-element.118.after_ref.refs_10_.vec_ref), custom_call_target="tpu_custom_call" | custom-call | bytes 21600000 | tf_op jit(solution)/shard_map/cotangent/pallas_call | solution.py:1167
  53.0 3.4 %all-to-all-done.1.msg_in_ref = f32[32,8,128]{2,1,0:T(8,128)} async-done(((f32[32,8,128]{2,1,0:T(8,128)}), f32[32,8,128]{2,1,0:T(8,128)}, u32[]{:S(2)}, u32[]{:S(2)}) %all-to-all-start.1) | async-done | bytes 131104 | tf_op jit(solution)/shard_map/all_to_all | solution.py:1089
  56.3 30.7 %mask.1 = (f32[4096,128]{1,0:T(8,128)}, f32[4096,128]{1,0:T(8,128)}, f32[4096,512]{1,0:T(8,128)}, f32[2048,768]{1,0:T(8,128)}, f32[2,16384]{1,0:T(2,128)}, /*ind...) custom-call(s32[5]{0:T(128)} %len_ref.11, ...), custom_call_target="tpu_custom_call" | custom-call | bytes 100800000 | tf_op jit(solution)/shard_map/mask/pallas_call | solution.py:1180
  87.2 1.8 %collective-permute-done.10 = f32[584,128]{1,0:T(8,128)S(1)} collective-permute-done((f32[584,128]{1,0:T(8,128)}, f32[584,128]{1,0:T(8,128)S(1)}, u32[]{:S(2)}, u32[]{:S(2)}) %collective-permute-start.10) | collective-permute-done | bytes 299040 | tf_op jit(solution)/shard_map/ppermute | solution.py:1221
  91.1 2.7 %all-to-all-start.2 = ((f32[32,8,128]{2,1,0:T(8,128)}), f32[32,8,128]{2,1,0:T(8,128)S(1)}, u32[]{:S(2)}, u32[]{:S(2)}) async-start(f32[32,8,128]{2,1,0:T(8,128)} %get-tuple-element.120), calls=%async_computation.2 | async-start | bytes 262144 | tf_op jit(solution)/shard_map/all_to_all | solution.py:1089
  93.8 2.8 %collective-permute-start.8 = (f32[136,256]{1,0:T(8,128)}, f32[136,256]{1,0:T(8,128)}, u32[]{:S(2)}, u32[]{:S(2)}) collective-permute-start(f32[136,256]{1,0:T(8,128)} %get-tuple-element.121), channel_id=1, source_target_pairs={{0,1},{1,4},{2,3},{3,6},{4,5},{5,8},{6,7},{7,10},{8,9},{9,12},{10,... | collective-permute-start | bytes 417800 | tf_op jit(solution)/shard_map/ppermute | solution.py:1222
  98.1 1.7 %collective-permute-start.13 = (f32[2,16384]{1,0:T(2,128)}, f32[2,16384]{1,0:T(2,128)S(1)}, u32[]{:S(2)}, u32[]{:S(2)}) collective-permute-start(f32[2,16384]{1,0:T(2,128)} %get-tuple-element.129.mine_ref), channel_id=1, source_target_pairs={{0,1},{1,0},{2,3},{3,2},{4,5},{5,4},{6,7},{7,6},{8,9},{9,8},{10,11... | collective-permute-start | bytes 393224 | tf_op jit(solution)/shard_map/ppermute | solution.py:1228
  102.9 4.4 %collective-permute-start.14 = (f32[584,128]{1,0:T(8,128)}, f32[584,128]{1,0:T(8,128)}, u32[]{:S(2)}, u32[]{:S(2)}) collective-permute-start(f32[584,128]{1,0:T(8,128)} %add.16), channel_id=1, source_target_pairs={{0,16},{4,20},{8,24},{12,28},{16,0},{20,4},{24,8},{28,12},{1,17},{... | collective-permute-start | bytes 897032 | tf_op jit(solution)/shard_map/ppermute | solution.py:1233
  107.3 18.7 %back.1 = (f32[4096,128]{1,0:T(8,128)}, f32[2048,128]{1,0:T(8,128)}, f32[144,128]{1,0:T(8,128)}, f32[144,128]{1,0:T(8,128)}, f32[8,128]{1,0:T(8,128)}, /*index=5...) custom-call(s32[5]{0:T(128)} %len_ref.11, ...), custom_call_target="tpu_custom_call", output_to_operand_aliasing={{5}: (19, {}), {6}: (20, {}), {7}: (21, {})} | custom-call | bytes 46800000 | tf_op jit(solution)/shard_map/back/pallas_call | solution.py:1244
  126.4 1.8 %add.17.early_ref = f32[584,128]{1,0:T(8,128)} add(f32[584,128]{1,0:T(8,128)} %add.16, f32[584,128]{1,0:T(8,128)} %collective-permute-done.14) | non-fusion elementwise | flops 74752 | bytes 897024 | tf_op jit(solution)/shard_map/add | solution.py:1278
  133.4 1.8 %collective-permute-done.16 = f32[144,128]{1,0:T(8,128)S(1)} collective-permute-done((f32[144,128]{1,0:T(8,128)S(1)}, f32[144,128]{1,0:T(8,128)S(1)}, u32[]{:S(2)}, u32[]{:S(2)}) %collective-permute-start.16) | collective-permute-done | bytes 73760 | tf_op jit(solution)/shard_map/ppermute | solution.py:1286
  136.9 1.8 %collective-permute-start.20 = (f32[144,128]{1,0:T(8,128)}, f32[144,128]{1,0:T(8,128)}, u32[]{:S(2)}, u32[]{:S(2)}) collective-permute-start(f32[144,128]{1,0:T(8,128)} %add.19.refs_0_), channel_id=1, source_target_pairs={{0,16},{4,20},{8,24},{12,28},{16,0},{20,4},{24,8},{28,12},{1,17},{... | collective-permute-start | bytes 221192 | tf_op jit(solution)/shard_map/ppermute | solution.py:1295
  138.7 1.5 %collective-permute-start.19 = (f32[144,128]{1,0:T(8,128)}, f32[144,128]{1,0:T(8,128)}, u32[]{:S(2)}, u32[]{:S(2)}) collective-permute-start(f32[144,128]{1,0:T(8,128)} %add.19.refs_0_), channel_id=1, source_target_pairs={{0,8},{4,12},{8,0},{12,4},{16,24},{20,28},{24,16},{28,20},{1,9},{5... | collective-permute-start | bytes 221192 | tf_op jit(solution)/shard_map/ppermute | solution.py:1295
  140.2 3.1 %merge.1 = (f32[4096,128]{1,0:T(8,128)}, f32[2,32768]{1,0:T(2,128)}) custom-call(s32[5]{0:T(128)} %len_ref.11, f32[2048,128]{1,0:T(8,128)} %collective-permute-done.17.got_ref, f32[4096,128]{1,0:T(8,128)} %get-tuple-element.165.mix_in, f32[2,16384]{1,0:T(2,128)} %get-tuple-element.129.mine_ref, ...), custom_call_target="tpu_custom_call", output_to_operand_aliasing={{0}: (2, {})} | custom-call | bytes 10800000 | tf_op jit(solution)/shard_map/merge/pallas_call | solution.py:1298
  143.3 2.3 %collective-permute-done.20.refs_2_ = f32[144,128]{1,0:T(8,128)} collective-permute-done((f32[144,128]{1,0:T(8,128)}, f32[144,128]{1,0:T(8,128)}, u32[]{:S(2)}, u32[]{:S(2)}) %collective-permute-start.20) | collective-permute-done | bytes 73760 | tf_op jit(solution)/shard_map/ppermute | solution.py:1295
  145.7 1.9 %last.1 = (f32[128,128]{1,0:T(8,128)}, f32[1,128]{1,0:T(1,128)}, f32[1,128]{1,0:T(1,128)}, f32[1,128]{1,0:T(1,128)}, f32[1,128]{1,0:T(1,128)}, /*index=5*/f32[3,...) custom-call(f32[584,128]{1,0:T(8,128)} %add.17.early_ref, ...), custom_call_target="tpu_custom_call" | custom-call | tf_op jit(solution)/shard_map/last/pallas_call | solution.py:1314
  (49 shorter events, 17.1 us)
Async XLA Ops:
  2.7 15.4 %collective-permute-start.3 = (f32[264,128]{1,0:T(8,128)}, f32[264,128]{1,0:T(8,128)}, u32[]{:S(2)}, u32[]{:S(2)}) collective-permute-start(f32[264,128]{1,0:T(8,128)} %get-tuple-element.110), channel_id=1, source_target_pairs={{4,0},{8,4},{12,8},{16,12},{20,16},{24,20},{28,24},{5,1},{9,5},{13... | collective-permute-start | bytes 405512 | tf_op jit(solution)/shard_map/ppermute | solution.py:1117
  4.0 14.1 %collective-permute-start.2 = (f32[256,128]{1,0:T(8,128)}, f32[256,128]{1,0:T(8,128)}, u32[]{:S(2)}, u32[]{:S(2)}) collective-permute-start(f32[256,128]{1,0:T(8,128)} %get-tuple-element.109), channel_id=1, source_target_pairs={{0,4},{4,8},{8,12},{12,16},{16,20},{20,24},{24,28},{1,5},{5,9},{9,... | collective-permute-start | bytes 393224 | tf_op jit(solution)/shard_map/ppermute | solution.py:1116
  10.2 7.9 %collective-permute-start.1 = (f32[144,128]{1,0:T(8,128)}, f32[144,128]{1,0:T(8,128)}, u32[]{:S(2)}, u32[]{:S(2)}) collective-permute-start(f32[144,128]{1,0:T(8,128)} %get-tuple-element.108.own_ref), channel_id=1, source_target_pairs={{0,1},{1,0},{2,3},{3,2},{4,5},{5,4},{6,7},{7,6},{8,9},{9,8},{10,11... | collective-permute-start | bytes 221192 | tf_op jit(solution)/shard_map/ppermute | solution.py:1115
  10.2 7.9 %collective-permute-start = (f32[144,128]{1,0:T(8,128)}, f32[144,128]{1,0:T(8,128)}, u32[]{:S(2)}, u32[]{:S(2)}) collective-permute-start(f32[144,128]{1,0:T(8,128)} %get-tuple-element.108.own_ref), channel_id=1, source_target_pairs={{0,2},{1,3},{2,0},{3,1},{4,6},{5,7},{6,4},{7,5},{8,10},{9,11},{10,... | collective-permute-start | bytes 221192 | tf_op jit(solution)/shard_map/ppermute | solution.py:1114
  12.1 12.2 %collective-permute-start.6 = (f32[512,128]{1,0:T(8,128)}, f32[512,128]{1,0:T(8,128)}, u32[]{:S(2)}, u32[]{:S(2)}) collective-permute-start(f32[512,128]{1,0:T(8,128)} %get-tuple-element.119.refs_13_), channel_id=1, source_target_pairs={{0,2},{1,3},{2,0},{3,1},{4,6},{5,7},{6,4},{7,5},{8,10},{9,11},{10,... | collective-permute-start | bytes 786440 | tf_op jit(solution)/shard_map/ppermute | solution.py:1130
  18.1 13.9 %all-to-all-start = ((f32[32,8,128]{2,1,0:T(8,128)}), f32[32,8,128]{2,1,0:T(8,128)}, u32[]{:S(2)}, u32[]{:S(2)}) async-start(f32[32,8,128]{2,1,0:T(8,128)} %first.1), calls=%async_computation | async-start | bytes 262144 | tf_op jit(solution)/shard_map/all_to_all | solution.py:1089
  24.0 28.9 %collective-permute-start.5 = (f32[512,128]{1,0:T(8,128)}, f32[512,128]{1,0:T(8,128)}, u32[]{:S(2)}, u32[]{:S(2)}) collective-permute-start(f32[512,128]{1,0:T(8,128)} %get-tuple-element.119.refs_13_), channel_id=1, source_target_pairs={{0,1},{1,0},{2,3},{3,2},{4,5},{5,4},{6,7},{7,6},{8,9},{9,8},{10,11... | collective-permute-start | bytes 786440 | tf_op jit(solution)/shard_map/ppermute | solution.py:1131
  24.4 28.6 %collective-permute-start.7 = (f32[512,128]{1,0:T(8,128)}, f32[512,128]{1,0:T(8,128)}, u32[]{:S(2)}, u32[]{:S(2)}) collective-permute-start(f32[512,128]{1,0:T(8,128)} %collective-permute-done.6.refs_15_), channel_id=1, source_target_pairs={{0,1},{1,0},{2,3},{3,2},{4,5},{5,4},{6,7},{7,6},{8,9},{9,8},{10,11... | collective-permute-start | bytes 786440 | tf_op jit(solution)/shard_map/ppermute | solution.py:1132
  44.8 11.5 %all-to-all-start.1 = ((f32[32,8,128]{2,1,0:T(8,128)}), f32[32,8,128]{2,1,0:T(8,128)}, u32[]{:S(2)}, u32[]{:S(2)}) async-start(f32[32,8,128]{2,1,0:T(8,128)} %get-tuple-element.116), calls=%async_computation.1 | async-start | bytes 262144 | tf_op jit(solution)/shard_map/all_to_all | solution.py:1089
  87.1 1.9 %collective-permute-start.10 = (f32[584,128]{1,0:T(8,128)}, f32[584,128]{1,0:T(8,128)S(1)}, u32[]{:S(2)}, u32[]{:S(2)}) collective-permute-start(f32[584,128]{1,0:T(8,128)} %get-tuple-element.124), channel_id=1, source_target_pairs={{0,1},{1,0},{2,3},{3,2},{4,5},{5,4},{6,7},{7,6},{8,9},{9,8},{10,11... | collective-permute-start | bytes 897032 | tf_op jit(solution)/shard_map/ppermute | solution.py:1221
  90.0 12.1 %collective-permute-start.12 = (f32[2048,768]{1,0:T(8,128)}, f32[2048,768]{1,0:T(8,128)}, u32[]{:S(2)}, u32[]{:S(2)}) collective-permute-start(f32[2048,768]{1,0:T(8,128)} %get-tuple-element.128), channel_id=1, source_target_pairs={{0,1},{1,0},{2,3},{3,2},{4,5},{5,4},{6,7},{7,6},{8,9},{9,8},{10,11... | collective-permute-start | bytes 18874376 | tf_op jit(solution)/shard_map/ppermute | solution.py:1227
  90.2 11.9 %collective-permute-start.11 = (f32[584,128]{1,0:T(8,128)S(1)}, f32[584,128]{1,0:T(8,128)S(1)}, u32[]{:S(2)}, u32[]{:S(2)}) collective-permute-start(f32[584,128]{1,0:T(8,128)S(1)} %add.15), channel_id=1, source_target_pairs={{0,4},{4,0},{8,12},{12,8},{16,20},{20,16},{24,28},{28,24},{1,5},{5... | collective-permute-start | bytes 897032 | tf_op jit(solution)/shard_map/ppermute | solution.py:1226
  91.1 10.9 %all-to-all-start.2 = ((f32[32,8,128]{2,1,0:T(8,128)}), f32[32,8,128]{2,1,0:T(8,128)S(1)}, u32[]{:S(2)}, u32[]{:S(2)}) async-start(f32[32,8,128]{2,1,0:T(8,128)} %get-tuple-element.120), calls=%async_computation.2 | async-start | bytes 262144 | tf_op jit(solution)/shard_map/all_to_all | solution.py:1089
  93.8 7.4 %collective-permute-start.8 = (f32[136,256]{1,0:T(8,128)}, f32[136,256]{1,0:T(8,128)}, u32[]{:S(2)}, u32[]{:S(2)}) collective-permute-start(f32[136,256]{1,0:T(8,128)} %get-tuple-element.121), channel_id=1, source_target_pairs={{0,1},{1,4},{2,3},{3,6},{4,5},{5,8},{6,7},{7,10},{8,9},{9,12},{10,... | collective-permute-start | bytes 417800 | tf_op jit(solution)/shard_map/ppermute | solution.py:1222
  96.6 4.0 %collective-permute-start.9 = (f32[128,256]{1,0:T(8,128)}, f32[128,256]{1,0:T(8,128)S(1)}, u32[]{:S(2)}, u32[]{:S(2)}) collective-permute-start(f32[128,256]{1,0:T(8,128)} %get-tuple-element.122), channel_id=1, source_target_pairs={{1,0},{4,1},{3,2},{6,3},{5,4},{8,5},{7,6},{10,7},{9,8},{12,9},{11,... | collective-permute-start | bytes 393224 | tf_op jit(solution)/shard_map/ppermute | solution.py:1223
  98.1 3.9 %collective-permute-start.13 = (f32[2,16384]{1,0:T(2,128)}, f32[2,16384]{1,0:T(2,128)S(1)}, u32[]{:S(2)}, u32[]{:S(2)}) collective-permute-start(f32[2,16384]{1,0:T(2,128)} %get-tuple-element.129.mine_ref), channel_id=1, source_target_pairs={{0,1},{1,0},{2,3},{3,2},{4,5},{5,4},{6,7},{7,6},{8,9},{9,8},{10,11... | collective-permute-start | bytes 393224 | tf_op jit(solution)/shard_map/ppermute | solution.py:1228
  102.9 23.1 %collective-permute-start.14 = (f32[584,128]{1,0:T(8,128)}, f32[584,128]{1,0:T(8,128)}, u32[]{:S(2)}, u32[]{:S(2)}) collective-permute-start(f32[584,128]{1,0:T(8,128)} %add.16), channel_id=1, source_target_pairs={{0,16},{4,20},{8,24},{12,28},{16,0},{20,4},{24,8},{28,12},{1,17},{... | collective-permute-start | bytes 897032 | tf_op jit(solution)/shard_map/ppermute | solution.py:1233
  126.0 2.3 %collective-permute-start.15 = (f32[144,128]{1,0:T(8,128)}, f32[144,128]{1,0:T(8,128)S(1)}, u32[]{:S(2)}, u32[]{:S(2)}) collective-permute-start(f32[144,128]{1,0:T(8,128)} %get-tuple-element.151), channel_id=1, source_target_pairs={{0,1},{1,0},{2,3},{3,2},{4,5},{5,4},{6,7},{7,6},{8,9},{9,8},{10,11... | collective-permute-start | bytes 221192 | tf_op jit(solution)/shard_map/ppermute | solution.py:1277
  129.2 6.0 %collective-permute-start.17 = (f32[2048,128]{1,0:T(8,128)}, f32[2048,128]{1,0:T(8,128)}, u32[]{:S(2)}, u32[]{:S(2)}) collective-permute-start(f32[2048,128]{1,0:T(8,128)} %get-tuple-element.158), channel_id=1, source_target_pairs={{0,1},{1,0},{2,3},{3,2},{4,5},{5,4},{6,7},{7,6},{8,9},{9,8},{10,11... | collective-permute-start | bytes 3145736 | tf_op jit(solution)/shard_map/ppermute | solution.py:1287
  129.4 16.3 %collective-permute-start.22 = (f32[584,128]{1,0:T(8,128)}, f32[584,128]{1,0:T(8,128)}, u32[]{:S(2)}, u32[]{:S(2)}) collective-permute-start(f32[584,128]{1,0:T(8,128)} %add.17.early_ref), channel_id=1, source_target_pairs={{0,8},{4,12},{8,0},{12,4},{16,24},{20,28},{24,16},{28,20},{1,9},{5... | collective-permute-start | bytes 897032 | tf_op jit(solution)/shard_map/ppermute | solution.py:1280
  130.9 4.4 %collective-permute-start.16 = (f32[144,128]{1,0:T(8,128)S(1)}, f32[144,128]{1,0:T(8,128)S(1)}, u32[]{:S(2)}, u32[]{:S(2)}) collective-permute-start(f32[144,128]{1,0:T(8,128)S(1)} %add.18), channel_id=1, source_target_pairs={{0,4},{4,0},{8,12},{12,8},{16,20},{20,16},{24,28},{28,24},{1,5},{5... | collective-permute-start | bytes 221192 | tf_op jit(solution)/shard_map/ppermute | solution.py:1286
  135.8 7.5 %collective-permute-start.21 = (f32[144,128]{1,0:T(8,128)}, f32[144,128]{1,0:T(8,128)}, u32[]{:S(2)}, u32[]{:S(2)}) collective-permute-start(f32[144,128]{1,0:T(8,128)} %add.19.refs_0_), channel_id=1, source_target_pairs={{0,24},{4,28},{8,16},{12,20},{16,8},{20,12},{24,0},{28,4},{1,25},{... | collective-permute-start | bytes 221192 | tf_op jit(solution)/shard_map/ppermute | solution.py:1295
  136.9 8.8 %collective-permute-start.20 = (f32[144,128]{1,0:T(8,128)}, f32[144,128]{1,0:T(8,128)}, u32[]{:S(2)}, u32[]{:S(2)}) collective-permute-start(f32[144,128]{1,0:T(8,128)} %add.19.refs_0_), channel_id=1, source_target_pairs={{0,16},{4,20},{8,24},{12,28},{16,0},{20,4},{24,8},{28,12},{1,17},{... | collective-permute-start | bytes 221192 | tf_op jit(solution)/shard_map/ppermute | solution.py:1295
  138.7 7.0 %collective-permute-start.19 = (f32[144,128]{1,0:T(8,128)}, f32[144,128]{1,0:T(8,128)}, u32[]{:S(2)}, u32[]{:S(2)}) collective-permute-start(f32[144,128]{1,0:T(8,128)} %add.19.refs_0_), channel_id=1, source_target_pairs={{0,8},{4,12},{8,0},{12,4},{16,24},{20,28},{24,16},{28,20},{1,9},{5... | collective-permute-start | bytes 221192 | tf_op jit(solution)/shard_map/ppermute | solution.py:1295
  (6 other events, 11.6 us)

commit v5 on v4

--- a/solution.py
+++ b/solution.py
@@ -15,8 +15,9 @@
 T = 256
 T1 = 512
 TM = 512
-ROWS = 32
+ROWS = 16
 LANES = 128
+GROUP = 16
 F32 = jnp.float32
 BF16 = jnp.bfloat16
 NVEC = 16
@@ -143,9 +144,13 @@
     item_mean = item_sum / jnp.maximum(item_number, 1.0)
     away = mean - item_mean
     item_spread = colsum(onehot * (spread + number * away * away))
-    msg = cat(
-        [item_sum, item_spread, item_number, item_mean, jnp.zeros((4, LANES), F32)], 0
-    )
+    lines = (item_sum, item_spread, item_number, item_mean)
+    if msg_ref.shape[1] == 1:
+        msg = lines[0]
+        for k, line in enumerate(lines[1:]):
+            msg = msg + pltpu.roll(line, GROUP * (k + 1), 1)
+    else:
+        msg = cat([*lines, jnp.zeros((4, LANES), F32)], 0)
     for i in range(msg_ref.shape[0]):
         msg_ref[i] = msg
 
@@ -159,11 +164,22 @@
 
 def merge_statistics(msg_ref, table_ref):
     msg = msg_ref[...]
-    item_sum = jnp.sum(msg[:, 0:1, :], axis=0)
-    number = jnp.sum(msg[:, 2:3, :], axis=0)
-    mean = item_sum / jnp.maximum(number, 1.0)
-    away = msg[:, 3:4, :] - mean[None]
-    squares = jnp.sum(msg[:, 1:2, :] + msg[:, 2:3, :] * away * away, axis=0)
+    if msg_ref.shape[1] == 1:
+        totals = jnp.sum(msg, axis=0)
+        first = iota((1, LANES), 1) < GROUP
+        item_sum = jnp.where(first, totals, 0.0)
+        number = jnp.where(first, pltpu.roll(totals, LANES - 2 * GROUP, 1), 0.0)
+        mean = item_sum / jnp.maximum(number, 1.0)
+        away = msg - pltpu.roll(mean, 3 * GROUP, 1)[None]
+        around = jnp.sum(pltpu.roll(msg, GROUP, 2) * away * away, axis=0)
+        squares = pltpu.roll(totals, LANES - GROUP, 1) + pltpu.roll(around, LANES - 3 * GROUP, 1)
+        squares = jnp.where(first, squares, 0.0)
+    else:
+        item_sum = jnp.sum(msg[:, 0:1, :], axis=0)
+        number = jnp.sum(msg[:, 2:3, :], axis=0)
+        mean = item_sum / jnp.maximum(number, 1.0)
+        away = msg[:, 3:4, :] - mean[None]
+        squares = jnp.sum(msg[:, 1:2, :] + msg[:, 2:3, :] * away * away, axis=0)
     inverse = lax.rsqrt(squares / jnp.maximum(number, 1.0) + EPS)
     padded = table_ref.shape[1]
     table_ref[0] = to_rows(mean, padded)
@@ -1084,6 +1100,8 @@
 
     msg_shape = (devices, 8, LANES)
     message = struct(*msg_shape)
+    stat_shape = (devices, 1, LANES) if items <= GROUP else msg_shape
+    statistic = struct(*stat_shape)
 
     def exchange(msg):
         return lax.all_to_all(msg, ("tm", "src"), 0, 0)
@@ -1142,10 +1160,10 @@
         [
             pl.BlockSpec((T, HIDDEN), lambda i, n: (i, 0)),
             pl.BlockSpec((T, HIDDEN), lambda i, n: (jnp.maximum(i - 1, 0), 0)),
-            whole(*msg_shape), whole(NVEC, HIDDEN), whole(2, padded, LANES),
+            whole(*stat_shape), whole(NVEC, HIDDEN), whole(2, padded, LANES),
         ],
         [
-            struct(own_rows + 2 * T, HIDDEN), struct(own_rows + T, HIDDEN), message, struct(NVEC, HIDDEN),
+            struct(own_rows + 2 * T, HIDDEN), struct(own_rows + T, HIDDEN), statistic, struct(NVEC, HIDDEN),
             struct(2, padded, LANES),
         ],
         [
@@ -1180,7 +1198,7 @@
     (block_out, grad_skip, grad_enc, send, wave_half, r, r_up, r_down, keep, give, msg3, table_mid, w_out_t) = call(
         mask_kernel, "mask", tiles_m,
         [
-            whole(*msg_shape), *[depth_piece(k) for k in range(pieces)],
+            whole(*stat_shape), *[depth_piece(k) for k in range(pieces)],
             half_rows(128), half_rows(128), half_rows(HIDDEN), half_rows(128),
             rows_m(128), whole(L, HIDDEN), whole(NVEC, HIDDEN), whole(1, 256), whole(1, 128),
             *[whole(512, 128)] * 4,
@@ -1222,13 +1240,13 @@
     got_low = lax.ppermute(r_up, both, later)
     got_high = lax.ppermute(r_down, both, earlier)
     msg3 = exchange(msg3)
-    early, send, wave_half = lax.optimization_barrier((early, send, wave_half))
+    early, send = lax.optimization_barrier((early, send))
     early_other = lax.ppermute(early, "tm", hops[0])
     got = lax.ppermute(send, "src", swap)
+    msg3, got_low, got_high, early, early_other, got, wave_half = lax.optimization_barrier(
+        (msg3, got_low, got_high, early, early_other, got, wave_half)
+    )
     wave_other = lax.ppermute(wave_half, "src", swap)
-    msg3, got_low, got_high, early, early_other, got, wave_other = lax.optimization_barrier(
-        (msg3, got_low, got_high, early, early_other, got, wave_other)
-    )
     early = early + early_other
     early_other = lax.ppermute(early, "tm", hops[-1])
 
@@ -1271,8 +1289,8 @@
         block_out, grad_skip, grad_enc,
     )
 
-    grad_mix, mix_send, keep, give, edge, early_other = lax.optimization_barrier(
-        (grad_mix, mix_send, keep, give, edge, early_other)
+    grad_mix, mix_send, keep, give, edge, early_other, wave_other = lax.optimization_barrier(
+        (grad_mix, mix_send, keep, give, edge, early_other, wave_other)
     )
     late_give = lax.ppermute(give, "src", swap)
     early = early + early_other

time: 149 us -> 148 us (level)
    ppermute x1, starting transfers between devices: 0.04 us -> 2.94 us  [local(): wide_x = lax.ppermute(wide, 'src', cross)]
    all_to_all x3, waiting for transfers between devices: 10.7 us -> 8.65 us  [exchange(): return lax.all_to_all(msg, ('tm', 'src'), 0, 0)]
    ppermute x1, starting transfers between devices: 1.99 us -> 0.04 us  [local(): pack_x = lax.ppermute(pack, 'src', cross)]
    ppermute x1, waiting for transfers between devices: 0.76 us -> 2.44 us  [local(): got_high = lax.ppermute(r_down, both, earlier)]
    all_to_all x3, starting transfers between devices: 11.8 us -> 13.4 us  [exchange(): return lax.all_to_all(msg, ('tm', 'src'), 0, 0)]
where the time goes in v5:
time: 148 us; the launch traced here: 147 us
  Pallas kernels  79.9 us (54%)
  starting transfers between devices  40.5 us (27%)
  waiting for transfers between devices  20 us (14%)
  other arithmetic  5.23 us (4%)
    pallas_call x1, Pallas kernels, local(): call(mask_kernel, 'mask', tiles_m, [whole(*stat_shape), *[depth_piece(k)...  30.7 us
    pallas_call x1, Pallas kernels, local(): call(back_kernel, 'back', tiles + 1, [whole(*msg_shape), rows(HIDDEN), pl...  18.7 us
    all_to_all x3, starting transfers between devices, exchange(): return lax.all_to_all(msg, ('tm', 'src'), 0, 0)  13.4 us
    pallas_call x1, Pallas kernels, local(): call(depth_kernel, 'depth', tiles + 2, [whole(*msg_shape), whole(frames,...  12.8 us
    all_to_all x3, waiting for transfers between devices, exchange(): return lax.all_to_all(msg, ('tm', 'src'), 0, 0)  8.65 us
    pallas_call x1, Pallas kernels, local(): call(first_kernel, 'first', 2, [pl.BlockSpec((frames // 2, 128), lambda i...  5.96 us
    ppermute x1, starting transfers between devices, local(): mix_prev = lax.ppermute(high, 'tm', up)  5.21 us
    pallas_call x1, Pallas kernels, local(): call(cotangent_kernel, 'cotangent', tiles_m, [pl.BlockSpec((2, TM * STRID...  4.66 us
  transfers between devices with their start and end apart: 26, of which 9 were waited for; matrix products, arithmetic and copies ran while one was open for 2% of the time, Pallas kernels for 31%

profile of v5, /device:TPU:0, one launch (start us, length us, event | category | flops | bytes accessed | tf_op | source)
XLA Modules:
  0.0 147.2 jit_solution(12720567656005540613)
XLA Ops:
  0.7 2.1 %prep.1 = (f32[144,128]{1,0:T(8,128)}, f32[512,128]{1,0:T(8,128)}, f32[264,128]{1,0:T(8,128)}, f32[256,128]{1,0:T(8,128)}) custom-call(f32[4096,128]{1,0:T(8,128)} %mix_ref.5, f32[4096,128]{1,0:T(8,128)} %mix_ref.5, f32[2,32768]{1,0:T(2,128)} %wave_next_ref.1, f32[128,128]{1,0:T(8,128)} %w_in_ref.3, f32[128,256]{1,0:T(8,128)} %w_out_ref.1, ...), custom_call_target="tpu_custom_call" | custom-call | tf_op jit(solution)/shard_map/prep/pallas_call | solution.py:1120
  2.7 2.9 %collective-permute-start.6 = (f32[512,128]{1,0:T(8,128)}, f32[512,128]{1,0:T(8,128)}, u32[]{:S(2)}, u32[]{:S(2)}) collective-permute-start(f32[512,128]{1,0:T(8,128)} %get-tuple-element.119.refs_13_), channel_id=1, source_target_pairs={{0,2},{1,3},{2,0},{3,1},{4,6},{5,7},{6,4},{7,5},{8,10},{9,11},{10,... | collective-permute-start | bytes 786440 | tf_op jit(solution)/shard_map/ppermute | solution.py:1148
  6.9 5.2 %collective-permute-start.2 = (f32[256,128]{1,0:T(8,128)}, f32[256,128]{1,0:T(8,128)}, u32[]{:S(2)}, u32[]{:S(2)}) collective-permute-start(f32[256,128]{1,0:T(8,128)} %get-tuple-element.109), channel_id=1, source_target_pairs={{0,4},{4,8},{8,12},{12,16},{16,20},{20,24},{24,28},{1,5},{5,9},{9,... | collective-permute-start | bytes 393224 | tf_op jit(solution)/shard_map/ppermute | solution.py:1134
  12.2 6.0 %first.1 = f32[32,8,128]{2,1,0:T(8,128)} custom-call(s32[5]{0:T(128)} %len_ref.11, f32[4096,128]{1,0:T(8,128)} %mix_ref.5, f32[128,128]{1,0:T(8,128)} %w_in_ref.3, f32[1,128]{1,0:T(1,128)} %bitcast.26, f32[1,128]{1,0:T(1,128)} %bitcast.28), custom_call_target="tpu_custom_call" | custom-call | bytes 14400000 | tf_op jit(solution)/shard_map/first/pallas_call | solution.py:1136
  18.2 5.9 %all-to-all-start = ((f32[32,8,128]{2,1,0:T(8,128)}), f32[32,8,128]{2,1,0:T(8,128)}, u32[]{:S(2)}, u32[]{:S(2)}) async-start(f32[32,8,128]{2,1,0:T(8,128)} %first.1), calls=%async_computation | async-start | bytes 262144 | tf_op jit(solution)/shard_map/all_to_all | solution.py:1107
  24.8 1.7 %collective-permute-done.4.far_ref = f32[144,128]{1,0:T(8,128)} collective-permute-done((f32[144,128]{1,0:T(8,128)}, f32[144,128]{1,0:T(8,128)}, u32[]{:S(2)}, u32[]{:S(2)}) %collective-permute-start.4) | collective-permute-done | bytes 73760 | tf_op jit(solution)/shard_map/ppermute | solution.py:1145
  26.5 5.8 %all-to-all-done.msg_in_ref = f32[32,8,128]{2,1,0:T(8,128)} async-done(((f32[32,8,128]{2,1,0:T(8,128)}), f32[32,8,128]{2,1,0:T(8,128)}, u32[]{:S(2)}, u32[]{:S(2)}) %all-to-all-start) | async-done | bytes 131104 | tf_op jit(solution)/shard_map/all_to_all | solution.py:1107
  32.3 12.8 %depth.1 = (f32[2560,512]{1,0:T(8,128)}, f32[2304,512]{1,0:T(8,128)}, f32[32,1,128]{2,1,0:T(1,128)}, f32[16,512]{1,0:T(8,128)}, f32[2,8,128]{2,1,0:T(8,128)}) custom-call(s32[5]{0:T(128)} %len_ref.11, f32[32,8,128]{2,1,0:T(8,128)} %all-to-all-done.msg_in_ref, f32[4096,128]{1,0:T(8,128)} %mix_ref.5, f32[256,128]{1,0:T(8,128)} %collective-permute-done.2.prev_ref, ...), custom_call_target="tpu_custom_call" | custom-call | bytes 28800000 | tf_op jit(solution)/shard_map/depth/pallas_call | solution.py:1154
  45.0 3.4 %all-to-all-start.1 = ((f32[32,1,128]{2,1,0:T(1,128)}), f32[32,1,128]{2,1,0:T(1,128)}, u32[]{:S(2)}, u32[]{:S(2)}) async-start(f32[32,1,128]{2,1,0:T(1,128)} %get-tuple-element.116), calls=%async_computation.1 | async-start | bytes 32768 | tf_op jit(solution)/shard_map/all_to_all | solution.py:1107
  48.5 4.7 %cotangent.1.refs_8_ = bf16[2048,128]{1,0:T(8,128)(2,1)} custom-call(s32[5]{0:T(128)} %len_ref.11, f32[2,32768]{1,0:T(2,128)} %wave_next_ref.1, f32[2,32768]{1,0:T(2,128)} %wave_next_ref.1, f32[264,128]{1,0:T(8,128)} %collective-permute-done.3.next_ref.edge_next_ref, f32[16,512]{1,0:T(8,128)} %get-tuple-element.118.after_ref.refs_10_.vec_ref), custom_call_target="tpu_custom_call" | custom-call | bytes 21600000 | tf_op jit(solution)/shard_map/cotangent/pallas_call | solution.py:1185
  53.2 2.1 %all-to-all-done.1.msg_in_ref = f32[32,1,128]{2,1,0:T(1,128)} async-done(((f32[32,1,128]{2,1,0:T(1,128)}), f32[32,1,128]{2,1,0:T(1,128)}, u32[]{:S(2)}, u32[]{:S(2)}) %all-to-all-start.1) | async-done | bytes 16416 | tf_op jit(solution)/shard_map/all_to_all | solution.py:1107
  55.2 30.7 %mask.1 = (f32[4096,128]{1,0:T(8,128)}, f32[4096,128]{1,0:T(8,128)}, f32[4096,512]{1,0:T(8,128)}, f32[2048,768]{1,0:T(8,128)}, f32[2,16384]{1,0:T(2,128)}, /*ind...) custom-call(s32[5]{0:T(128)} %len_ref.11, ...), custom_call_target="tpu_custom_call" | custom-call | bytes 100800000 | tf_op jit(solution)/shard_map/mask/pallas_call | solution.py:1198
  86.0 1.8 %collective-permute-done.10 = f32[584,128]{1,0:T(8,128)S(1)} collective-permute-done((f32[584,128]{1,0:T(8,128)}, f32[584,128]{1,0:T(8,128)S(1)}, u32[]{:S(2)}, u32[]{:S(2)}) %collective-permute-start.10) | collective-permute-done | bytes 299040 | tf_op jit(solution)/shard_map/ppermute | solution.py:1239
  89.1 4.1 %all-to-all-start.2 = ((f32[32,8,128]{2,1,0:T(8,128)}), f32[32,8,128]{2,1,0:T(8,128)S(1)}, u32[]{:S(2)}, u32[]{:S(2)}) async-start(f32[32,8,128]{2,1,0:T(8,128)} %get-tuple-element.120), calls=%async_computation.2 | async-start | bytes 262144 | tf_op jit(solution)/shard_map/all_to_all | solution.py:1107
  93.2 2.8 %collective-permute-start.8 = (f32[136,256]{1,0:T(8,128)}, f32[136,256]{1,0:T(8,128)}, u32[]{:S(2)}, u32[]{:S(2)}) collective-permute-start(f32[136,256]{1,0:T(8,128)} %get-tuple-element.121), channel_id=1, source_target_pairs={{0,1},{1,4},{2,3},{3,6},{4,5},{5,8},{6,7},{7,10},{8,9},{9,12},{10,... | collective-permute-start | bytes 417800 | tf_op jit(solution)/shard_map/ppermute | solution.py:1240
  97.5 2.4 %collective-permute-done.9.high_ref = f32[128,256]{1,0:T(8,128)S(1)} collective-permute-done((f32[128,256]{1,0:T(8,128)}, f32[128,256]{1,0:T(8,128)S(1)}, u32[]{:S(2)}, u32[]{:S(2)}) %collective-permute-start.9) | collective-permute-done | bytes 131104 | tf_op jit(solution)/shard_map/ppermute | solution.py:1241
  102.3 4.4 %collective-permute-start.13 = (f32[584,128]{1,0:T(8,128)}, f32[584,128]{1,0:T(8,128)}, u32[]{:S(2)}, u32[]{:S(2)}) collective-permute-start(f32[584,128]{1,0:T(8,128)} %add.16), channel_id=1, source_target_pairs={{0,16},{4,20},{8,24},{12,28},{16,0},{20,4},{24,8},{28,12},{1,17},{... | collective-permute-start | bytes 897032 | tf_op jit(solution)/shard_map/ppermute | solution.py:1251
  107.1 18.7 %back.1 = (f32[4096,128]{1,0:T(8,128)}, f32[2048,128]{1,0:T(8,128)}, f32[144,128]{1,0:T(8,128)}, f32[144,128]{1,0:T(8,128)}, f32[8,128]{1,0:T(8,128)}, /*index=5...) custom-call(s32[5]{0:T(128)} %len_ref.11, ...), custom_call_target="tpu_custom_call", output_to_operand_aliasing={{5}: (19, {}), {6}: (20, {}), {7}: (21, {})} | custom-call | bytes 46800000 | tf_op jit(solution)/shard_map/back/pallas_call | solution.py:1262
  125.9 1.9 %add.17.early_ref = f32[584,128]{1,0:T(8,128)} add(f32[584,128]{1,0:T(8,128)} %add.16, f32[584,128]{1,0:T(8,128)} %collective-permute-done.13) | non-fusion elementwise | flops 74752 | bytes 897024 | tf_op jit(solution)/shard_map/add | solution.py:1296
  132.9 2.3 %collective-permute-done.16 = f32[144,128]{1,0:T(8,128)S(1)} collective-permute-done((f32[144,128]{1,0:T(8,128)S(1)}, f32[144,128]{1,0:T(8,128)S(1)}, u32[]{:S(2)}, u32[]{:S(2)}) %collective-permute-start.16) | collective-permute-done | bytes 73760 | tf_op jit(solution)/shard_map/ppermute | solution.py:1304
  138.0 2.2 %collective-permute-start.19 = (f32[144,128]{1,0:T(8,128)}, f32[144,128]{1,0:T(8,128)}, u32[]{:S(2)}, u32[]{:S(2)}) collective-permute-start(f32[144,128]{1,0:T(8,128)} %add.19.refs_0_), channel_id=1, source_target_pairs={{0,8},{4,12},{8,0},{12,4},{16,24},{20,28},{24,16},{28,20},{1,9},{5... | collective-permute-start | bytes 221192 | tf_op jit(solution)/shard_map/ppermute | solution.py:1313
  140.2 3.1 %merge.1 = (f32[4096,128]{1,0:T(8,128)}, f32[2,32768]{1,0:T(2,128)}) custom-call(s32[5]{0:T(128)} %len_ref.11, f32[2048,128]{1,0:T(8,128)} %collective-permute-done.17.got_ref, f32[4096,128]{1,0:T(8,128)} %get-tuple-element.165.mix_in, f32[2,16384]{1,0:T(2,128)} %get-tuple-element.149.mine_ref, ...), custom_call_target="tpu_custom_call", output_to_operand_aliasing={{0}: (2, {})} | custom-call | bytes 10800000 | tf_op jit(solution)/shard_map/merge/pallas_call | solution.py:1316
  143.3 1.8 %collective-permute-done.20.refs_2_ = f32[144,128]{1,0:T(8,128)} collective-permute-done((f32[144,128]{1,0:T(8,128)}, f32[144,128]{1,0:T(8,128)}, u32[]{:S(2)}, u32[]{:S(2)}) %collective-permute-start.20) | collective-permute-done | bytes 73760 | tf_op jit(solution)/shard_map/ppermute | solution.py:1313
  145.1 1.9 %last.1 = (f32[128,128]{1,0:T(8,128)}, f32[1,128]{1,0:T(1,128)}, f32[1,128]{1,0:T(1,128)}, f32[1,128]{1,0:T(1,128)}, f32[1,128]{1,0:T(1,128)}, /*index=5*/f32[3,...) custom-call(f32[584,128]{1,0:T(8,128)} %add.17.early_ref, ...), custom_call_target="tpu_custom_call" | custom-call | tf_op jit(solution)/shard_map/last/pallas_call | solution.py:1332
  (47 shorter events, 15.8 us)
Async XLA Ops:
  2.7 21.6 %collective-permute-start.6 = (f32[512,128]{1,0:T(8,128)}, f32[512,128]{1,0:T(8,128)}, u32[]{:S(2)}, u32[]{:S(2)}) collective-permute-start(f32[512,128]{1,0:T(8,128)} %get-tuple-element.119.refs_13_), channel_id=1, source_target_pairs={{0,2},{1,3},{2,0},{3,1},{4,6},{5,7},{6,4},{7,5},{8,10},{9,11},{10,... | collective-permute-start | bytes 786440 | tf_op jit(solution)/shard_map/ppermute | solution.py:1148
  5.7 12.5 %collective-permute-start.3 = (f32[264,128]{1,0:T(8,128)}, f32[264,128]{1,0:T(8,128)}, u32[]{:S(2)}, u32[]{:S(2)}) collective-permute-start(f32[264,128]{1,0:T(8,128)} %get-tuple-element.110), channel_id=1, source_target_pairs={{4,0},{8,4},{12,8},{16,12},{20,16},{24,20},{28,24},{5,1},{9,5},{13... | collective-permute-start | bytes 405512 | tf_op jit(solution)/shard_map/ppermute | solution.py:1135
  6.9 11.2 %collective-permute-start.2 = (f32[256,128]{1,0:T(8,128)}, f32[256,128]{1,0:T(8,128)}, u32[]{:S(2)}, u32[]{:S(2)}) collective-permute-start(f32[256,128]{1,0:T(8,128)} %get-tuple-element.109), channel_id=1, source_target_pairs={{0,4},{4,8},{8,12},{12,16},{16,20},{20,24},{24,28},{1,5},{5,9},{9,... | collective-permute-start | bytes 393224 | tf_op jit(solution)/shard_map/ppermute | solution.py:1134
  12.1 6.0 %collective-permute-start.1 = (f32[144,128]{1,0:T(8,128)}, f32[144,128]{1,0:T(8,128)}, u32[]{:S(2)}, u32[]{:S(2)}) collective-permute-start(f32[144,128]{1,0:T(8,128)} %get-tuple-element.108.own_ref), channel_id=1, source_target_pairs={{0,1},{1,0},{2,3},{3,2},{4,5},{5,4},{6,7},{7,6},{8,9},{9,8},{10,11... | collective-permute-start | bytes 221192 | tf_op jit(solution)/shard_map/ppermute | solution.py:1133
  12.1 6.0 %collective-permute-start = (f32[144,128]{1,0:T(8,128)}, f32[144,128]{1,0:T(8,128)}, u32[]{:S(2)}, u32[]{:S(2)}) collective-permute-start(f32[144,128]{1,0:T(8,128)} %get-tuple-element.108.own_ref), channel_id=1, source_target_pairs={{0,2},{1,3},{2,0},{3,1},{4,6},{5,7},{6,4},{7,5},{8,10},{9,11},{10,... | collective-permute-start | bytes 221192 | tf_op jit(solution)/shard_map/ppermute | solution.py:1132
  18.2 14.1 %all-to-all-start = ((f32[32,8,128]{2,1,0:T(8,128)}), f32[32,8,128]{2,1,0:T(8,128)}, u32[]{:S(2)}, u32[]{:S(2)}) async-start(f32[32,8,128]{2,1,0:T(8,128)} %first.1), calls=%async_computation | async-start | bytes 262144 | tf_op jit(solution)/shard_map/all_to_all | solution.py:1107
  24.1 29.1 %collective-permute-start.5 = (f32[512,128]{1,0:T(8,128)}, f32[512,128]{1,0:T(8,128)}, u32[]{:S(2)}, u32[]{:S(2)}) collective-permute-start(f32[512,128]{1,0:T(8,128)} %get-tuple-element.119.refs_13_), channel_id=1, source_target_pairs={{0,1},{1,0},{2,3},{3,2},{4,5},{5,4},{6,7},{7,6},{8,9},{9,8},{10,11... | collective-permute-start | bytes 786440 | tf_op jit(solution)/shard_map/ppermute | solution.py:1149
  24.3 30.9 %collective-permute-start.7 = (f32[512,128]{1,0:T(8,128)}, f32[512,128]{1,0:T(8,128)}, u32[]{:S(2)}, u32[]{:S(2)}) collective-permute-start(f32[512,128]{1,0:T(8,128)} %collective-permute-done.6.refs_15_), channel_id=1, source_target_pairs={{0,1},{1,0},{2,3},{3,2},{4,5},{5,4},{6,7},{7,6},{8,9},{9,8},{10,11... | collective-permute-start | bytes 786440 | tf_op jit(solution)/shard_map/ppermute | solution.py:1150
  45.0 10.2 %all-to-all-start.1 = ((f32[32,1,128]{2,1,0:T(1,128)}), f32[32,1,128]{2,1,0:T(1,128)}, u32[]{:S(2)}, u32[]{:S(2)}) async-start(f32[32,1,128]{2,1,0:T(1,128)} %get-tuple-element.116), calls=%async_computation.1 | async-start | bytes 32768 | tf_op jit(solution)/shard_map/all_to_all | solution.py:1107
  85.9 1.9 %collective-permute-start.10 = (f32[584,128]{1,0:T(8,128)}, f32[584,128]{1,0:T(8,128)S(1)}, u32[]{:S(2)}, u32[]{:S(2)}) collective-permute-start(f32[584,128]{1,0:T(8,128)} %get-tuple-element.124), channel_id=1, source_target_pairs={{0,1},{1,0},{2,3},{3,2},{4,5},{5,4},{6,7},{7,6},{8,9},{9,8},{10,11... | collective-permute-start | bytes 897032 | tf_op jit(solution)/shard_map/ppermute | solution.py:1239
  88.8 12.7 %collective-permute-start.12 = (f32[2048,768]{1,0:T(8,128)}, f32[2048,768]{1,0:T(8,128)}, u32[]{:S(2)}, u32[]{:S(2)}) collective-permute-start(f32[2048,768]{1,0:T(8,128)} %get-tuple-element.127), channel_id=1, source_target_pairs={{0,1},{1,0},{2,3},{3,2},{4,5},{5,4},{6,7},{7,6},{8,9},{9,8},{10,11... | collective-permute-start | bytes 18874376 | tf_op jit(solution)/shard_map/ppermute | solution.py:1245
  89.0 12.5 %collective-permute-start.11 = (f32[584,128]{1,0:T(8,128)S(1)}, f32[584,128]{1,0:T(8,128)S(1)}, u32[]{:S(2)}, u32[]{:S(2)}) collective-permute-start(f32[584,128]{1,0:T(8,128)S(1)} %add.15), channel_id=1, source_target_pairs={{0,4},{4,0},{8,12},{12,8},{16,20},{20,16},{24,28},{28,24},{1,5},{5... | collective-permute-start | bytes 897032 | tf_op jit(solution)/shard_map/ppermute | solution.py:1244
  89.1 12.3 %all-to-all-start.2 = ((f32[32,8,128]{2,1,0:T(8,128)}), f32[32,8,128]{2,1,0:T(8,128)S(1)}, u32[]{:S(2)}, u32[]{:S(2)}) async-start(f32[32,8,128]{2,1,0:T(8,128)} %get-tuple-element.120), calls=%async_computation.2 | async-start | bytes 262144 | tf_op jit(solution)/shard_map/all_to_all | solution.py:1107
  93.2 7.4 %collective-permute-start.8 = (f32[136,256]{1,0:T(8,128)}, f32[136,256]{1,0:T(8,128)}, u32[]{:S(2)}, u32[]{:S(2)}) collective-permute-start(f32[136,256]{1,0:T(8,128)} %get-tuple-element.121), channel_id=1, source_target_pairs={{0,1},{1,4},{2,3},{3,6},{4,5},{5,8},{6,7},{7,10},{8,9},{9,12},{10,... | collective-permute-start | bytes 417800 | tf_op jit(solution)/shard_map/ppermute | solution.py:1240
  96.0 3.9 %collective-permute-start.9 = (f32[128,256]{1,0:T(8,128)}, f32[128,256]{1,0:T(8,128)S(1)}, u32[]{:S(2)}, u32[]{:S(2)}) collective-permute-start(f32[128,256]{1,0:T(8,128)} %get-tuple-element.122), channel_id=1, source_target_pairs={{1,0},{4,1},{3,2},{6,3},{5,4},{8,5},{7,6},{10,7},{9,8},{12,9},{11,... | collective-permute-start | bytes 393224 | tf_op jit(solution)/shard_map/ppermute | solution.py:1241
  102.3 23.6 %collective-permute-start.13 = (f32[584,128]{1,0:T(8,128)}, f32[584,128]{1,0:T(8,128)}, u32[]{:S(2)}, u32[]{:S(2)}) collective-permute-start(f32[584,128]{1,0:T(8,128)} %add.16), channel_id=1, source_target_pairs={{0,16},{4,20},{8,24},{12,28},{16,0},{20,4},{24,8},{28,12},{1,17},{... | collective-permute-start | bytes 897032 | tf_op jit(solution)/shard_map/ppermute | solution.py:1251
  106.7 19.1 %collective-permute-start.14 = (f32[2,16384]{1,0:T(2,128)}, f32[2,16384]{1,0:T(2,128)}, u32[]{:S(2)}, u32[]{:S(2)}) collective-permute-start(f32[2,16384]{1,0:T(2,128)} %get-tuple-element.149.mine_ref), channel_id=1, source_target_pairs={{0,1},{1,0},{2,3},{3,2},{4,5},{5,4},{6,7},{7,6},{8,9},{9,8},{10,11... | collective-permute-start | bytes 393224 | tf_op jit(solution)/shard_map/ppermute | solution.py:1249
  125.9 1.9 %collective-permute-start.15 = (f32[144,128]{1,0:T(8,128)}, f32[144,128]{1,0:T(8,128)S(1)}, u32[]{:S(2)}, u32[]{:S(2)}) collective-permute-start(f32[144,128]{1,0:T(8,128)} %get-tuple-element.151), channel_id=1, source_target_pairs={{0,1},{1,0},{2,3},{3,2},{4,5},{5,4},{6,7},{7,6},{8,9},{9,8},{10,11... | collective-permute-start | bytes 221192 | tf_op jit(solution)/shard_map/ppermute | solution.py:1295
  128.7 6.5 %collective-permute-start.17 = (f32[2048,128]{1,0:T(8,128)}, f32[2048,128]{1,0:T(8,128)}, u32[]{:S(2)}, u32[]{:S(2)}) collective-permute-start(f32[2048,128]{1,0:T(8,128)} %get-tuple-element.158), channel_id=1, source_target_pairs={{0,1},{1,0},{2,3},{3,2},{4,5},{5,4},{6,7},{7,6},{8,9},{9,8},{10,11... | collective-permute-start | bytes 3145736 | tf_op jit(solution)/shard_map/ppermute | solution.py:1305
  129.3 15.9 %collective-permute-start.22 = (f32[584,128]{1,0:T(8,128)}, f32[584,128]{1,0:T(8,128)}, u32[]{:S(2)}, u32[]{:S(2)}) collective-permute-start(f32[584,128]{1,0:T(8,128)} %add.17.early_ref), channel_id=1, source_target_pairs={{0,8},{4,12},{8,0},{12,4},{16,24},{20,28},{24,16},{28,20},{1,9},{5... | collective-permute-start | bytes 897032 | tf_op jit(solution)/shard_map/ppermute | solution.py:1298
  130.9 4.4 %collective-permute-start.16 = (f32[144,128]{1,0:T(8,128)S(1)}, f32[144,128]{1,0:T(8,128)S(1)}, u32[]{:S(2)}, u32[]{:S(2)}) collective-permute-start(f32[144,128]{1,0:T(8,128)S(1)} %add.18), channel_id=1, source_target_pairs={{0,4},{4,0},{8,12},{12,8},{16,20},{20,16},{24,28},{28,24},{1,5},{5... | collective-permute-start | bytes 221192 | tf_op jit(solution)/shard_map/ppermute | solution.py:1304
  135.8 7.5 %collective-permute-start.21 = (f32[144,128]{1,0:T(8,128)}, f32[144,128]{1,0:T(8,128)}, u32[]{:S(2)}, u32[]{:S(2)}) collective-permute-start(f32[144,128]{1,0:T(8,128)} %add.19.refs_0_), channel_id=1, source_target_pairs={{0,24},{4,28},{8,16},{12,20},{16,8},{20,12},{24,0},{28,4},{1,25},{... | collective-permute-start | bytes 221192 | tf_op jit(solution)/shard_map/ppermute | solution.py:1313
  136.6 8.5 %collective-permute-start.20 = (f32[144,128]{1,0:T(8,128)}, f32[144,128]{1,0:T(8,128)}, u32[]{:S(2)}, u32[]{:S(2)}) collective-permute-start(f32[144,128]{1,0:T(8,128)} %add.19.refs_0_), channel_id=1, source_target_pairs={{0,16},{4,20},{8,24},{12,28},{16,0},{20,4},{24,8},{28,12},{1,17},{... | collective-permute-start | bytes 221192 | tf_op jit(solution)/shard_map/ppermute | solution.py:1313
  138.0 7.1 %collective-permute-start.19 = (f32[144,128]{1,0:T(8,128)}, f32[144,128]{1,0:T(8,128)}, u32[]{:S(2)}, u32[]{:S(2)}) collective-permute-start(f32[144,128]{1,0:T(8,128)} %add.19.refs_0_), channel_id=1, source_target_pairs={{0,8},{4,12},{8,0},{12,4},{16,24},{20,28},{24,16},{28,20},{1,9},{5... | collective-permute-start | bytes 221192 | tf_op jit(solution)/shard_map/ppermute | solution.py:1313
  (5 other events, 7.0 us)

commit v6 on v5

--- a/solution.py
+++ b/solution.py
@@ -1241,13 +1241,11 @@
     got_high = lax.ppermute(r_down, both, earlier)
     msg3 = exchange(msg3)
     early, send = lax.optimization_barrier((early, send))
-    early_other = lax.ppermute(early, "tm", hops[0])
     got = lax.ppermute(send, "src", swap)
-    msg3, got_low, got_high, early, early_other, got, wave_half = lax.optimization_barrier(
-        (msg3, got_low, got_high, early, early_other, got, wave_half)
+    msg3, got_low, got_high, early, got, wave_half = lax.optimization_barrier(
+        (msg3, got_low, got_high, early, got, wave_half)
     )
     wave_other = lax.ppermute(wave_half, "src", swap)
-    early = early + early_other
     early_other = lax.ppermute(early, "tm", hops[-1])
 
     def rows(width):
@@ -1294,25 +1292,14 @@
     )
     late_give = lax.ppermute(give, "src", swap)
     early = early + early_other
-    for hop in hops[1:-1]:
-        early_other = lax.ppermute(early, "tm", hop)
-        if hop is not hops[-2]:
-            early = early + early_other
+    early_other = lax.ppermute(early, "tm", hops[0])
     late_give, early = lax.optimization_barrier((late_give, early))
     late = keep + late_give
     late, edge, mix_send = lax.optimization_barrier((late, edge, mix_send))
-    late_other = lax.ppermute(late, "tm", hops[0])
+    lates = [late] + [lax.ppermute(late, "tm", [(i, i ^ (2 * k)) for i in range(n_tm)]) for k in range(1, n_tm // 2)]
     mix_got = lax.ppermute(mix_send, "src", swap)
     edge_other = lax.ppermute(edge, "src", swap)
-    late, late_other, early, mix_got, edge_other = lax.optimization_barrier(
-        (late, late_other, early, mix_got, edge_other)
-    )
-    late = late + late_other
-    lates = [late]
-    for k in range(1, n_tm // 2):
-        lates.append(lax.ppermute(late, "tm", [(i, i ^ (2 * k)) for i in range(n_tm)]))
     wave_width = own_rows * STRIDE
-    late, mix_got, edge_other = lax.optimization_barrier((late, mix_got, edge_other))
     grad_mix, wave = call(
         merge_kernel, "merge", 1,
         [
@@ -1323,7 +1310,16 @@
         input_output_aliases={2: 0},
     )(lengths, mix_got, grad_mix, wave_half, wave_other, edge, edge_other)
     *lates, grad_mix, wave = lax.optimization_barrier((*lates, grad_mix, wave))
-
+    while len(lates) > 1:
+        lates = [a + b for a, b in zip(lates[0::2], lates[1::2])]
+    late = lates[0]
+    late_other = lax.ppermute(late, "tm", hops[0])
+    late, early, early_other = lax.optimization_barrier((late, early, early_other))
+    for hop in hops[1:-1]:
+        early = early + early_other
+        early_other = lax.ppermute(early, "tm", hop)
+
+    lates = [late, late_other]
     parts = (early, early_other, *lates)
     shapes = (
         (128, 128), (1, 128), (1, 128), (1, 128), (1, 128), (3, 128), (1, 128), (1, 128), (1, 128), (1, 128), (128, 256),

time: 148 us -> 158 us (1.068)
  waiting for transfers between devices: 20 us -> 26.9 us
  other arithmetic: 5.23 us -> 7.16 us
    ppermute x1, waiting for transfers between devices: 0.01 us -> 3.78 us  [local(): early_other = lax.ppermute(early, 'tm', hop)]
    ppermute x1, waiting for transfers between devices: 0.01 us -> 3.59 us  [local(): early_other = lax.ppermute(early, 'tm', hops[0])]
    ppermute x1, starting transfers between devices: 0.13 us -> 2.39 us  [local(): early_other = lax.ppermute(early, 'tm', hops[0])]
    ppermute x3, waiting for transfers between devices: 1.8 us -> 0.01 us  [local(): lax.ppermute(late, 'tm', [(i, i ^ 2 * k) for i in range(n_tm)])]
    ppermute x1, starting transfers between devices: 1.58 us -> 0.01 us  [local(): early_other = lax.ppermute(early, 'tm', hop)]
  transfers between devices with their start and end apart: 26 -> 26, of which waited for: 9 -> 10; matrix products, arithmetic and copies ran while one was open for 2% -> 2% of each run, Pallas kernels for 31% -> 29%
where the time goes in v6:
time: 158 us; the launch traced here: 157 us
  Pallas kernels  80 us (51%)
  starting transfers between devices  40.5 us (26%)
  waiting for transfers between devices  26.9 us (17%)
  other arithmetic  7.16 us (5%)
    pallas_call x1, Pallas kernels, local(): call(mask_kernel, 'mask', tiles_m, [whole(*stat_shape), *[depth_piece(k)...  30.7 us
    pallas_call x1, Pallas kernels, local(): call(back_kernel, 'back', tiles + 1, [whole(*msg_shape), rows(HIDDEN), pl...  18.7 us
    pallas_call x1, Pallas kernels, local(): call(depth_kernel, 'depth', tiles + 2, [whole(*msg_shape), whole(frames,...  12.8 us
    all_to_all x3, starting transfers between devices, exchange(): return lax.all_to_all(msg, ('tm', 'src'), 0, 0)  12.4 us
    all_to_all x3, waiting for transfers between devices, exchange(): return lax.all_to_all(msg, ('tm', 'src'), 0, 0)  9.24 us
    pallas_call x1, Pallas kernels, local(): call(first_kernel, 'first', 2, [pl.BlockSpec((frames // 2, 128), lambda i...  6.18 us
    ppermute x1, starting transfers between devices, local(): mix_prev = lax.ppermute(high, 'tm', up)  5.21 us
    pallas_call x1, Pallas kernels, local(): call(cotangent_kernel, 'cotangent', tiles_m, [pl.BlockSpec((2, TM * STRID...  4.66 us
  transfers between devices with their start and end apart: 26, of which 10 were waited for; matrix products, arithmetic and copies ran while one was open for 2% of the time, Pallas kernels for 29%

profile of v6, /device:TPU:0, one launch (start us, length us, event | category | flops | bytes accessed | tf_op | source)
XLA Modules:
  0.0 156.9 jit_solution(10161161926989238969)
XLA Ops:
  0.7 2.0 %prep.1 = (f32[144,128]{1,0:T(8,128)}, f32[512,128]{1,0:T(8,128)}, f32[264,128]{1,0:T(8,128)}, f32[256,128]{1,0:T(8,128)}) custom-call(f32[4096,128]{1,0:T(8,128)} %mix_ref.5, f32[4096,128]{1,0:T(8,128)} %mix_ref.5, f32[2,32768]{1,0:T(2,128)} %wave_next_ref.1, f32[128,128]{1,0:T(8,128)} %w_in_ref.3, f32[128,256]{1,0:T(8,128)} %w_out_ref.1, ...), custom_call_target="tpu_custom_call" | custom-call | tf_op jit(solution)/shard_map/prep/pallas_call | solution.py:1120
  2.7 2.9 %collective-permute-start.6 = (f32[512,128]{1,0:T(8,128)}, f32[512,128]{1,0:T(8,128)}, u32[]{:S(2)}, u32[]{:S(2)}) collective-permute-start(f32[512,128]{1,0:T(8,128)} %get-tuple-element.114.refs_13_), channel_id=1, source_target_pairs={{0,2},{1,3},{2,0},{3,1},{4,6},{5,7},{6,4},{7,5},{8,10},{9,11},{10,... | collective-permute-start | bytes 786440 | tf_op jit(solution)/shard_map/ppermute | solution.py:1148
  6.9 5.2 %collective-permute-start.2 = (f32[256,128]{1,0:T(8,128)}, f32[256,128]{1,0:T(8,128)}, u32[]{:S(2)}, u32[]{:S(2)}) collective-permute-start(f32[256,128]{1,0:T(8,128)} %get-tuple-element.104), channel_id=1, source_target_pairs={{0,4},{4,8},{8,12},{12,16},{16,20},{20,24},{24,28},{1,5},{5,9},{9,... | collective-permute-start | bytes 393224 | tf_op jit(solution)/shard_map/ppermute | solution.py:1134
  12.2 6.2 %first.1 = f32[32,8,128]{2,1,0:T(8,128)} custom-call(s32[5]{0:T(128)} %len_ref.11, f32[4096,128]{1,0:T(8,128)} %mix_ref.5, f32[128,128]{1,0:T(8,128)} %w_in_ref.3, f32[1,128]{1,0:T(1,128)} %bitcast.26, f32[1,128]{1,0:T(1,128)} %bitcast.28), custom_call_target="tpu_custom_call" | custom-call | bytes 14400000 | tf_op jit(solution)/shard_map/first/pallas_call | solution.py:1136
  18.4 5.4 %all-to-all-start = ((f32[32,8,128]{2,1,0:T(8,128)}), f32[32,8,128]{2,1,0:T(8,128)}, u32[]{:S(2)}, u32[]{:S(2)}) async-start(f32[32,8,128]{2,1,0:T(8,128)} %first.1), calls=%async_computation | async-start | bytes 262144 | tf_op jit(solution)/shard_map/all_to_all | solution.py:1107
  26.3 5.8 %all-to-all-done.msg_in_ref = f32[32,8,128]{2,1,0:T(8,128)} async-done(((f32[32,8,128]{2,1,0:T(8,128)}), f32[32,8,128]{2,1,0:T(8,128)}, u32[]{:S(2)}, u32[]{:S(2)}) %all-to-all-start) | async-done | bytes 131104 | tf_op jit(solution)/shard_map/all_to_all | solution.py:1107
  32.0 12.8 %depth.1 = (f32[2560,512]{1,0:T(8,128)}, f32[2304,512]{1,0:T(8,128)}, f32[32,1,128]{2,1,0:T(1,128)}, f32[16,512]{1,0:T(8,128)}, f32[2,8,128]{2,1,0:T(8,128)}) custom-call(s32[5]{0:T(128)} %len_ref.11, f32[32,8,128]{2,1,0:T(8,128)} %all-to-all-done.msg_in_ref, f32[4096,128]{1,0:T(8,128)} %mix_ref.5, f32[256,128]{1,0:T(8,128)} %collective-permute-done.2.prev_ref, ...), custom_call_target="tpu_custom_call" | custom-call | bytes 28800000 | tf_op jit(solution)/shard_map/depth/pallas_call | solution.py:1154
  44.8 3.4 %all-to-all-start.1 = ((f32[32,1,128]{2,1,0:T(1,128)}), f32[32,1,128]{2,1,0:T(1,128)}, u32[]{:S(2)}, u32[]{:S(2)}) async-start(f32[32,1,128]{2,1,0:T(1,128)} %get-tuple-element.111), calls=%async_computation.1 | async-start | bytes 32768 | tf_op jit(solution)/shard_map/all_to_all | solution.py:1107
  48.2 4.7 %cotangent.1.refs_8_ = bf16[2048,128]{1,0:T(8,128)(2,1)} custom-call(s32[5]{0:T(128)} %len_ref.11, f32[2,32768]{1,0:T(2,128)} %wave_next_ref.1, f32[2,32768]{1,0:T(2,128)} %wave_next_ref.1, f32[264,128]{1,0:T(8,128)} %collective-permute-done.3.next_ref.edge_next_ref, f32[16,512]{1,0:T(8,128)} %get-tuple-element.113.after_ref.refs_10_.vec_ref), custom_call_target="tpu_custom_call" | custom-call | bytes 21600000 | tf_op jit(solution)/shard_map/cotangent/pallas_call | solution.py:1185
  52.9 2.2 %all-to-all-done.1.msg_in_ref = f32[32,1,128]{2,1,0:T(1,128)} async-done(((f32[32,1,128]{2,1,0:T(1,128)}), f32[32,1,128]{2,1,0:T(1,128)}, u32[]{:S(2)}, u32[]{:S(2)}) %all-to-all-start.1) | async-done | bytes 16416 | tf_op jit(solution)/shard_map/all_to_all | solution.py:1107
  55.1 30.7 %mask.1 = (f32[4096,128]{1,0:T(8,128)}, f32[4096,128]{1,0:T(8,128)}, f32[4096,512]{1,0:T(8,128)}, f32[2048,768]{1,0:T(8,128)}, f32[2,16384]{1,0:T(2,128)}, /*ind...) custom-call(s32[5]{0:T(128)} %len_ref.11, ...), custom_call_target="tpu_custom_call" | custom-call | bytes 100800000 | tf_op jit(solution)/shard_map/mask/pallas_call | solution.py:1198
  85.9 1.8 %collective-permute-done.10 = f32[584,128]{1,0:T(8,128)S(1)} collective-permute-done((f32[584,128]{1,0:T(8,128)}, f32[584,128]{1,0:T(8,128)S(1)}, u32[]{:S(2)}, u32[]{:S(2)}) %collective-permute-start.10) | collective-permute-done | bytes 299040 | tf_op jit(solution)/shard_map/ppermute | solution.py:1239
  89.5 3.6 %all-to-all-start.2 = ((f32[32,8,128]{2,1,0:T(8,128)}), f32[32,8,128]{2,1,0:T(8,128)}, u32[]{:S(2)}, u32[]{:S(2)}) async-start(f32[32,8,128]{2,1,0:T(8,128)} %get-tuple-element.115), calls=%async_computation.2 | async-start | bytes 262144 | tf_op jit(solution)/shard_map/all_to_all | solution.py:1107
  93.1 2.7 %collective-permute-start.8 = (f32[136,256]{1,0:T(8,128)}, f32[136,256]{1,0:T(8,128)}, u32[]{:S(2)}, u32[]{:S(2)}) collective-permute-start(f32[136,256]{1,0:T(8,128)} %get-tuple-element.116), channel_id=1, source_target_pairs={{0,1},{1,4},{2,3},{3,6},{4,5},{5,8},{6,7},{7,10},{8,9},{9,12},{10,... | collective-permute-start | bytes 417800 | tf_op jit(solution)/shard_map/ppermute | solution.py:1240
  97.4 2.7 %collective-permute-done.9.high_ref = f32[128,256]{1,0:T(8,128)} collective-permute-done((f32[128,256]{1,0:T(8,128)}, f32[128,256]{1,0:T(8,128)}, u32[]{:S(2)}, u32[]{:S(2)}) %collective-permute-start.9) | collective-permute-done | bytes 131104 | tf_op jit(solution)/shard_map/ppermute | solution.py:1241
  101.4 3.8 %collective-permute-start.12 = (f32[584,128]{1,0:T(8,128)}, f32[584,128]{1,0:T(8,128)}, u32[]{:S(2)}, u32[]{:S(2)}) collective-permute-start(f32[584,128]{1,0:T(8,128)} %add.21), channel_id=1, source_target_pairs={{0,16},{4,20},{8,24},{12,28},{16,0},{20,4},{24,8},{28,12},{1,17},{... | collective-permute-start | bytes 897032 | tf_op jit(solution)/shard_map/ppermute | solution.py:1249
  105.7 18.7 %back.1 = (f32[4096,128]{1,0:T(8,128)}, f32[2048,128]{1,0:T(8,128)}, f32[144,128]{1,0:T(8,128)}, f32[144,128]{1,0:T(8,128)}, f32[8,128]{1,0:T(8,128)}, /*index=5...) custom-call(s32[5]{0:T(128)} %len_ref.11, ...), custom_call_target="tpu_custom_call", output_to_operand_aliasing={{5}: (19, {}), {6}: (20, {}), {7}: (21, {})} | custom-call | bytes 46800000 | tf_op jit(solution)/shard_map/back/pallas_call | solution.py:1260
  124.5 1.8 %add.22 = f32[584,128]{1,0:T(8,128)} add(f32[584,128]{1,0:T(8,128)} %add.21, f32[584,128]{1,0:T(8,128)} %collective-permute-done.12) | non-fusion elementwise | flops 74752 | bytes 897024 | tf_op jit(solution)/shard_map/add | solution.py:1294
  134.2 2.4 %collective-permute-start.20 = (f32[584,128]{1,0:T(8,128)}, f32[584,128]{1,0:T(8,128)}, u32[]{:S(2)}, u32[]{:S(2)}) collective-permute-start(f32[584,128]{1,0:T(8,128)} %add.22), channel_id=1, source_target_pairs={{0,4},{4,0},{8,12},{12,8},{16,20},{20,16},{24,28},{28,24},{1,5},{5... | collective-permute-start | bytes 897032 | tf_op jit(solution)/shard_map/ppermute | solution.py:1295
  136.6 3.1 %merge.1 = (f32[4096,128]{1,0:T(8,128)}, f32[2,32768]{1,0:T(2,128)}) custom-call(s32[5]{0:T(128)} %len_ref.11, f32[2048,128]{1,0:T(8,128)} %collective-permute-done.18.got_ref, f32[4096,128]{1,0:T(8,128)} %get-tuple-element.152.mix_in, f32[2,16384]{1,0:T(2,128)} %get-tuple-element.143.mine_ref, ...), custom_call_target="tpu_custom_call", output_to_operand_aliasing={{0}: (2, {})} | custom-call | bytes 10800000 | tf_op jit(solution)/shard_map/merge/pallas_call | solution.py:1303
  140.7 3.6 %collective-permute-done.20 = f32[584,128]{1,0:T(8,128)} collective-permute-done((f32[584,128]{1,0:T(8,128)}, f32[584,128]{1,0:T(8,128)}, u32[]{:S(2)}, u32[]{:S(2)}) %collective-permute-start.20) | collective-permute-done | bytes 299040 | tf_op jit(solution)/shard_map/ppermute | solution.py:1295
  147.9 2.6 %collective-permute-done.22.refs_1_ = f32[144,128]{1,0:T(8,128)S(1)} collective-permute-done((f32[144,128]{1,0:T(8,128)S(1)}, f32[144,128]{1,0:T(8,128)S(1)}, u32[]{:S(2)}, u32[]{:S(2)}) %collective-permute-start.22) | collective-permute-done | bytes 73760 | tf_op jit(solution)/shard_map/ppermute | solution.py:1316
  151.1 3.8 %collective-permute-done.21.early_other_ref = f32[584,128]{1,0:T(8,128)} collective-permute-done((f32[584,128]{1,0:T(8,128)S(1)}, f32[584,128]{1,0:T(8,128)}, u32[]{:S(2)}, u32[]{:S(2)}) %collective-permute-start.21) | collective-permute-done | bytes 299040 | tf_op jit(solution)/shard_map/ppermute | solution.py:1320
  154.9 1.9 %last.1 = (f32[128,128]{1,0:T(8,128)}, f32[1,128]{1,0:T(1,128)}, f32[1,128]{1,0:T(1,128)}, f32[1,128]{1,0:T(1,128)}, f32[1,128]{1,0:T(1,128)}, /*index=5*/f32[3,...) custom-call(f32[584,128]{1,0:T(8,128)} %copy-done, ...), custom_call_target="tpu_custom_call" | custom-call | tf_op jit(solution)/shard_map/last/pallas_call | solution.py:1328
  (47 shorter events, 22.2 us)
Async XLA Ops:
  2.7 21.4 %collective-permute-start.6 = (f32[512,128]{1,0:T(8,128)}, f32[512,128]{1,0:T(8,128)}, u32[]{:S(2)}, u32[]{:S(2)}) collective-permute-start(f32[512,128]{1,0:T(8,128)} %get-tuple-element.114.refs_13_), channel_id=1, source_target_pairs={{0,2},{1,3},{2,0},{3,1},{4,6},{5,7},{6,4},{7,5},{8,10},{9,11},{10,... | collective-permute-start | bytes 786440 | tf_op jit(solution)/shard_map/ppermute | solution.py:1148
  5.7 12.7 %collective-permute-start.3 = (f32[264,128]{1,0:T(8,128)}, f32[264,128]{1,0:T(8,128)}, u32[]{:S(2)}, u32[]{:S(2)}) collective-permute-start(f32[264,128]{1,0:T(8,128)} %get-tuple-element.105), channel_id=1, source_target_pairs={{4,0},{8,4},{12,8},{16,12},{20,16},{24,20},{28,24},{5,1},{9,5},{13... | collective-permute-start | bytes 405512 | tf_op jit(solution)/shard_map/ppermute | solution.py:1135
  6.9 11.4 %collective-permute-start.2 = (f32[256,128]{1,0:T(8,128)}, f32[256,128]{1,0:T(8,128)}, u32[]{:S(2)}, u32[]{:S(2)}) collective-permute-start(f32[256,128]{1,0:T(8,128)} %get-tuple-element.104), channel_id=1, source_target_pairs={{0,4},{4,8},{8,12},{12,16},{16,20},{20,24},{24,28},{1,5},{5,9},{9,... | collective-permute-start | bytes 393224 | tf_op jit(solution)/shard_map/ppermute | solution.py:1134
  12.1 6.2 %collective-permute-start.1 = (f32[144,128]{1,0:T(8,128)}, f32[144,128]{1,0:T(8,128)}, u32[]{:S(2)}, u32[]{:S(2)}) collective-permute-start(f32[144,128]{1,0:T(8,128)} %get-tuple-element.103.own_ref), channel_id=1, source_target_pairs={{0,1},{1,0},{2,3},{3,2},{4,5},{5,4},{6,7},{7,6},{8,9},{9,8},{10,11... | collective-permute-start | bytes 221192 | tf_op jit(solution)/shard_map/ppermute | solution.py:1133
  12.1 6.2 %collective-permute-start = (f32[144,128]{1,0:T(8,128)}, f32[144,128]{1,0:T(8,128)}, u32[]{:S(2)}, u32[]{:S(2)}) collective-permute-start(f32[144,128]{1,0:T(8,128)} %get-tuple-element.103.own_ref), channel_id=1, source_target_pairs={{0,2},{1,3},{2,0},{3,1},{4,6},{5,7},{6,4},{7,5},{8,10},{9,11},{10,... | collective-permute-start | bytes 221192 | tf_op jit(solution)/shard_map/ppermute | solution.py:1132
  18.4 13.6 %all-to-all-start = ((f32[32,8,128]{2,1,0:T(8,128)}), f32[32,8,128]{2,1,0:T(8,128)}, u32[]{:S(2)}, u32[]{:S(2)}) async-start(f32[32,8,128]{2,1,0:T(8,128)} %first.1), calls=%async_computation | async-start | bytes 262144 | tf_op jit(solution)/shard_map/all_to_all | solution.py:1107
  23.8 29.1 %collective-permute-start.5 = (f32[512,128]{1,0:T(8,128)}, f32[512,128]{1,0:T(8,128)}, u32[]{:S(2)}, u32[]{:S(2)}) collective-permute-start(f32[512,128]{1,0:T(8,128)} %get-tuple-element.114.refs_13_), channel_id=1, source_target_pairs={{0,1},{1,0},{2,3},{3,2},{4,5},{5,4},{6,7},{7,6},{8,9},{9,8},{10,11... | collective-permute-start | bytes 786440 | tf_op jit(solution)/shard_map/ppermute | solution.py:1149
  24.1 31.0 %collective-permute-start.7 = (f32[512,128]{1,0:T(8,128)}, f32[512,128]{1,0:T(8,128)}, u32[]{:S(2)}, u32[]{:S(2)}) collective-permute-start(f32[512,128]{1,0:T(8,128)} %collective-permute-done.6.refs_15_), channel_id=1, source_target_pairs={{0,1},{1,0},{2,3},{3,2},{4,5},{5,4},{6,7},{7,6},{8,9},{9,8},{10,11... | collective-permute-start | bytes 786440 | tf_op jit(solution)/shard_map/ppermute | solution.py:1150
  44.8 10.3 %all-to-all-start.1 = ((f32[32,1,128]{2,1,0:T(1,128)}), f32[32,1,128]{2,1,0:T(1,128)}, u32[]{:S(2)}, u32[]{:S(2)}) async-start(f32[32,1,128]{2,1,0:T(1,128)} %get-tuple-element.111), calls=%async_computation.1 | async-start | bytes 32768 | tf_op jit(solution)/shard_map/all_to_all | solution.py:1107
  85.8 1.9 %collective-permute-start.10 = (f32[584,128]{1,0:T(8,128)}, f32[584,128]{1,0:T(8,128)S(1)}, u32[]{:S(2)}, u32[]{:S(2)}) collective-permute-start(f32[584,128]{1,0:T(8,128)} %get-tuple-element.119), channel_id=1, source_target_pairs={{0,1},{1,0},{2,3},{3,2},{4,5},{5,4},{6,7},{7,6},{8,9},{9,8},{10,11... | collective-permute-start | bytes 897032 | tf_op jit(solution)/shard_map/ppermute | solution.py:1239
  89.4 12.0 %collective-permute-start.11 = (f32[2048,768]{1,0:T(8,128)}, f32[2048,768]{1,0:T(8,128)}, u32[]{:S(2)}, u32[]{:S(2)}) collective-permute-start(f32[2048,768]{1,0:T(8,128)} %get-tuple-element.122), channel_id=1, source_target_pairs={{0,1},{1,0},{2,3},{3,2},{4,5},{5,4},{6,7},{7,6},{8,9},{9,8},{10,11... | collective-permute-start | bytes 18874376 | tf_op jit(solution)/shard_map/ppermute | solution.py:1244
  89.5 11.8 %all-to-all-start.2 = ((f32[32,8,128]{2,1,0:T(8,128)}), f32[32,8,128]{2,1,0:T(8,128)}, u32[]{:S(2)}, u32[]{:S(2)}) async-start(f32[32,8,128]{2,1,0:T(8,128)} %get-tuple-element.115), calls=%async_computation.2 | async-start | bytes 262144 | tf_op jit(solution)/shard_map/all_to_all | solution.py:1107
  93.1 7.0 %collective-permute-start.8 = (f32[136,256]{1,0:T(8,128)}, f32[136,256]{1,0:T(8,128)}, u32[]{:S(2)}, u32[]{:S(2)}) collective-permute-start(f32[136,256]{1,0:T(8,128)} %get-tuple-element.116), channel_id=1, source_target_pairs={{0,1},{1,4},{2,3},{3,6},{4,5},{5,8},{6,7},{7,10},{8,9},{9,12},{10,... | collective-permute-start | bytes 417800 | tf_op jit(solution)/shard_map/ppermute | solution.py:1240
  95.9 4.2 %collective-permute-start.9 = (f32[128,256]{1,0:T(8,128)}, f32[128,256]{1,0:T(8,128)}, u32[]{:S(2)}, u32[]{:S(2)}) collective-permute-start(f32[128,256]{1,0:T(8,128)} %get-tuple-element.117), channel_id=1, source_target_pairs={{1,0},{4,1},{3,2},{6,3},{5,4},{8,5},{7,6},{10,7},{9,8},{12,9},{11,... | collective-permute-start | bytes 393224 | tf_op jit(solution)/shard_map/ppermute | solution.py:1241
  101.4 23.0 %collective-permute-start.12 = (f32[584,128]{1,0:T(8,128)}, f32[584,128]{1,0:T(8,128)}, u32[]{:S(2)}, u32[]{:S(2)}) collective-permute-start(f32[584,128]{1,0:T(8,128)} %add.21), channel_id=1, source_target_pairs={{0,16},{4,20},{8,24},{12,28},{16,0},{20,4},{24,8},{28,12},{1,17},{... | collective-permute-start | bytes 897032 | tf_op jit(solution)/shard_map/ppermute | solution.py:1249
  105.1 19.2 %collective-permute-start.13 = (f32[2,16384]{1,0:T(2,128)}, f32[2,16384]{1,0:T(2,128)}, u32[]{:S(2)}, u32[]{:S(2)}) collective-permute-start(f32[2,16384]{1,0:T(2,128)} %get-tuple-element.143.mine_ref), channel_id=1, source_target_pairs={{0,1},{1,0},{2,3},{3,2},{4,5},{5,4},{6,7},{7,6},{8,9},{9,8},{10,11... | collective-permute-start | bytes 393224 | tf_op jit(solution)/shard_map/ppermute | solution.py:1248
  124.4 1.9 %collective-permute-start.14 = (f32[144,128]{1,0:T(8,128)}, f32[144,128]{1,0:T(8,128)S(1)}, u32[]{:S(2)}, u32[]{:S(2)}) collective-permute-start(f32[144,128]{1,0:T(8,128)} %get-tuple-element.145), channel_id=1, source_target_pairs={{0,1},{1,0},{2,3},{3,2},{4,5},{5,4},{6,7},{7,6},{8,9},{9,8},{10,11... | collective-permute-start | bytes 221192 | tf_op jit(solution)/shard_map/ppermute | solution.py:1293
  127.8 8.8 %collective-permute-start.18 = (f32[2048,128]{1,0:T(8,128)}, f32[2048,128]{1,0:T(8,128)}, u32[]{:S(2)}, u32[]{:S(2)}) collective-permute-start(f32[2048,128]{1,0:T(8,128)} %get-tuple-element.151), channel_id=1, source_target_pairs={{0,1},{1,0},{2,3},{3,2},{4,5},{5,4},{6,7},{7,6},{8,9},{9,8},{10,11... | collective-permute-start | bytes 3145736 | tf_op jit(solution)/shard_map/ppermute | solution.py:1300
  128.3 11.4 %collective-permute-start.17 = (f32[144,128]{1,0:T(8,128)}, f32[144,128]{1,0:T(8,128)}, u32[]{:S(2)}, u32[]{:S(2)}) collective-permute-start(f32[144,128]{1,0:T(8,128)} %add.23), channel_id=1, source_target_pairs={{0,24},{4,28},{8,16},{12,20},{16,8},{20,12},{24,0},{28,4},{1,25},{... | collective-permute-start | bytes 221192 | tf_op jit(solution)/shard_map/ppermute | solution.py:1299
  129.8 9.9 %collective-permute-start.16 = (f32[144,128]{1,0:T(8,128)}, f32[144,128]{1,0:T(8,128)}, u32[]{:S(2)}, u32[]{:S(2)}) collective-permute-start(f32[144,128]{1,0:T(8,128)} %add.23), channel_id=1, source_target_pairs={{0,16},{4,20},{8,24},{12,28},{16,0},{20,4},{24,8},{28,12},{1,17},{... | collective-permute-start | bytes 221192 | tf_op jit(solution)/shard_map/ppermute | solution.py:1299
  131.2 8.5 %collective-permute-start.15 = (f32[144,128]{1,0:T(8,128)}, f32[144,128]{1,0:T(8,128)}, u32[]{:S(2)}, u32[]{:S(2)}) collective-permute-start(f32[144,128]{1,0:T(8,128)} %add.23), channel_id=1, source_target_pairs={{0,8},{4,12},{8,0},{12,4},{16,24},{20,28},{24,16},{28,20},{1,9},{5... | collective-permute-start | bytes 221192 | tf_op jit(solution)/shard_map/ppermute | solution.py:1299
  134.2 10.1 %collective-permute-start.20 = (f32[584,128]{1,0:T(8,128)}, f32[584,128]{1,0:T(8,128)}, u32[]{:S(2)}, u32[]{:S(2)}) collective-permute-start(f32[584,128]{1,0:T(8,128)} %add.22), channel_id=1, source_target_pairs={{0,4},{4,0},{8,12},{12,8},{16,20},{20,16},{24,28},{28,24},{1,5},{5... | collective-permute-start | bytes 897032 | tf_op jit(solution)/shard_map/ppermute | solution.py:1295
  146.1 8.8 %collective-permute-start.21 = (f32[584,128]{1,0:T(8,128)S(1)}, f32[584,128]{1,0:T(8,128)}, u32[]{:S(2)}, u32[]{:S(2)}) collective-permute-start(f32[584,128]{1,0:T(8,128)S(1)} %add.27.early_ref), channel_id=1, source_target_pairs={{0,8},{4,12},{8,0},{12,4},{16,24},{20,28},{24,16},{28,20},{1,9},{5... | collective-permute-start | bytes 897032 | tf_op jit(solution)/shard_map/ppermute | solution.py:1320
  146.1 4.4 %collective-permute-start.22 = (f32[144,128]{1,0:T(8,128)S(1)}, f32[144,128]{1,0:T(8,128)S(1)}, u32[]{:S(2)}, u32[]{:S(2)}) collective-permute-start(f32[144,128]{1,0:T(8,128)S(1)} %add_add_fusion.refs_0_), channel_id=1, source_target_pairs={{0,4},{4,0},{8,12},{12,8},{16,20},{20,16},{24,28},{28,24},{1,5},{5... | collective-permute-start | bytes 221192 | tf_op jit(solution)/shard_map/ppermute | solution.py:1316
  (5 other events, 10.1 us)
